TPU v7x, 32 devices: a whole 2x2x4 slice. The times are simulated.
32 devices in a mesh: dp: 8 (over z, core), tensor: 4 (over y, x).
Axes of the slice: x: 2, y: 2, z: 4, core: 2. Of those that a mesh axis runs over, the one named last changes fastest.
Arguments:
- inputs: bfloat16 [8192, 2048], P(('dp', 'tensor')), may hold values from -6 to 6
- cotangent: bfloat16 [8192, 2048], P(('dp', 'tensor')), may hold values from -6 to 6
- gains: float32 [2, 2048], replicated, may hold values from 0.1 to 1.9
- shifts: float32 [2, 2048], replicated, may hold values from -2 to 2
- qkv_weight: float32 [3, 2048, 2048], P(None, 'dp', 'tensor'), may hold values from -0.125 to 0.125
- biases: float32 [3, 32, 64], P(None, 'tensor', 'dp'), may hold values from -3 to 3
- out_weight: float32 [2048, 2048], P('tensor', 'dp'), may hold values from -1 to 1
- gate_up: float32 [2, 2048, 5632], P(None, 'dp', 'tensor'), may hold values from -0.125 to 0.125
- down_weight: float32 [5632, 2048], P('tensor', 'dp'), may hold values from -0.078125 to 0.078125
- momentum_gains: float32 [2, 2048], replicated, may hold values from -160 to 160
- momentum_shifts: float32 [2, 2048], replicated, may hold values from -160 to 160
- momentum_qkv: float32 [3, 2048, 2048], P(None, 'dp', 'tensor'), may hold values from -112 to 112
- momentum_biases: float32 [3, 32, 64], P(None, 'tensor', 'dp'), may hold values from -112 to 112
- momentum_out: float32 [2048, 2048], P('tensor', 'dp'), may hold values from -28 to 28
- momentum_gate: float32 [2, 2048, 5632], P(None, 'dp', 'tensor'), may hold values from -56 to 56
- momentum_down: float32 [5632, 2048], P('tensor', 'dp'), may hold values from -112 to 112
- variance_gains: float32 [2, 2048], replicated, may hold values from 245.76 to 3276.8
- variance_shifts: float32 [2, 2048], replicated, may hold values from 245.76 to 3276.8
- variance_qkv: float32 [3, 2048, 2048], P(None, 'dp', 'tensor'), may hold values from 81.92 to 1638.4
- variance_biases: float32 [3, 32, 64], P(None, 'tensor', 'dp'), may hold values from 81.92 to 1638.4
- variance_out: float32 [2048, 2048], P('tensor', 'dp'), may hold values from 5.7344 to 81.92
- variance_gate: float32 [2, 2048, 5632], P(None, 'dp', 'tensor'), may hold values from 24.576 to 327.68
- variance_down: float32 [5632, 2048], P('tensor', 'dp'), may hold values from 81.92 to 1228.8
Outputs:
- block_out: bfloat16 [8192, 2048], P(('dp', 'tensor'))
- input_grad: float32 [8192, 2048], P(('dp', 'tensor'))
- gains_grad: float32 [2, 2048], replicated
- shifts_grad: float32 [2, 2048], replicated
- qkv_grad: float32 [3, 2048, 2048], P(None, 'dp', 'tensor')
- biases_grad: float32 [3, 32, 64], P(None, 'tensor', 'dp')
- out_grad: float32 [2048, 2048], P('tensor', 'dp')
- gate_grad: float32 [2, 2048, 5632], P(None, 'dp', 'tensor')
- down_grad: float32 [5632, 2048], P('tensor', 'dp')
- new_gains: float32 [2, 2048], replicated
- new_shifts: float32 [2, 2048], replicated
- new_qkv: float32 [3, 2048, 2048], P(None, 'dp', 'tensor')
- new_biases: float32 [3, 32, 64], P(None, 'tensor', 'dp')
- new_out: float32 [2048, 2048], P('tensor', 'dp')
- new_gate: float32 [2, 2048, 5632], P(None, 'dp', 'tensor')
- new_down: float32 [5632, 2048], P('tensor', 'dp')
- new_momentum_gains: float32 [2, 2048], replicated
- new_momentum_shifts: float32 [2, 2048], replicated
- new_momentum_qkv: float32 [3, 2048, 2048], P(None, 'dp', 'tensor')
- new_momentum_biases: float32 [3, 32, 64], P(None, 'tensor', 'dp')
- new_momentum_out: float32 [2048, 2048], P('tensor', 'dp')
- new_momentum_gate: float32 [2, 2048, 5632], P(None, 'dp', 'tensor')
- new_momentum_down: float32 [5632, 2048], P('tensor', 'dp')
- new_variance_gains: float32 [2, 2048], replicated
- new_variance_shifts: float32 [2, 2048], replicated
- new_variance_qkv: float32 [3, 2048, 2048], P(None, 'dp', 'tensor')
- new_variance_biases: float32 [3, 32, 64], P(None, 'tensor', 'dp')
- new_variance_out: float32 [2048, 2048], P('tensor', 'dp')
- new_variance_gate: float32 [2, 2048, 5632], P(None, 'dp', 'tensor')
- new_variance_down: float32 [5632, 2048], P('tensor', 'dp')
All inputs are finite; a program needn't handle non-finite values.
Results may differ from a plain program's by a relative error of at most 0.015.
Values may be sent and summed in bfloat16 or wider, within the bound.
A program may use at most 256 MiB of HBM per device.

v0:
```python
import jax
import jax.numpy as jnp
from jax import lax
from jax.sharding import PartitionSpec as P

ROT = 16
SEQ = 1024
ADAM_STEP = 3


norm_eps = 1e-05
learn_rate = 0.03
vector_rate = 0.25
decay_rate = 0.1
adam_eps = 1e-08


def layer_norm(values, gain, shift):
    centred = values - jnp.mean(values, -1, keepdims=True)
    recip = lax.rsqrt(jnp.mean(centred * centred, -1, keepdims=True) + norm_eps)
    normed = centred * recip
    return (normed * gain + shift, normed, recip)


def norm_back(grad, normed, recip, gain):
    scaled = grad * gain
    inner = (
        scaled
        - jnp.mean(scaled, -1, keepdims=True)
        - normed * jnp.mean(scaled * normed, -1, keepdims=True)
    )
    return recip * inner


def rope_tables(row_count):
    halfway = ROT // 2
    position = (jnp.arange(row_count) % SEQ).astype(jnp.float32)
    frequency = jnp.power(10000.0, -2.0 * jnp.arange(halfway).astype(jnp.float32) / ROT)
    angles = position[:, None] * frequency[None, :]
    return (jnp.cos(angles)[:, None, :], jnp.sin(angles)[:, None, :])


def rotate(values, cosine, sine):
    halfway = cosine.shape[-1]
    leading = values[..., :halfway]
    trailing = values[..., halfway : 2 * halfway]
    return jnp.concatenate(
        [
            leading * cosine - trailing * sine,
            trailing * cosine + leading * sine,
            values[..., 2 * halfway :],
        ],
        -1,
    )


def masked_scores(query_blk, keys, begin):
    block_rows = query_blk.shape[0]
    scores = 0.125 * jnp.einsum("qhd,khd->hqk", query_blk, keys, preferred_element_type=jnp.float32)
    allowed = (begin + jnp.arange(block_rows))[:, None] >= jnp.arange(keys.shape[0])[None, :]
    return jnp.where(allowed[None], scores, -1e30)


def attend_forward(triple):
    query, keys, values = triple
    block_rows = min(512, SEQ)
    pieces = []
    totals = []
    for begin in range(0, SEQ, block_rows):
        scores = masked_scores(query[begin : begin + block_rows], keys, begin)
        top = jnp.max(scores, -1, keepdims=True)
        expo = jnp.exp(scores - top)
        total = jnp.sum(expo, -1, keepdims=True)
        probs = (expo / total).astype(jnp.bfloat16)
        pieces.append(jnp.einsum("hqk,khd->qhd", probs, values, preferred_element_type=jnp.float32))
        totals.append(top + jnp.log(total))
    return (jnp.concatenate(pieces, 0), jnp.concatenate(totals, 1))


def attend_backward(bundle):
    query, keys, values, grad_heads, log_total = bundle
    block_rows = min(512, SEQ)
    query_grads = []
    key_grad = jnp.zeros(keys.shape, jnp.float32)
    value_grad = jnp.zeros(values.shape, jnp.float32)
    for begin in range(0, SEQ, block_rows):
        query_blk = query[begin : begin + block_rows]
        grad_blk = grad_heads[begin : begin + block_rows]
        scores = masked_scores(query_blk, keys, begin)
        probs = jnp.exp(scores - log_total[:, begin : begin + block_rows])
        prob_grad = jnp.einsum("qhd,khd->hqk", grad_blk, values, preferred_element_type=jnp.float32)
        inner = jnp.sum(probs * prob_grad, -1, keepdims=True)
        score_grad = (probs * (prob_grad - inner)).astype(jnp.bfloat16)
        query_grads.append(
            0.125 * jnp.einsum("hqk,khd->qhd", score_grad, keys, preferred_element_type=jnp.float32)
        )
        key_grad = key_grad + 0.125 * jnp.einsum(
            "hqk,qhd->khd", score_grad, query_blk, preferred_element_type=jnp.float32
        )
        value_grad = value_grad + jnp.einsum(
            "hqk,qhd->khd", probs.astype(jnp.bfloat16), grad_blk, preferred_element_type=jnp.float32
        )
    return (jnp.concatenate(query_grads, 0), key_grad, value_grad)


def adamw(weight, grad, moment, second, decay, rate):
    moment_new = 0.9 * moment + 0.1 * grad
    second_new = 0.95 * second + 0.05 * grad * grad
    fixed_one = 1.0 - 0.9**ADAM_STEP
    fixed_two = 1.0 - 0.95**ADAM_STEP
    change = moment_new / fixed_one / (jnp.sqrt(second_new / fixed_two) + adam_eps) + decay * weight
    return (weight - rate * change, moment_new, second_new)


def contract_rows(left, right):
    return lax.dot_general(
        left, right, (((0,), (0,)), ((), ())), preferred_element_type=jnp.float32
    )


def contract_cols(left, right):
    return lax.dot_general(
        left, right, (((1,), (1,)), ((), ())), preferred_element_type=jnp.float32
    )


def local(
    inputs,
    cotangent,
    gains,
    shifts,
    qkv_weight,
    biases,
    out_weight,
    gate_up,
    down_weight,
    momentum_gains,
    momentum_shifts,
    momentum_qkv,
    momentum_biases,
    momentum_out,
    momentum_gate,
    momentum_down,
    variance_gains,
    variance_shifts,
    variance_qkv,
    variance_biases,
    variance_out,
    variance_gate,
    variance_down,
):
    tok_rows = inputs.shape[0]
    xin = inputs.astype(jnp.float32)
    w_qkv, w_output, bias_all = (
        lax.all_gather(qkv_weight.astype(jnp.bfloat16), "dp", axis=1, tiled=True),
        lax.all_gather(out_weight.astype(jnp.bfloat16), "dp", axis=1, tiled=True),
        lax.all_gather(biases.astype(jnp.bfloat16), "dp", axis=2, tiled=True),
    )
    local_heads = bias_all.shape[1]
    head_size = bias_all.shape[2]
    local_width = local_heads * head_size
    first_out, first_normed, first_recip = layer_norm(xin, gains[0], shifts[0])
    piece = lax.all_gather(first_out.astype(jnp.bfloat16), "tensor", axis=0, tiled=True)
    gathered_a = piece
    qkv_lin = jnp.einsum("rd,kdc->rkc", piece, w_qkv, preferred_element_type=jnp.float32)
    group_rows = gathered_a.shape[0]
    shaped = (group_rows, local_heads, head_size)
    seq_shape = (group_rows // SEQ, SEQ, local_heads, head_size)
    cosine, sine = rope_tables(group_rows)
    query_lin = qkv_lin[:, 0] + bias_all[0].reshape(local_width).astype(jnp.float32)
    key_lin = qkv_lin[:, 1] + bias_all[1].reshape(local_width).astype(jnp.float32)
    value_lin = qkv_lin[:, 2] + bias_all[2].reshape(local_width).astype(jnp.float32)
    query_rot = rotate(query_lin.reshape(shaped), cosine, sine).astype(jnp.bfloat16)
    key_rot = rotate(key_lin.reshape(shaped), cosine, sine).astype(jnp.bfloat16)
    value_low = value_lin.reshape(shaped).astype(jnp.bfloat16)
    attended, log_totals = lax.map(
        attend_forward,
        (query_rot.reshape(seq_shape), key_rot.reshape(seq_shape), value_low.reshape(seq_shape)),
    )
    heads = attended.reshape(group_rows, local_width).astype(jnp.bfloat16)
    resid = xin + lax.psum_scatter(
        jnp.dot(
            lax.slice_in_dim(heads, 0, tok_rows * lax.axis_size("tensor"), axis=0),
            w_output,
            preferred_element_type=jnp.float32,
        ),
        "tensor",
        scatter_dimension=0,
        tiled=True,
    )
    w_gate_up, w_down = (
        lax.all_gather(gate_up.astype(jnp.bfloat16), "dp", axis=1, tiled=True),
        lax.all_gather(down_weight.astype(jnp.bfloat16), "dp", axis=1, tiled=True),
    )
    second_out, second_normed, second_recip = layer_norm(resid, gains[1], shifts[1])
    piece = lax.all_gather(second_out.astype(jnp.bfloat16), "tensor", axis=0, tiled=True)
    gate_vals = jnp.einsum("rd,kdc->rkc", piece, w_gate_up, preferred_element_type=jnp.float32)
    gate_lin = gate_vals[:, 0]
    upward = gate_vals[:, 1]
    sigmoid_gate = jax.nn.sigmoid(gate_lin)
    silu_gate = gate_lin * sigmoid_gate
    hidden = (silu_gate * upward).astype(jnp.bfloat16)
    block_out = (
        resid
        + lax.psum_scatter(
            jnp.dot(
                lax.slice_in_dim(hidden, 0, tok_rows * lax.axis_size("tensor"), axis=0),
                w_down,
                preferred_element_type=jnp.float32,
            ).astype(jnp.bfloat16),
            "tensor",
            scatter_dimension=0,
            tiled=True,
        ).astype(jnp.float32)
    ).astype(jnp.bfloat16)
    grad_full = lax.all_gather(cotangent, "tensor", axis=0, tiled=True)
    down_terms = contract_rows(hidden, grad_full)
    hidden_grad = contract_cols(grad_full, w_down)
    gate_grad_low = (
        hidden_grad * upward * sigmoid_gate * (1.0 + gate_lin * (1.0 - sigmoid_gate))
    ).astype(jnp.bfloat16)
    up_grad_low = (hidden_grad * silu_gate).astype(jnp.bfloat16)
    both_grads = jnp.stack([gate_grad_low, up_grad_low], 1)
    gate_terms = jnp.einsum("rd,rkc->kdc", piece, both_grads, preferred_element_type=jnp.float32)
    rows_grad = lax.slice_in_dim(both_grads, 0, tok_rows * lax.axis_size("tensor"), axis=0)
    second_grad = lax.psum_scatter(
        jnp.einsum("rkc,kdc->rd", rows_grad, w_gate_up, preferred_element_type=jnp.float32),
        "tensor",
        scatter_dimension=0,
        tiled=True,
    )
    resid_grad = cotangent.astype(jnp.float32) + norm_back(
        second_grad, second_normed, second_recip, gains[1]
    )
    gain_second = jnp.sum(second_grad * second_normed, 0)
    shift_second = jnp.sum(second_grad, 0)
    resid_full = lax.all_gather(resid_grad.astype(jnp.bfloat16), "tensor", axis=0, tiled=True)
    out_terms = contract_rows(heads, resid_full)
    heads_grad = contract_cols(resid_full, w_output).astype(jnp.bfloat16)
    query_back, key_back, value_back = lax.map(
        attend_backward,
        (
            query_rot.reshape(seq_shape),
            key_rot.reshape(seq_shape),
            value_low.reshape(seq_shape),
            heads_grad.reshape(seq_shape),
            log_totals,
        ),
    )
    query_grad = (
        rotate(query_back.reshape(shaped), cosine, -sine)
        .reshape(group_rows, local_width)
        .astype(jnp.bfloat16)
    )
    key_grad = (
        rotate(key_back.reshape(shaped), cosine, -sine)
        .reshape(group_rows, local_width)
        .astype(jnp.bfloat16)
    )
    value_grad = value_back.reshape(group_rows, local_width).astype(jnp.bfloat16)
    lin_grads = jnp.stack([query_grad, key_grad, value_grad], 1)
    bias_terms = jnp.sum(lin_grads.astype(jnp.float32), 0).reshape(3, local_heads, head_size)
    qkv_terms = jnp.einsum("rd,rkc->kdc", gathered_a, lin_grads, preferred_element_type=jnp.float32)
    rows_grad = lax.slice_in_dim(lin_grads, 0, tok_rows * lax.axis_size("tensor"), axis=0)
    first_grad = lax.psum_scatter(
        jnp.einsum("rkc,kdc->rd", rows_grad, w_qkv, preferred_element_type=jnp.float32).astype(
            jnp.bfloat16
        ),
        "tensor",
        scatter_dimension=0,
        tiled=True,
    ).astype(jnp.float32)
    input_grad = resid_grad + norm_back(first_grad, first_normed, first_recip, gains[0])
    gain_terms = jnp.stack([jnp.sum(first_grad * first_normed, 0), gain_second])
    shift_terms = jnp.stack([jnp.sum(first_grad, 0), shift_second])
    gains_grad, shifts_grad = lax.psum((gain_terms, shift_terms), ("dp", "tensor"))
    qkv_grad, biases_grad, out_grad, gate_grad, down_grad = (
        lax.psum_scatter(qkv_terms, "dp", scatter_dimension=1, tiled=True),
        lax.psum_scatter(bias_terms, "dp", scatter_dimension=2, tiled=True),
        lax.psum_scatter(out_terms, "dp", scatter_dimension=1, tiled=True),
        lax.psum_scatter(gate_terms, "dp", scatter_dimension=1, tiled=True),
        lax.psum_scatter(down_terms, "dp", scatter_dimension=1, tiled=True),
    )
    gain_new = adamw(gains, gains_grad, momentum_gains, variance_gains, 0.0, vector_rate)
    shift_new = adamw(shifts, shifts_grad, momentum_shifts, variance_shifts, 0.0, vector_rate)
    qkv_new = adamw(qkv_weight, qkv_grad, momentum_qkv, variance_qkv, decay_rate, learn_rate)
    bias_new = adamw(biases, biases_grad, momentum_biases, variance_biases, 0.0, vector_rate)
    out_new = adamw(out_weight, out_grad, momentum_out, variance_out, decay_rate, learn_rate)
    gate_new = adamw(gate_up, gate_grad, momentum_gate, variance_gate, decay_rate, learn_rate)
    down_new = adamw(down_weight, down_grad, momentum_down, variance_down, decay_rate, learn_rate)
    return (
        block_out,
        input_grad,
        gains_grad,
        shifts_grad,
        qkv_grad,
        biases_grad,
        out_grad,
        gate_grad,
        down_grad,
        gain_new[0],
        shift_new[0],
        qkv_new[0],
        bias_new[0],
        out_new[0],
        gate_new[0],
        down_new[0],
        gain_new[1],
        shift_new[1],
        qkv_new[1],
        bias_new[1],
        out_new[1],
        gate_new[1],
        down_new[1],
        gain_new[2],
        shift_new[2],
        qkv_new[2],
        bias_new[2],
        out_new[2],
        gate_new[2],
        down_new[2],
    )


def solution(mesh):
    return jax.shard_map(
        local,
        mesh=mesh,
        in_specs=(
            P(("dp", "tensor"), None),
            P(("dp", "tensor"), None),
            P(),
            P(),
            P(None, "dp", "tensor"),
            P(None, "tensor", "dp"),
            P("tensor", "dp"),
            P(None, "dp", "tensor"),
            P("tensor", "dp"),
            P(),
            P(),
            P(None, "dp", "tensor"),
            P(None, "tensor", "dp"),
            P("tensor", "dp"),
            P(None, "dp", "tensor"),
            P("tensor", "dp"),
            P(),
            P(),
            P(None, "dp", "tensor"),
            P(None, "tensor", "dp"),
            P("tensor", "dp"),
            P(None, "dp", "tensor"),
            P("tensor", "dp"),
        ),
        out_specs=(
            P(("dp", "tensor"), None),
            P(("dp", "tensor"), None),
            P(),
            P(),
            P(None, "dp", "tensor"),
            P(None, "tensor", "dp"),
            P("tensor", "dp"),
            P(None, "dp", "tensor"),
            P("tensor", "dp"),
            P(),
            P(),
            P(None, "dp", "tensor"),
            P(None, "tensor", "dp"),
            P("tensor", "dp"),
            P(None, "dp", "tensor"),
            P("tensor", "dp"),
            P(),
            P(),
            P(None, "dp", "tensor"),
            P(None, "tensor", "dp"),
            P("tensor", "dp"),
            P(None, "dp", "tensor"),
            P("tensor", "dp"),
            P(),
            P(),
            P(None, "dp", "tensor"),
            P(None, "tensor", "dp"),
            P("tensor", "dp"),
            P(None, "dp", "tensor"),
            P("tensor", "dp"),
        ),
        check_vma=False,
    )
```

profile of v0, /device:TPU:0, one launch (start us, length us, event | category | flops | bytes accessed | tf_op | source)
XLA Modules:
  0.0 1392.6 jit_solution(15363078877345794620)
XLA Ops:
  18.6 15.6 %all_gather.29 = bf16[3,8,64]{1,0,2:T(4,128)(2,1)S(1)} all-gather(bf16[3,8,8]{1,0,2:T(4,128)(2,1)S(1)} %copy.104), channel_id=1, replica_groups=mesh['dp'=8,'tensor'=4] {'dp'}, dimensions={2}, use_global_device_ids=true | all-gather | bytes 3456 | tf_op jit(solution)/shard_map/all_gather | solution.py:157
  36.5 32.6 %all-gather.9.cloned.1.call-done = bf16[1024,2048]{1,0:T(8,128)(2,1)} async-done(((bf16[256,2048]{1,0:T(8,128)(2,1)}), bf16[1024,2048]{1,0:T(8,128)(2,1)}) %all-gather.9.cloned.1.call-update) | async-done | bytes 4194320 | tf_op jit(solution)/shard_map/all_gather | solution.py:163
  69.1 67.4 %all-gather.11.cloned.1.call-done = bf16[3,2048,512]{1,2,0:T(8,128)(2,1)} async-done(((bf16[3,256,512]{1,2,0:T(8,128)(2,1)}), bf16[3,2048,512]{1,2,0:T(8,128)(2,1)}) %all-gather.11.cloned.1.call-update) | async-done | bytes 6291472 | tf_op jit(solution)/shard_map/all_gather | solution.py:155
  187.1 81.6 %reduce-scatter.10.cloned.1.call-done = f32[256,2048]{1,0:T(8,128)} async-done(((f32[1024,2048]{1,0:T(8,128)}), f32[256,2048]{1,0:T(8,128)}) %reduce-scatter.10.cloned.1.call-update) | async-done | bytes 2097168 | tf_op jit(solution)/shard_map/reduce_scatter | solution.py:181
  274.8 104.1 %all-gather.17.cloned.1.call-done = bf16[2,2048,1408]{2,1,0:T(8,128)(2,1)} async-done(((bf16[2,256,1408]{2,1,0:T(8,128)(2,1)}), bf16[2,2048,1408]{2,1,0:T(8,128)(2,1)}) %all-gather.17.cloned.1.call-update) | async-done | bytes 11534352 | tf_op jit(solution)/shard_map/all_gather | solution.py:192
  378.9 53.5 %all-gather.15.cloned.1.call-done = bf16[1024,2048]{1,0:T(8,128)(2,1)} async-done(((bf16[256,2048]{1,0:T(8,128)(2,1)}), bf16[1024,2048]{1,0:T(8,128)(2,1)}) %all-gather.15.cloned.1.call-update) | async-done | bytes 4194320 | tf_op jit(solution)/shard_map/all_gather | solution.py:196
  432.4 18.9 %fusion.14 = f32[1024,2,1408]{2,0,1:T(8,128)} fusion(bf16[2,2048,1408]{2,1,0:T(8,128)(2,1)} %all-gather.17.cloned.1.call-done, bf16[1024,2048]{1,0:T(8,128)(2,1)} %all-gather.15.cloned.1.call-done), kind=kOutput, calls=%fused_computation.37 | convolution fusion | flops 11811160064 | bytes 27262976 | tf_op jit(solution)/shard_map/rd,kdc->rkc/dot_general | solution.py:197
  451.2 35.9 %all-gather.21.cloned.1.call-done = bf16[1024,2048]{1,0:T(8,128)(2,1)} async-done(((bf16[256,2048]{1,0:T(8,128)(2,1)}), bf16[1024,2048]{1,0:T(8,128)(2,1)}) %all-gather.21.cloned.1.call-update) | async-done | bytes 4194320 | tf_op jit(solution)/shard_map/all_gather | solution.py:216
  487.1 63.1 %all-gather.19.cloned.1.call-done = bf16[1408,2048]{1,0:T(8,128)(2,1)} async-done(((bf16[1408,256]{1,0:T(8,128)(2,1)}), bf16[1408,2048]{1,0:T(8,128)(2,1)}) %all-gather.19.cloned.1.call-update) | async-done | bytes 5767184 | tf_op jit(solution)/shard_map/all_gather | solution.py:193
  550.2 15.6 %fusion.24 = (bf16[1024,1,1408]{2,0,1:T(8,128)(2,1)S(1)}, bf16[1024,1,1408]{2,0,1:T(8,128)(2,1)S(1)}, bf16[1024,1408]{1,0:T(8,128)(2,1)}) fusion(f32[1024,2,1408]{2,0,1:T(8,128)} %fusion.14, bf16[1024,2048]{1,0:T(8,128)(2,1)} %all-gather.21.cloned.1.call-done, bf16[1408,2048]{1,0:T(8,128)(2,1)} %all-gather.19.cloned.1.call-done), kind=kOutput, calls=%fused_computation.57 | convolution fusion | flops 5927206912 | bytes 30146560 | tf_op jit(solution)/shard_map/dot_general | solution.py:122
  568.3 16.9 %convolution_bitcast_fusion.2 = f32[1024,2048]{1,0:T(8,128)} fusion(bf16[2,2048,1408]{2,1,0:T(8,128)(2,1)} %all-gather.17.cloned.1.call-done, bf16[1024,1,1408]{2,0,1:T(8,128)(2,1)S(1)} %get-tuple-element.202, bf16[1024,1,1408]{2,0,1:T(8,128)(2,1)S(1)} %get-tuple-element.201), kind=kOutput, calls=%fused_computation.35 | convolution fusion | flops 11814043648 | bytes 25690112 | tf_op jit(solution)/shard_map/rkc,kdc->rd/dot_general | solution.py:227
  596.6 73.4 %reduce-scatter.14.cloned.1.call-done = f32[256,2048]{1,0:T(8,128)} async-done(((f32[1024,2048]{1,0:T(8,128)}), f32[256,2048]{1,0:T(8,128)}) %reduce-scatter.14.cloned.1.call-update) | async-done | bytes 2097168 | tf_op jit(solution)/shard_map/reduce_scatter | solution.py:226
  673.1 52.4 %reduce-scatter.12.cloned.1.call-done = bf16[256,2048]{1,0:T(8,128)(2,1)} async-done(((bf16[1024,2048]{1,0:T(8,128)(2,1)}), bf16[256,2048]{1,0:T(8,128)(2,1)}) %reduce-scatter.12.cloned.1.call-update) | async-done | bytes 1048592 | tf_op jit(solution)/shard_map/reduce_scatter | solution.py:205
  730.6 11.3 fusion.83
  742.7 40.7 %all-gather.23.cloned.1.call-done = bf16[1024,2048]{1,0:T(8,128)(2,1)} async-done(((bf16[256,2048]{1,0:T(8,128)(2,1)}), bf16[1024,2048]{1,0:T(8,128)(2,1)}) %all-gather.23.cloned.1.call-update) | async-done | bytes 4194320 | tf_op jit(solution)/shard_map/all_gather | solution.py:237
  802.5 13.1 multiply_reduce_fusion.1
  815.6 12.5 multiply_convert_fusion.1
  867.8 11.4 bitcast_convert_fusion
  886.2 20.1 %convolution_bitcast_fusion = f32[2,2048,1408]{1,2,0:T(8,128)} fusion(bf16[1024,2048]{1,0:T(8,128)(2,1)} %all-gather.15.cloned.1.call-done, bf16[1024,1,1408]{2,0,1:T(8,128)(2,1)} %copy-done.74, bf16[1024,1,1408]{2,0,1:T(8,128)(2,1)} %copy-done.73), kind=kOutput, calls=%fused_computation.14 | convolution fusion | flops 11814043648 | bytes 33030144 | tf_op jit(solution)/shard_map/rd,rkc->kdc/dot_general | solution.py:224
  906.4 12.1 convolution_bitcast_fusion.1
  939.0 28.8 %all-reduce = f32[3,8,64]{2,1,0:T(8,128)S(1)} all-reduce(f32[3,8,64]{2,1,0:T(8,128)S(1)} %reshape.352), channel_id=7, replica_groups=mesh['dp'=8,'tensor'=4] {'dp'}, use_global_device_ids=true, to_apply=%region_26.27.clone | all-reduce | flops 1536 | bytes 12288
  977.0 39.2 %all-reduce.1 = (f32[2,2048]{1,0:T(2,128)S(1)}, f32[2,2048]{1,0:T(2,128)S(1)}) all-reduce(f32[2,2048]{1,0:T(2,128)S(1)} %pad_maximum_fusion.10, f32[2,2048]{1,0:T(2,128)S(1)} %pad_maximum_fusion.11), channel_id=1, replica_groups=mesh['dp'=8,'tensor'=4] {'dp','tensor'}, use_global_device_ids=true, to_apply=%region_20.21 | all-reduce | flops 8192 | bytes 65536 | tf_op jit(solution)/shard_map/psum | solution.py:276
  1022.8 218.7 %reduce-scatter.22.cloned.1.call-done = f32[2,256,1408]{1,2,0:T(8,128)} async-done(((f32[2,2048,1408]{1,2,0:T(8,128)}), f32[2,256,1408]{1,2,0:T(8,128)}) %reduce-scatter.22.cloned.1.call-update) | async-done | bytes 2883600 | tf_op jit(solution)/shard_map/reduce_scatter | solution.py:281
  1261.5 109.7 %reduce-scatter.18.cloned.1.call-done = f32[3,256,512]{1,2,0:T(8,128)} async-done(((f32[3,2048,512]{1,2,0:T(8,128)}), f32[3,256,512]{1,2,0:T(8,128)}) %reduce-scatter.18.cloned.1.call-update) | async-done | bytes 1572880 | tf_op jit(solution)/shard_map/reduce_scatter | solution.py:278
  (304 shorter events, 227.8 us)
Async XLA Ops:
  7.2 61.9 %all-gather.9.cloned.1.call-start = ((), (), s32[]{:S(2)}) async-start(), calls=%async_computation.8 | async-start | bytes 5242880 | tf_op jit(solution)/shard_map/all_gather | solution.py:163
  13.5 122.9 %all-gather.11.cloned.1.call-start = ((), (), s32[]{:S(2)}) async-start(), calls=%async_computation.9 | async-start | bytes 7077888 | tf_op jit(solution)/shard_map/all_gather | solution.py:155
  16.6 159.7 %all-gather.13.cloned.1.call-start = ((), (), s32[]{:S(2)}) async-start(), calls=%async_computation.10 | async-start | bytes 2359296 | tf_op jit(solution)/shard_map/all_gather | solution.py:156
  17.4 251.3 %reduce-scatter.10.cloned.1.call-start = ((), (), s32[]{:S(2)}) async-start(), calls=%async_computation.11 | async-start | bytes 10485760 | tf_op jit(solution)/shard_map/reduce_scatter | solution.py:181
  36.5 111.8 %copy-start.39 = (f32[1024,8]{0,1:T(8,128)}, f32[1024,8]{0,1:T(8,128)S(1)}, u32[]{:S(2)}) copy-start(f32[1024,8]{0,1:T(8,128)S(1)} %get-tuple-element.231) | copy-start | bytes 98308
  183.9 195.0 %all-gather.17.cloned.1.call-start = ((), (), s32[]{:S(2)}) async-start(), calls=%async_computation.13 | async-start | bytes 12976128 | tf_op jit(solution)/shard_map/all_gather | solution.py:192
  187.1 245.3 %all-gather.15.cloned.1.call-start = ((), (), s32[]{:S(2)}) async-start(), calls=%async_computation.12 | async-start | bytes 5242880 | tf_op jit(solution)/shard_map/all_gather | solution.py:196
  273.0 214.1 %all-gather.21.cloned.1.call-start = ((), (), s32[]{:S(2)}) async-start(), calls=%async_computation.16 | async-start | bytes 5242880 | tf_op jit(solution)/shard_map/all_gather | solution.py:216
  273.7 276.5 %all-gather.19.cloned.1.call-start = ((), (), s32[]{:S(2)}) async-start(), calls=%async_computation.14 | async-start | bytes 6488064 | tf_op jit(solution)/shard_map/all_gather | solution.py:193
  274.7 395.3 %reduce-scatter.14.cloned.1.call-start = ((), (), s32[]{:S(2)}) async-start(), calls=%async_computation.17 | async-start | bytes 10485760 | tf_op jit(solution)/shard_map/reduce_scatter | solution.py:226
  585.3 140.3 %reduce-scatter.12.cloned.1.call-start = ((), (), s32[]{:S(2)}) async-start(), calls=%async_computation.15 | async-start | bytes 5242880 | tf_op jit(solution)/shard_map/reduce_scatter | solution.py:205
  596.5 73.5 %copy-start.59 = (f32[256]{0:T(256)S(1)}, f32[256]{0:T(256)}, u32[]{:S(2)}) copy-start(f32[256]{0:T(256)} %copy-done.58) | copy-start | bytes 3076
  596.5 73.5 %copy-start.63 = (f32[256]{0:T(256)S(1)}, f32[256]{0:T(256)}, u32[]{:S(2)}) copy-start(f32[256]{0:T(256)} %copy-done.62) | copy-start | bytes 3076
  596.6 129.0 %copy-start.29 = (bf16[256,2048]{1,0:T(8,128)(2,1)S(1)}, bf16[256,2048]{1,0:T(8,128)(2,1)}, u32[]{:S(2)}) copy-start(bf16[256,2048]{1,0:T(8,128)(2,1)} %param.24) | copy-start | bytes 3145732
  596.6 186.8 %all-gather.23.cloned.1.call-start = ((), (), s32[]{:S(2)}) async-start(), calls=%async_computation.18 | async-start | bytes 5242880 | tf_op jit(solution)/shard_map/all_gather | solution.py:237
  730.5 238.8 %reduce-scatter.24.cloned.1.call-start = ((), (), s32[]{:S(2)}) async-start(), calls=%async_computation.23 | async-start | bytes 12976128 | tf_op jit(solution)/shard_map/reduce_scatter | solution.py:282
  741.9 232.5 %reduce-scatter.16.cloned.1.call-start = ((), (), s32[]{:S(2)}) async-start(), calls=%async_computation.19 | async-start | bytes 5242880 | tf_op jit(solution)/shard_map/reduce_scatter | solution.py:265
  879.2 137.1 %reduce-scatter.20.cloned.1.call-start = ((), (), s32[]{:S(2)}) async-start(), calls=%async_computation.21 | async-start | bytes 4718592 | tf_op jit(solution)/shard_map/reduce_scatter | solution.py:280
  886.1 355.4 %reduce-scatter.22.cloned.1.call-start = ((), (), s32[]{:S(2)}) async-start(), calls=%async_computation.22 | async-start | bytes 25952256 | tf_op jit(solution)/shard_map/reduce_scatter | solution.py:281
  906.3 465.0 %reduce-scatter.18.cloned.1.call-start = ((), (), s32[]{:S(2)}) async-start(), calls=%async_computation.20 | async-start | bytes 14155776 | tf_op jit(solution)/shard_map/reduce_scatter | solution.py:278
  974.4 45.6 %copy-start.45 = (f32[2,2048]{1,0:T(2,128)S(1)}, f32[2,2048]{1,0:T(2,128)}, u32[]{:S(2)}) copy-start(f32[2,2048]{1,0:T(2,128)} %param.26) | copy-start | bytes 49156
  974.4 46.3 %copy-start.12 = (f32[256,2048]{1,0:T(8,128)S(1)}, f32[256,2048]{1,0:T(8,128)}, u32[]{:S(2)}) copy-start(f32[256,2048]{1,0:T(8,128)} %get-tuple-element.198) | copy-start | bytes 6291460
  1258.0 113.3 %copy-start.8 = (f32[3,256,512]{1,2,0:T(8,128)S(1)}, f32[3,256,512]{1,2,0:T(8,128)}, u32[]{:S(2)}) copy-start(f32[3,256,512]{1,2,0:T(8,128)} %copy-done.7) | copy-start | bytes 4718596
  1258.0 113.3 %copy-start.16 = (f32[3,256,512]{1,2,0:T(8,128)S(1)}, f32[3,256,512]{1,2,0:T(8,128)}, u32[]{:S(2)}) copy-start(f32[3,256,512]{1,2,0:T(8,128)} %copy.114) | copy-start | bytes 4718596
  (75 other events, 801.3 us)
Sparse Core Ops, SparseCore 0:
  13.6 55.3 all-gather.8
  71.2 65.1 all-gather.10
  138.6 29.0 all-gather.12
  184.1 84.5 reduce-scatter.9
  270.8 108.0 all-gather.16
  381.3 50.9 all-gather.14
  434.4 52.6 all-gather.20
  489.4 60.8 all-gather.18
  585.4 84.5 reduce-scatter.13
  672.8 52.6 reduce-scatter.11
  730.7 52.6 all-gather.22
  786.2 119.3 reduce-scatter.23
  908.8 51.0 reduce-scatter.15
  962.6 51.0 reduce-scatter.19
  1015.9 225.5 reduce-scatter.21
  1243.7 127.5 reduce-scatter.17
where the time goes:
time: 1400 us; the launch traced here: 1390 us
  waiting for transfers between devices  934 us (67%)
  matrix products  209 us (15%)
  other arithmetic  84.8 us (6%)
  blocking collectives  83.7 us (6%)
  local copies, waits for them, and re-layouts  64.3 us (5%)
  between operations  16.2 us (1%)
    reduce_scatter x1, waiting for transfers between devices, local(): lax.psum_scatter(gate_terms, 'dp', scatter_dimension=1, tiled=True)  219 us
    reduce_scatter x1, waiting for transfers between devices, local(): lax.psum_scatter(qkv_terms, 'dp', scatter_dimension=1, tiled=True)  110 us
    all_gather x1, waiting for transfers between devices, local(): lax.all_gather(gate_up.astype(jnp.bfloat16), 'dp', axis=1, tiled=True)  104 us
    reduce_scatter x1, waiting for transfers between devices, local(): lax.psum_scatter(jnp.dot(lax.slice_in_dim(heads, 0, tok_rows * lax.axis_s...  81.6 us
    reduce_scatter x1, waiting for transfers between devices, local(): lax.psum_scatter(jnp.einsum('rkc,kdc->rd', rows_grad, w_gate_up, preferre...  73.4 us
    all_gather x1, waiting for transfers between devices, local(): lax.all_gather(qkv_weight.astype(jnp.bfloat16), 'dp', axis=1, tiled=True)  67.4 us
    all_gather x1, waiting for transfers between devices, local(): lax.all_gather(down_weight.astype(jnp.bfloat16), 'dp', axis=1, tiled=True)  63.1 us
    unnamed x181, local copies, waits for them, and re-layouts  56.1 us
  transfers between devices with their start and end apart: 16, of which 12 were waited for; matrix products, arithmetic and copies ran while one was open for 20% of the time, Pallas kernels for 0%

commit v1 on v0

v1 whole, which is shorter than its diff:
```python
import functools

import jax
import jax.numpy as jnp
import numpy as np
from jax import lax
from jax.experimental import pallas as pl
from jax.experimental.layout import Layout, with_layout_constraint
from jax.experimental.pallas import tpu as pltpu
from jax.sharding import PartitionSpec as P

ROT = 16
SEQ = 1024
ADAM_STEP = 3


norm_eps = 1e-05
learn_rate = 0.03
vector_rate = 0.25
decay_rate = 0.1
adam_eps = 1e-08


def layer_norm(values, gain, shift):
    centred = values - jnp.mean(values, -1, keepdims=True)
    recip = lax.rsqrt(jnp.mean(centred * centred, -1, keepdims=True) + norm_eps)
    normed = centred * recip
    return (normed * gain + shift, normed, recip)


def norm_back(grad, normed, recip, gain):
    scaled = grad * gain
    inner = (
        scaled
        - jnp.mean(scaled, -1, keepdims=True)
        - normed * jnp.mean(scaled * normed, -1, keepdims=True)
    )
    return recip * inner


def adamw(weight, grad, moment, second, decay, rate):
    moment_new = 0.9 * moment + 0.1 * grad
    second_new = 0.95 * second + 0.05 * grad * grad
    fixed_one = 1.0 - 0.9**ADAM_STEP
    fixed_two = 1.0 - 0.95**ADAM_STEP
    change = moment_new / fixed_one / (jnp.sqrt(second_new / fixed_two) + adam_eps) + decay * weight
    return (weight - rate * change, moment_new, second_new)


def lane_head(shape, head_size):
    return lax.broadcasted_iota(jnp.int32, shape, len(shape) - 1) // head_size


def turn(values, tables, sign=1.0):
    width = values.shape[-1]
    own, ahead, behind = (jnp.concatenate([table] * (width // table.shape[-1]), 1) for table in tables)
    ahead = pltpu.roll(values, width - ROT // 2, 1) * ahead
    behind = pltpu.roll(values, ROT // 2, 1) * behind
    return values * own + sign * (ahead + behind)


def turn_tables(head_size):
    halfway = ROT // 2
    lane = np.arange(max(128, head_size)) % head_size
    position = np.arange(SEQ).astype(np.float32)
    frequency = np.power(np.float32(10000.0), -2.0 * (lane % halfway).astype(np.float32) / ROT)
    angles = position[:, None] * frequency.astype(np.float32)[None, :]
    cosine, sine = np.cos(angles), np.sin(angles)
    tables = [
        np.where(lane < ROT, cosine, 1.0),
        np.where(lane < halfway, -sine, 0.0),
        np.where((lane >= halfway) & (lane < ROT), sine, 0.0),
    ]
    return jnp.asarray(np.stack(tables).astype(np.float32))


LOG2E = 1.4426950408889634
NT = (((1,), (1,)), ((), ()))
NN = (((1,), (0,)), ((), ()))
TN = (((0,), (0,)), ((), ()))


def mxu(left, right, dims):
    return lax.dot_general(left, right, dims, preferred_element_type=jnp.float32)


def forward_kernel(head_size, lin_ref, bias_ref, table_ref, qkv_ref, out_ref, lse_ref):
    rows, width = out_ref.shape
    low = jnp.bfloat16
    step = min(256, rows)
    for part in range(3):
        for begin in range(0, rows, step):
            here = slice(begin, begin + step)
            values = lin_ref[part, here, :] + bias_ref[part : part + 1, :]
            if part < 2:
                values = turn(values, [table_ref[i, here, :] for i in range(3)])
            qkv_ref[part, here, :] = values.astype(low)
    owner = lane_head((step, width), head_size)
    lanes = lax.broadcasted_iota(jnp.int32, (step, 128), 1)
    for begin in range(0, rows, step):
        end = begin + step
        query = qkv_ref[0, begin:end, :]
        result = jnp.zeros((step, width), jnp.float32)
        logs = jnp.zeros((step, 128), jnp.float32)
        keep = lax.broadcasted_iota(jnp.int32, (step, step), 0) >= lax.broadcasted_iota(
            jnp.int32, (step, step), 1
        )
        for head in range(width // head_size):
            mine = jnp.where(owner == head, query, jnp.zeros_like(query))
            scores = mxu(mine, qkv_ref[1, :end, :], NT)
            last = jnp.where(keep, scores[:, begin:], -1e30)
            scores = jnp.concatenate([scores[:, :begin], last], 1) if begin else last
            top = jnp.max(scores, 1, keepdims=True)
            expo = jnp.exp2((scores - top) * (0.125 * LOG2E))
            total = jnp.sum(expo, 1, keepdims=True)
            found = mxu(expo.astype(low), qkv_ref[2, :end, :], NN)
            result = jnp.where(owner == head, found / total, result)
            logs = jnp.where(lanes == head, top * (0.125 * LOG2E) + jnp.log2(total), logs)
        out_ref[begin:end, :] = result.astype(low)
        lse_ref[:, begin:end] = logs.T[:8]


def attention_forward(lin, bias, head_size):
    _, rows, width = lin.shape
    lanes = min(256, width)
    groups = width // lanes
    tables = turn_tables(head_size)
    low = jnp.bfloat16
    return pl.pallas_call(
        functools.partial(forward_kernel, head_size),
        grid=(rows // SEQ, groups),
        out_shape=(
            jax.ShapeDtypeStruct((3, rows, width), low),
            jax.ShapeDtypeStruct((rows, width), low),
            jax.ShapeDtypeStruct((groups, 8, rows), jnp.float32),
        ),
        in_specs=[
            pl.BlockSpec((3, SEQ, lanes), lambda i, j: (0, i, j)),
            pl.BlockSpec((3, lanes), lambda i, j: (0, j)),
            pl.BlockSpec(tables.shape, lambda i, j: (0, 0, 0)),
        ],
        out_specs=(
            pl.BlockSpec((3, SEQ, lanes), lambda i, j: (0, i, j)),
            pl.BlockSpec((SEQ, lanes), lambda i, j: (i, j)),
            pl.BlockSpec((None, 8, SEQ), lambda i, j: (j, 0, i)),
        ),
        compiler_params=pltpu.CompilerParams(vmem_limit_bytes=48 * 1024 * 1024),
        cost_estimate=pl.CostEstimate(
            flops=rows * SEQ * width * 8, bytes_accessed=rows * width * 26, transcendentals=0
        ),
        name="attend_forward",
    )(lin, bias, tables)


def backward_kernel(head_size, qkv_ref, grad_ref, lse_ref, table_ref, out_ref, sum_ref, acc_ref):
    _, rows, width = qkv_ref.shape
    low = jnp.bfloat16
    step = min(256, rows)
    owner = lane_head((step, width), head_size)
    acc_ref[...] = jnp.zeros_like(acc_ref)
    blank = jnp.zeros((step, width), low)
    for begin in range(0, rows, step):
        end = begin + step
        query = qkv_ref[0, begin:end, :]
        grad = grad_ref[begin:end, :]
        keep = lax.broadcasted_iota(jnp.int32, (step, step), 1) >= lax.broadcasted_iota(
            jnp.int32, (step, step), 0
        )
        query_grad = jnp.zeros((step, width), jnp.float32)
        for head in range(width // head_size):
            mine = jnp.where(owner == head, query, blank)
            grad_mine = jnp.where(owner == head, grad, blank)
            scores = mxu(qkv_ref[1, :end, :], mine, NT)
            expo = jnp.exp2(scores * (0.125 * LOG2E) - lse_ref[head : head + 1, begin:end])
            last = jnp.where(keep, expo[begin:, :], 0.0)
            probs = jnp.concatenate([expo[:begin], last], 0) if begin else last
            prob_grad = mxu(qkv_ref[2, :end, :], grad_mine, NT)
            inner = jnp.sum(probs * prob_grad, 0, keepdims=True)
            score_grad = (probs * (prob_grad - inner)).astype(low)
            acc_ref[0, :end, :] += mxu(score_grad, mine, NN)
            acc_ref[1, :end, :] += mxu(probs.astype(low), grad_mine, NN)
            found = mxu(score_grad, qkv_ref[1, :end, :], TN)
            query_grad = jnp.where(owner == head, found, query_grad)
        turned = turn(0.125 * query_grad, [table_ref[i, begin:end, :] for i in range(3)], -1.0).astype(low)
        out_ref[0, begin:end, :] = turned
        added = jnp.sum(turned.astype(jnp.float32), 0, keepdims=True)
        sum_ref[0:1, :] = added if begin == 0 else sum_ref[0:1, :] + added
    for begin in range(0, rows, step):
        here = slice(begin, begin + step)
        turned = turn(0.125 * acc_ref[0, here, :], [table_ref[i, here, :] for i in range(3)], -1.0).astype(low)
        out_ref[1, here, :] = turned
        added = jnp.sum(turned.astype(jnp.float32), 0, keepdims=True)
        sum_ref[1:2, :] = added if begin == 0 else sum_ref[1:2, :] + added
        turned = acc_ref[1, here, :].astype(low)
        out_ref[2, here, :] = turned
        added = jnp.sum(turned.astype(jnp.float32), 0, keepdims=True)
        sum_ref[2:3, :] = added if begin == 0 else sum_ref[2:3, :] + added


def attention_backward(qkv, grad, logs, head_size):
    _, rows, width = qkv.shape
    lanes = min(256, width)
    groups = width // lanes
    tables = turn_tables(head_size)
    low = jnp.bfloat16
    grads, sums = pl.pallas_call(
        functools.partial(backward_kernel, head_size),
        grid=(rows // SEQ, groups),
        out_shape=(
            jax.ShapeDtypeStruct((3, rows, width), low),
            jax.ShapeDtypeStruct((rows // SEQ, 3, width), jnp.float32),
        ),
        in_specs=[
            pl.BlockSpec((3, SEQ, lanes), lambda i, j: (0, i, j)),
            pl.BlockSpec((SEQ, lanes), lambda i, j: (i, j)),
            pl.BlockSpec((None, 8, SEQ), lambda i, j: (j, 0, i)),
            pl.BlockSpec(tables.shape, lambda i, j: (0, 0, 0)),
        ],
        out_specs=(
            pl.BlockSpec((3, SEQ, lanes), lambda i, j: (0, i, j)),
            pl.BlockSpec((None, 3, lanes), lambda i, j: (i, 0, j)),
        ),
        scratch_shapes=[pltpu.VMEM((2, SEQ, lanes), jnp.float32)],
        compiler_params=pltpu.CompilerParams(vmem_limit_bytes=48 * 1024 * 1024),
        cost_estimate=pl.CostEstimate(
            flops=rows * SEQ * width * 20, bytes_accessed=rows * width * 26, transcendentals=0
        ),
        name="attend_backward",
    )(qkv, grad, logs, tables)
    return grads, jnp.sum(sums, 0)


MESH = pl.DeviceIdType.MESH


def partners():
    me = lax.axis_index("tensor")
    return me, me + 1 - 2 * (me % 2), (me + 2) % 4


def greet(devices):
    barrier = pltpu.get_barrier_semaphore()
    for device in devices:
        pl.semaphore_signal(barrier, inc=1, device_id={"tensor": device}, device_id_type=MESH)
    pl.semaphore_wait(barrier, len(devices))


def gather_kernel(block_ref, whole_ref, send_sem, recv_sem, local_sem):
    me, along_x, along_y = partners()
    rows = block_ref.shape[0]
    half = rows // 2

    def part(owner, which):
        return whole_ref.at[pl.ds(pl.multiple_of(owner * rows + which * half, half), half)]

    def send(source, owner, which, target, index):
        copy = pltpu.make_async_remote_copy(
            src_ref=source,
            dst_ref=part(owner, which),
            send_sem=send_sem.at[index],
            recv_sem=recv_sem.at[index],
            device_id={"tensor": target},
            device_id_type=MESH,
        )
        copy.start()
        return copy

    mine = pltpu.make_async_copy(block_ref, whole_ref.at[pl.ds(pl.multiple_of(me * rows, rows), rows)], local_sem)
    mine.start()
    greet((along_x, along_y))
    halves = [block_ref.at[pl.ds(0, half)], block_ref.at[pl.ds(half, half)]]
    x_first = send(halves[0], me, 0, along_x, 0)
    y_first = send(halves[1], me, 1, along_y, 1)
    x_second = send(halves[1], me, 1, along_x, 2)
    y_second = send(halves[0], me, 0, along_y, 3)
    x_first.wait_recv()
    y_third = send(part(along_x, 0), along_x, 0, along_y, 4)
    y_first.wait_recv()
    x_third = send(part(along_y, 1), along_y, 1, along_x, 5)
    for copy in (x_second, y_second, y_third, x_third):
        copy.wait_recv()
    for copy in (x_first, y_first, x_second, y_second, y_third, x_third):
        copy.wait_send()
    mine.wait()


def square_gather(block):
    rows, width = block.shape
    return pl.pallas_call(
        gather_kernel,
        out_shape=jax.ShapeDtypeStruct((4 * rows, width), block.dtype),
        in_specs=[pl.BlockSpec(memory_space=pltpu.VMEM)],
        out_specs=pl.BlockSpec(memory_space=pl.ANY),
        scratch_shapes=[
            pltpu.SemaphoreType.DMA((6,)),
            pltpu.SemaphoreType.DMA((6,)),
            pltpu.SemaphoreType.DMA,
        ],
        compiler_params=pltpu.CompilerParams(collective_id=0, has_side_effects=True),
        cost_estimate=pl.CostEstimate(flops=0, bytes_accessed=rows * width * 120, transcendentals=0),
        name="square_gather",
    )(block)


def reduce_kernel(terms_ref, ready_ref, out_ref, first_x, first_y, staged, second, send_sem, recv_sem):
    del ready_ref
    me, along_x, along_y = partners()
    rows = out_ref.shape[0]
    half = rows // 2
    corner = 3 - me

    def term(owner, which):
        return terms_ref.at[pl.ds(pl.multiple_of(owner * rows + which * half, half), half)]

    def send(source, target_ref, target, index):
        copy = pltpu.make_async_remote_copy(
            src_ref=source,
            dst_ref=target_ref,
            send_sem=send_sem.at[index],
            recv_sem=recv_sem.at[index],
            device_id={"tensor": target},
            device_id_type=MESH,
        )
        copy.start()
        return copy

    greet((along_x, along_y))
    x_on = send(term(corner, 0), first_x.at[1], along_x, 0)
    y_on = send(term(corner, 1), first_y.at[1], along_y, 1)
    x_own = send(term(along_x, 0), first_x.at[0], along_x, 2)
    y_own = send(term(along_y, 1), first_y.at[0], along_y, 3)

    def added(one, two):
        return (one.astype(jnp.float32) + two.astype(jnp.float32)).astype(jnp.bfloat16)

    x_on.wait_recv()
    staged[0] = added(term(along_y, 0)[...], first_x[1])
    y_last = send(staged.at[0], second.at[0], along_y, 4)
    y_on.wait_recv()
    staged[1] = added(term(along_x, 1)[...], first_y[1])
    x_last = send(staged.at[1], second.at[1], along_x, 5)
    x_own.wait_recv()
    out_ref[:half] = term(me, 0)[...].astype(jnp.float32) + first_x[0].astype(jnp.float32)
    y_own.wait_recv()
    out_ref[half:] = term(me, 1)[...].astype(jnp.float32) + first_y[0].astype(jnp.float32)
    y_last.wait_recv()
    out_ref[:half] += second[0].astype(jnp.float32)
    x_last.wait_recv()
    out_ref[half:] += second[1].astype(jnp.float32)
    for copy in (x_on, y_on, x_own, y_own, y_last, x_last):
        copy.wait_send()


def square_reduce(terms, ready, name):
    rows, width = terms.shape[0] // 4, terms.shape[1]
    part = pltpu.VMEM((2, rows // 2, width), jnp.bfloat16)
    return pl.pallas_call(
        reduce_kernel,
        out_shape=jax.ShapeDtypeStruct((rows, width), jnp.float32),
        in_specs=[pl.BlockSpec(memory_space=pltpu.VMEM), pl.BlockSpec(memory_space=pl.ANY)],
        out_specs=pl.BlockSpec(memory_space=pltpu.VMEM),
        scratch_shapes=[
            part,
            part,
            part,
            part,
            pltpu.SemaphoreType.DMA((6,)),
            pltpu.SemaphoreType.DMA((6,)),
        ],
        compiler_params=pltpu.CompilerParams(
            collective_id=name, has_side_effects=True, vmem_limit_bytes=24 * 1024 * 1024
        ),
        cost_estimate=pl.CostEstimate(flops=0, bytes_accessed=rows * width * 240, transcendentals=0),
        name="square_reduce",
    )(terms, ready)


def start_kernel(
    a_ref, dy_ref, bias_ref, wq_ref, wo_ref, a_all, dy_all, bias_all, wq_all, wo_all,
    square_send, square_recv, bias_send, bias_recv, line_send, line_recv, core_send, core_recv, local_sem,
):
    place, along_x, along_y = partners()
    me = lax.axis_index("dp")
    chip, core = me // 2, me % 2
    sibling = me + 1 - 2 * core
    rows = a_ref.shape[0]
    half = rows // 2
    depth = wq_ref.shape[1]

    def start(source, target, send_sem, recv_sem, device):
        copy = pltpu.make_async_remote_copy(
            src_ref=source, dst_ref=target, send_sem=send_sem, recv_sem=recv_sem,
            device_id=device, device_id_type=MESH,
        )
        copy.start()
        return copy

    def piece(part, owner):
        if part < 3:
            return wq_all.at[part, pl.ds(pl.multiple_of(owner * depth, depth), depth)]
        width = wo_ref.shape[1]
        return wo_all.at[:, pl.ds(pl.multiple_of(owner * width, width), width)]

    def own(part):
        return wq_ref.at[part] if part < 3 else wo_ref

    def turned(step):
        return 2 * ((chip + step) % 4) + core

    locals_ = [
        pltpu.make_async_copy(a_ref, a_all.at[pl.ds(pl.multiple_of(place * rows, rows), rows)], local_sem.at[0]),
        pltpu.make_async_copy(dy_ref, dy_all.at[pl.ds(pl.multiple_of(place * rows, rows), rows)], local_sem.at[1]),
    ] + [pltpu.make_async_copy(own(part), piece(part, me), local_sem.at[2 + part]) for part in range(4)]
    for copy in locals_:
        copy.start()
    bias_all[me] = bias_ref[...]

    barrier = pltpu.get_barrier_semaphore()
    for step in range(1, 8):
        pl.semaphore_signal(barrier, inc=1, device_id={"dp": (me + step) % 8}, device_id_type=MESH)
    for device in (along_x, along_y):
        pl.semaphore_signal(barrier, inc=1, device_id={"tensor": device}, device_id_type=MESH)
    pl.semaphore_wait(barrier, 9)

    def rows_of(whole, owner, which):
        return whole.at[pl.ds(pl.multiple_of(owner * rows + which * half, half), half)]

    def square_first(block, whole, base):
        halves = [block.at[pl.ds(0, half)], block.at[pl.ds(half, half)]]
        plan = [(0, along_x), (1, along_y), (1, along_x), (0, along_y)]
        return [
            start(halves[which], rows_of(whole, place, which), square_send.at[base + i], square_recv.at[base + i], {"tensor": device})
            for i, (which, device) in enumerate(plan)
        ]

    def square_next(whole, base, copies):
        copies[0].wait_recv()
        on_y = start(rows_of(whole, along_x, 0), rows_of(whole, along_x, 0), square_send.at[base + 4], square_recv.at[base + 4], {"tensor": along_y})
        copies[1].wait_recv()
        on_x = start(rows_of(whole, along_y, 1), rows_of(whole, along_y, 1), square_send.at[base + 5], square_recv.at[base + 5], {"tensor": along_x})
        return copies + [on_y, on_x]

    a_copies = square_first(a_ref, a_all, 0)
    bias_copies = [
        start(bias_all.at[me], bias_all.at[me], bias_send.at[step], bias_recv.at[step], {"dp": (me + step) % 8})
        for step in range(1, 8)
    ]

    def line(part, slot, step, source=None):
        owner = me if source is None else source
        return pltpu.make_async_remote_copy(
            src_ref=own(part) if source is None else piece(part, source),
            dst_ref=piece(part, owner),
            send_sem=line_send.at[part, slot if source is None else 0],
            recv_sem=line_recv.at[part, slot],
            device_id={"dp": turned(step)},
            device_id_type=MESH,
        )

    def to_sibling(part, slot):
        owner = turned(slot)
        return start(
            own(part) if slot == 0 else piece(part, owner), piece(part, owner),
            core_send.at[part, slot], core_recv.at[part, slot], {"dp": sibling},
        )

    for part in range(4):
        line(part, 2, 2).start()

        @pl.when(chip % 2 == 0)
        def _():
            line(part, 3, 1).start()

        @pl.when(chip % 2 == 1)
        def _():
            line(part, 1, 3).start()

    def came(part, slot):
        line(part, slot, 4 - slot).wait_recv()

    def onward(part):
        @pl.when(chip == 2)
        def _():
            line(part, 1, 1, turned(2)).start()
            line(part, 1, 3).start()

        @pl.when(chip == 1)
        def _():
            line(part, 3, 3, turned(2)).start()
            line(part, 3, 1).start()

    siblings = [to_sibling(part, 0) for part in range(4)]
    a_copies = square_next(a_all, 0, a_copies)
    dy_copies = square_first(dy_ref, dy_all, 6)
    for part in range(4):
        came(part, 2)
        onward(part)
        siblings.append(to_sibling(part, 2))
    dy_copies = square_next(dy_all, 6, dy_copies)
    for part in range(4):
        for slot in (1, 3):
            came(part, slot)
            siblings.append(to_sibling(part, slot))
    for copy in a_copies[2:] + dy_copies[2:] + bias_copies + siblings:
        copy.wait_recv()
    for copy in a_copies + dy_copies + bias_copies + siblings:
        copy.wait_send()
    for part in range(4):
        line(part, 2, 2).wait_send()

        @pl.when(chip < 3)
        def _():
            line(part, 3, 1).wait_send()

        @pl.when(chip > 0)
        def _():
            line(part, 1, 3).wait_send()

        @pl.when(chip == 2)
        def _():
            line(part, 1, 1, turned(2)).wait_send()

        @pl.when(chip == 1)
        def _():
            line(part, 3, 3, turned(2)).wait_send()

    for copy in locals_:
        copy.wait()


def start_gather(a, dy, bias, wq, wo):
    dma = pltpu.SemaphoreType.DMA
    anywhere = pl.BlockSpec(memory_space=pl.ANY)
    local_ = pl.BlockSpec(memory_space=pltpu.VMEM)
    shape = jax.ShapeDtypeStruct
    return pl.pallas_call(
        start_kernel,
        out_shape=(
            shape((4 * a.shape[0], a.shape[1]), a.dtype),
            shape((4 * dy.shape[0], dy.shape[1]), dy.dtype),
            shape((8, *bias.shape), bias.dtype),
            shape((wq.shape[0], 8 * wq.shape[1], wq.shape[2]), wq.dtype),
            shape((wo.shape[0], 8 * wo.shape[1]), wo.dtype),
        ),
        in_specs=[local_] * 5,
        out_specs=(anywhere, anywhere, local_, anywhere, anywhere),
        scratch_shapes=[
            dma((12,)), dma((12,)), dma((8,)), dma((8,)),
            dma((4, 4)), dma((4, 4)), dma((4, 4)), dma((4, 4)), dma((6,)),
        ],
        compiler_params=pltpu.CompilerParams(collective_id=2, has_side_effects=True),
        cost_estimate=pl.CostEstimate(flops=0, bytes_accessed=200_000_000, transcendentals=0),
        name="start_gather",
    )(a, dy, bias, wq, wo)


def total_kernel(split, values_ref, out_ref, corners, came, mine, slots_ref, send_sem, recv_sem):
    place, along_x, along_y = partners()
    me = lax.axis_index("dp")
    chip, sibling = me // 2, me + 1 - 2 * (me % 2)
    others = [{"tensor": device} for device in (along_x, along_y, 3 - place)]
    others += [{"dp": sibling}] + [{"dp": (me + 2 * step) % 8} for step in (1, 2, 3)]
    barrier = pltpu.get_barrier_semaphore()
    for other in others:
        pl.semaphore_signal(barrier, inc=1, device_id=other, device_id_type=MESH)
    pl.semaphore_wait(barrier, len(others))

    def start(source, target, index):
        copy = pltpu.make_async_remote_copy(
            src_ref=source,
            dst_ref=target,
            send_sem=send_sem.at[index],
            recv_sem=recv_sem.at[index],
            device_id=others[index],
            device_id_type=MESH,
        )
        copy.start()
        return copy

    corners[place] = values_ref[:, :split]
    copies = [start(corners.at[place], corners.at[place], index) for index in range(3)]
    for copy in copies:
        copy.wait_recv()
    mine[:, :split] = (corners[0] + corners[1]) + (corners[2] + corners[3])
    mine[:, split:] = values_ref[:, split:]
    copies.append(start(mine, came, 3))
    copies[3].wait_recv()
    slots_ref[chip] = mine[...] + came[...]
    last = [start(slots_ref.at[chip], slots_ref.at[chip], index) for index in (4, 5, 6)]
    for copy in last:
        copy.wait_recv()
    out_ref[...] = (slots_ref[0] + slots_ref[1]) + (slots_ref[2] + slots_ref[3])
    for copy in copies + last:
        copy.wait_send()


def slice_total(values, split):
    dma = pltpu.SemaphoreType.DMA
    shape = values.shape
    return pl.pallas_call(
        functools.partial(total_kernel, split),
        out_shape=jax.ShapeDtypeStruct(shape, values.dtype),
        in_specs=[pl.BlockSpec(memory_space=pltpu.VMEM)],
        out_specs=pl.BlockSpec(memory_space=pltpu.VMEM),
        scratch_shapes=[
            pltpu.VMEM((4, 8, split), values.dtype),
            pltpu.VMEM(shape, values.dtype),
            pltpu.VMEM(shape, values.dtype),
            pltpu.VMEM((4, *shape), values.dtype),
            dma((7,)),
            dma((7,)),
        ],
        compiler_params=pltpu.CompilerParams(collective_id=3, has_side_effects=True),
        cost_estimate=pl.CostEstimate(flops=0, bytes_accessed=30_000_000, transcendentals=0),
        name="slice_total",
    )(values)


def after(late, early):
    return lax.optimization_barrier((late, early))[0]


class Plain:
    def gather_rows(self, block):
        return lax.all_gather(block, "tensor", axis=0, tiled=True)

    def reduce_rows(self, terms, ready, name):
        return lax.psum_scatter(terms, "tensor", scatter_dimension=0, tiled=True).astype(jnp.float32)

    def begin(self, a, dy, bias, w_qkv, w_output):
        return (
            self.gather_rows(a),
            self.gather_rows(dy),
            lax.all_gather(bias, "dp", axis=2, tiled=True),
            gather_dp(w_qkv, 1),
            gather_dp(w_output, 1),
        )

    def totals(self, vectors, sums):
        return lax.psum(vectors, ("dp", "tensor")), lax.psum(sums, "dp")


class Line(Plain):
    def gather_rows(self, block):
        return square_gather(block)

    def reduce_rows(self, terms, ready, name):
        return square_reduce(terms, ready, name)

    def begin(self, a, dy, bias, w_qkv, w_output):
        parts, heads, few = bias.shape
        flat = bias.astype(jnp.float32).reshape(-1)
        width = -(-flat.shape[0] // 1024) * 1024
        flat = jnp.pad(flat, (0, width - flat.shape[0])).reshape(8, -1)
        a, dy, came, w_qkv, w_output = start_gather(a, dy, flat, w_qkv, w_output)
        came = came.reshape(8, -1)[:, : parts * heads * few].reshape(8, parts, heads, few)
        return a, dy, came.transpose(1, 2, 0, 3).reshape(parts, heads, -1), w_qkv, w_output

    def totals(self, vectors, sums):
        split = vectors.size // 8
        flat = sums.reshape(-1)
        width = -(-flat.shape[0] // 1024) * 1024
        flat = jnp.pad(flat, (0, width - flat.shape[0])).reshape(8, -1)
        total = slice_total(jnp.concatenate([vectors.reshape(8, split), flat], 1), split)
        return (
            total[:, :split].reshape(vectors.shape),
            total[:, split:].reshape(-1)[: sums.size].reshape(sums.shape),
        )


def row_major(values):
    return with_layout_constraint(values, Layout(tuple(range(values.ndim))))


def gather_dp(block, axis):
    return row_major(lax.all_gather(block.astype(jnp.bfloat16), "dp", axis=axis, tiled=True))


def scatter_dp(terms, axis):
    return lax.psum_scatter(terms.astype(jnp.bfloat16), "dp", scatter_dimension=axis, tiled=True).astype(
        jnp.float32
    )


def local(
    routes,
    inputs,
    cotangent,
    gains,
    shifts,
    qkv_weight,
    biases,
    out_weight,
    gate_up,
    down_weight,
    momentum_gains,
    momentum_shifts,
    momentum_qkv,
    momentum_biases,
    momentum_out,
    momentum_gate,
    momentum_down,
    variance_gains,
    variance_shifts,
    variance_qkv,
    variance_biases,
    variance_out,
    variance_gate,
    variance_down,
):
    low = jnp.bfloat16
    local_heads = biases.shape[1]
    local_width = qkv_weight.shape[2]
    head_size = local_width // local_heads
    xin = inputs.astype(jnp.float32)
    first_out, first_normed, first_recip = layer_norm(xin, gains[0], shifts[0])
    a_all, dy_all, bias_all, w_qkv, w_output = routes.begin(
        first_out.astype(low), cotangent, biases.astype(low), qkv_weight.astype(low), out_weight.astype(low)
    )
    bias_all = bias_all.reshape(3, local_width).astype(jnp.float32)
    w_gate_up = gather_dp(after(gate_up, w_output), 1)
    lin = jnp.einsum("rd,kdc->krc", a_all, w_qkv, preferred_element_type=jnp.float32)
    qkv, heads, logs = attention_forward(lin, bias_all, head_size)
    resid = xin + routes.reduce_rows(mxu(heads, w_output, NN).astype(low), logs, 4)
    second_out, second_normed, second_recip = layer_norm(resid, gains[1], shifts[1])
    m_all = routes.gather_rows(second_out.astype(low))
    w_down = gather_dp(after(down_weight, (w_gate_up, m_all)), 1)
    gate_vals = jnp.einsum("rd,kdc->krc", m_all, w_gate_up, preferred_element_type=jnp.float32)
    gate_lin, upward = gate_vals[0], gate_vals[1]
    sigmoid_gate = jax.nn.sigmoid(gate_lin)
    silu_gate = gate_lin * sigmoid_gate
    hidden = (silu_gate * upward).astype(low)
    down_terms = mxu(hidden, dy_all, TN).astype(low)
    down_grad = scatter_dp(down_terms, 1)
    w_down = after(w_down, down_terms)
    hidden_grad = mxu(dy_all, w_down, NT)
    gate_grad_low = (
        hidden_grad * upward * sigmoid_gate * (1.0 + gate_lin * (1.0 - sigmoid_gate))
    ).astype(low)
    up_grad_low = (hidden_grad * silu_gate).astype(low)
    both_grads = jnp.stack([gate_grad_low, up_grad_low], 0)
    gate_terms = jnp.einsum("rd,krc->kdc", m_all, both_grads, preferred_element_type=jnp.float32)
    gate_terms = row_major(gate_terms.astype(low))
    second_terms = jnp.einsum(
        "krc,kdc->rd", both_grads, w_gate_up, preferred_element_type=jnp.float32
    ).astype(low)
    block_terms = mxu(hidden, w_down, NN).astype(low)
    gate_grad = scatter_dp(after(gate_terms, (down_grad, second_terms, block_terms)), 1)
    second_grad = routes.reduce_rows(second_terms, down_grad, 5)
    resid_grad = cotangent.astype(jnp.float32) + norm_back(
        second_grad, second_normed, second_recip, gains[1]
    )
    gain_second = jnp.sum(second_grad * second_normed, 0)
    shift_second = jnp.sum(second_grad, 0)
    resid_full = routes.gather_rows(resid_grad.astype(low))
    out_terms = mxu(heads, resid_full, TN).astype(low)
    heads_grad = mxu(resid_full, w_output, NT).astype(low)
    lin_grads, bias_terms = attention_backward(qkv, heads_grad, logs, head_size)
    qkv_terms = jnp.einsum("rd,krc->kdc", a_all, lin_grads, preferred_element_type=jnp.float32)
    qkv_terms = row_major(qkv_terms.astype(low))
    out_grad = scatter_dp(after(out_terms, (gate_grad, lin_grads)), 1)
    down_sum = routes.reduce_rows(block_terms, bias_terms, 6)
    qkv_grad = scatter_dp(after(qkv_terms, (out_grad, down_sum)), 1)
    first_terms = jnp.einsum(
        "krc,kdc->rd", lin_grads, w_qkv, preferred_element_type=jnp.float32
    ).astype(low)
    first_grad = routes.reduce_rows(first_terms, bias_terms, 7)
    input_grad = resid_grad + norm_back(first_grad, first_normed, first_recip, gains[0])
    vectors = jnp.stack(
        [jnp.sum(first_grad * first_normed, 0), gain_second, jnp.sum(first_grad, 0), shift_second]
    )
    vectors, bias_sum = routes.totals(vectors, bias_terms)
    gains_grad, shifts_grad = vectors[:2], vectors[2:]
    out_grad, down_grad, gate_grad = after((out_grad, down_grad, gate_grad), first_grad)
    per_dp = biases.shape[2]
    biases_grad = lax.dynamic_slice_in_dim(
        bias_sum.reshape(3, local_heads, head_size), lax.axis_index("dp") * per_dp, per_dp, 2
    )
    block_out = (resid + down_sum).astype(low)
    gain_new = adamw(gains, gains_grad, momentum_gains, variance_gains, 0.0, vector_rate)
    shift_new = adamw(shifts, shifts_grad, momentum_shifts, variance_shifts, 0.0, vector_rate)
    qkv_new = adamw(qkv_weight, qkv_grad, momentum_qkv, variance_qkv, decay_rate, learn_rate)
    bias_new = adamw(biases, biases_grad, momentum_biases, variance_biases, 0.0, vector_rate)
    out_new = adamw(out_weight, out_grad, momentum_out, variance_out, decay_rate, learn_rate)
    gate_new = adamw(gate_up, gate_grad, momentum_gate, variance_gate, decay_rate, learn_rate)
    down_new = adamw(down_weight, down_grad, momentum_down, variance_down, decay_rate, learn_rate)
    return (
        block_out,
        input_grad,
        gains_grad,
        shifts_grad,
        qkv_grad,
        biases_grad,
        out_grad,
        gate_grad,
        down_grad,
        gain_new[0],
        shift_new[0],
        qkv_new[0],
        bias_new[0],
        out_new[0],
        gate_new[0],
        down_new[0],
        gain_new[1],
        shift_new[1],
        qkv_new[1],
        bias_new[1],
        out_new[1],
        gate_new[1],
        down_new[1],
        gain_new[2],
        shift_new[2],
        qkv_new[2],
        bias_new[2],
        out_new[2],
        gate_new[2],
        down_new[2],
    )


def solution(mesh):
    routes = Line() if dict(mesh.shape) == {"dp": 8, "tensor": 4} else Plain()

    def step(*arrays):
        return local(routes, *arrays)

    return jax.shard_map(
        step,
        mesh=mesh,
        in_specs=(
            P(("dp", "tensor"), None),
            P(("dp", "tensor"), None),
            P(),
            P(),
            P(None, "dp", "tensor"),
            P(None, "tensor", "dp"),
            P("tensor", "dp"),
            P(None, "dp", "tensor"),
            P("tensor", "dp"),
            P(),
            P(),
            P(None, "dp", "tensor"),
            P(None, "tensor", "dp"),
            P("tensor", "dp"),
            P(None, "dp", "tensor"),
            P("tensor", "dp"),
            P(),
            P(),
            P(None, "dp", "tensor"),
            P(None, "tensor", "dp"),
            P("tensor", "dp"),
            P(None, "dp", "tensor"),
            P("tensor", "dp"),
        ),
        out_specs=(
            P(("dp", "tensor"), None),
            P(("dp", "tensor"), None),
            P(),
            P(),
            P(None, "dp", "tensor"),
            P(None, "tensor", "dp"),
            P("tensor", "dp"),
            P(None, "dp", "tensor"),
            P("tensor", "dp"),
            P(),
            P(),
            P(None, "dp", "tensor"),
            P(None, "tensor", "dp"),
            P("tensor", "dp"),
            P(None, "dp", "tensor"),
            P("tensor", "dp"),
            P(),
            P(),
            P(None, "dp", "tensor"),
            P(None, "tensor", "dp"),
            P("tensor", "dp"),
            P(None, "dp", "tensor"),
            P("tensor", "dp"),
            P(),
            P(),
            P(None, "dp", "tensor"),
            P(None, "tensor", "dp"),
            P("tensor", "dp"),
            P(None, "dp", "tensor"),
            P("tensor", "dp"),
        ),
        check_vma=False,
    )
```

time: 1400 us -> 627 us (0.45)
  waiting for transfers between devices: 934 us -> 39.4 us
  Pallas kernels: 0 us -> 351 us
  blocking collectives: 83.7 us -> 0 us
  matrix products: 209 us -> 131 us
  local copies, waits for them, and re-layouts: 64.3 us -> 27.1 us
  other arithmetic: 84.8 us -> 53.5 us
    reduce_scatter x8 -> x4, waiting for transfers between devices: 536 us -> 11.1 us  [scatter_dp(): lax.psum_scatter(terms.astype(jnp.bfloat16), 'dp', scatter_dimension=axis...]
    all_gather x8 -> x2, waiting for transfers between devices: 397 us -> 28.2 us  [gather_dp(): lax.all_gather(block.astype(jnp.bfloat16), 'dp', axis=axis, tiled=True)]
    pallas_call x0 -> x10, Pallas kernels: none -> 351 us  [the longest x4 142 us: square_reduce(): pl.pallas_call(reduce_kernel, out_shape=jax.ShapeDtypeStruct((rows, width...]
    dot_general x24 -> x12, matrix products: 209 us -> 131 us  [the longest x6 45.9 us: mxu(): lax.dot_general(left, right, dims, preferred_element_type=jnp.float32)]
    psum x1 -> x0, blocking collectives: 39.2 us -> none  [local(): lax.psum((gain_terms, shift_terms), ('dp', 'tensor'))]
    unnamed x181 -> x111, local copies, waits for them, and re-layouts: 56.1 us -> 17.3 us
    unnamed x1 -> x0, blocking collectives: 28.8 us -> none
    all_gather x1 -> x0, blocking collectives: 15.6 us -> none  [local(): lax.all_gather(biases.astype(jnp.bfloat16), 'dp', axis=2, tiled=True)]
  transfers between devices with their start and end apart: 16 -> 6, of which waited for: 12 -> 3; matrix products, arithmetic and copies ran while one was open for 20% -> 28% of each run, Pallas kernels for 0% -> 44%
where the time goes in v1:
time: 627 us; the launch traced here: 617 us
  Pallas kernels  351 us (56%)
  matrix products  131 us (21%)
  other arithmetic  53.5 us (9%)
  waiting for transfers between devices  39.4 us (6%)
  local copies, waits for them, and re-layouts  27.1 us (4%)
  between operations  15 us (2%)
    pallas_call x4, Pallas kernels, square_reduce(): pl.pallas_call(reduce_kernel, out_shape=jax.ShapeDtypeStruct((rows, width...  142 us
    pallas_call x1, Pallas kernels, start_gather(): pl.pallas_call(start_kernel, out_shape=(shape((4 * a.shape[0], a.shape[1]...  79.6 us
    pallas_call x2, Pallas kernels, square_gather(): pl.pallas_call(gather_kernel, out_shape=jax.ShapeDtypeStruct((4 * rows, w...  72.3 us
    dot_general x6, matrix products, mxu(): lax.dot_general(left, right, dims, preferred_element_type=jnp.float32)  45.9 us
    all_gather x2, waiting for transfers between devices, gather_dp(): lax.all_gather(block.astype(jnp.bfloat16), 'dp', axis=axis, tiled=True)  28.2 us
    pallas_call x1, Pallas kernels, attention_backward(): pl.pallas_call(functools.partial(backward_kernel, head_size), grid=(rows...  23.4 us
    pallas_call x1, Pallas kernels, slice_total(): pl.pallas_call(functools.partial(total_kernel, split), out_shape=jax.Shap...  18.5 us
    dot_general x1, matrix products, local(): jnp.einsum('krc,kdc->rd', both_grads, w_gate_up, preferred_element_type=j...  18.3 us
  transfers between devices with their start and end apart: 6, of which 3 were waited for; matrix products, arithmetic and copies ran while one was open for 28% of the time, Pallas kernels for 44%

profile of v1, /device:TPU:0, one launch (start us, length us, event | category | flops | bytes accessed | tf_op | source)
XLA Modules:
  0.0 617.1 jit_solution(10668438169429362308)
XLA Ops:
  14.6 79.6 %start_gather.1 = (bf16[1024,2048]{1,0:T(8,128)(2,1)}, bf16[1024,2048]{1,0:T(8,128)(2,1)}, f32[8,8,128]{2,1,0:T(8,128)}, bf16[3,2048,512]{2,1,0:T(8,128)(2,1)}, bf16[512,2048]{1,0:T(8,128)(2,1)}) custom-call(bf16[256,2048]{1,0:T(8,128)(2,1)} %fusion.19.a_ref, bf16[256,2048]{1,0:T(8,128)(2,1)} %dy_ref.1, f32[8,128]{1,0:T(8,128)} %bitcast_convert_fusion.2.bias_ref, ...), custom_call_target="tpu_custom_call" | custom-call | bytes 200000000 | tf_op jit(solution)/shard_map/start_gather/pallas_call | solution.py:536
  97.7 11.8 %fusion.9.lin_ref = f32[3,1024,512]{2,1,0:T(8,128)} fusion(bf16[3,2048,512]{2,1,0:T(8,128)(2,1)} %get-tuple-element.49, bf16[1024,2048]{1,0:T(8,128)(2,1)} %get-tuple-element.50), kind=kOutput, calls=%fused_computation.31 | convolution fusion | flops 6442450944 | bytes 16777216 | tf_op jit(solution)/shard_map/rd,kdc->krc/dot_general | solution.py:722
  109.5 14.9 %attend_forward.1 = (bf16[3,1024,512]{2,1,0:T(8,128)(2,1)S(1)}, bf16[1024,512]{1,0:T(8,128)(2,1)S(1)}, f32[2,8,1024]{2,1,0:T(8,128)S(1)}) custom-call(f32[3,1024,512]{2,1,0:T(8,128)} %fusion.9.lin_ref, f32[3,512]{1,0:T(4,128)S(1)} %reshape_reshape.6.bias_ref, f32[3,1024,128]{2,1,0:T(8,128)S(1)} %copy-done.6), custom_call_target="tpu_custom_call" | custom-call | flops 4294967296 | bytes 13631488 | tf_op jit(solution)/shard_map/attend_forward/pallas_call | solution.py:129
  126.8 38.0 %square_reduce.4 = f32[256,2048]{1,0:T(8,128)S(1)} custom-call(bf16[1024,2048]{1,0:T(8,128)(2,1)S(1)} %convolution_convert_fusion.2.terms_ref, f32[2,8,1024]{2,1,0:T(8,128)S(1)} %get-tuple-element.54.ready_ref.lse_ref), custom_call_target="tpu_custom_call" | custom-call | bytes 125829120 | tf_op jit(solution)/shard_map/square_reduce/pallas_call | solution.py:357
  167.8 37.7 %square_gather.2 = bf16[1024,2048]{1,0:T(8,128)(2,1)} custom-call(bf16[256,2048]{1,0:T(8,128)(2,1)} %add_convert_fusion.1.block_ref), custom_call_target="tpu_custom_call" | custom-call | bytes 62914560 | tf_op jit(solution)/shard_map/square_gather/pallas_call | solution.py:289
  206.6 16.6 %convolution_bitcast_fusion = f32[2,1024,1408]{1,2,0:T(8,128)S(1)} fusion(bf16[2,2048,1408]{2,1,0:T(8,128)(2,1)} %all-gather.3.cloned.1.call-done, bf16[1024,2048]{1,0:T(8,128)(2,1)} %square_gather.2), kind=kOutput, calls=%fused_computation.4 | convolution fusion | flops 11811160064 | bytes 27262976 | tf_op jit(solution)/shard_map/rd,kdc->krc/dot_general | solution.py:728
  230.2 8.1 %convolution_convert_fusion = bf16[1408,2048]{1,0:T(8,128)(2,1)} fusion(bf16[1024,1408]{0,1:T(8,128)(2,1)S(1)} %multiply_convert_fusion.2, bf16[1024,2048]{1,0:T(8,128)(2,1)S(1)} %copy-done.52), kind=kOutput, calls=%fused_computation.3 | convolution fusion | flops 5908463616 | bytes 12845056 | tf_op jit(solution)/shard_map/dot_general | solution.py:84
  238.3 28.2 %all-gather.5.cloned.1.call-done = bf16[1408,2048]{1,0:T(8,128)(2,1)} async-done(((bf16[1408,256]{1,0:T(8,128)(2,1)}), bf16[1408,2048]{1,0:T(8,128)(2,1)}) %all-gather.5.cloned.1.call-update) | async-done | bytes 5767184 | tf_op jit(solution)/shard_map/all_gather | solution.py:676
  266.5 11.6 %convolution_convert_fusion.1.terms_ref = bf16[1024,2048]{1,0:T(8,128)(2,1)} fusion(bf16[1024,1408]{0,1:T(8,128)(2,1)} %copy-done.28, bf16[1408,2048]{1,0:T(8,128)(2,1)} %all-gather.5.cloned.1.call-done), kind=kOutput, calls=%fused_computation.20 | convolution fusion | flops 5907677184 | bytes 12845056 | tf_op jit(solution)/shard_map/dot_general | solution.py:84
  278.1 12.6 %fusion.8 = (bf16[1,1024,1408]{1,2,0:T(8,128)(2,1)}, bf16[1,1024,1408]{1,2,0:T(8,128)(2,1)}) fusion(f32[2,1024,1408]{1,2,0:T(8,128)} %copy-done.18, bf16[1024,2048]{1,0:T(8,128)(2,1)S(1)} %copy-done.53, bf16[1408,2048]{1,0:T(8,128)(2,1)S(1)} %copy-done.51), kind=kOutput, calls=%fused_computation.30 | convolution fusion | flops 5924323328 | bytes 27262976 | tf_op jit(solution)/shard_map/dot_general | solution.py:84
  290.7 17.4 %convert_bitcast_fusion = bf16[2,2048,1408]{2,1,0:T(8,128)(2,1)} fusion(bf16[1024,2048]{1,0:T(8,128)(2,1)S(1)} %copy-done.24, bf16[1,1024,1408]{1,2,0:T(8,128)(2,1)} %get-tuple-element.104, bf16[1,1024,1408]{1,2,0:T(8,128)(2,1)} %get-tuple-element.103), kind=kOutput, calls=%fused_computation | convolution fusion | flops 11819810816 | bytes 21495808 | tf_op jit(solution)/shard_map/rd,krc->kdc/dot_general | solution.py:742
  308.1 18.3 %bitcast_convert_fusion.1.terms_ref = bf16[1024,2048]{1,0:T(8,128)(2,1)} fusion(bf16[2,2048,1408]{2,1,0:T(8,128)(2,1)} %all-gather.3.cloned.1.call-done, bf16[1,1024,1408]{1,2,0:T(8,128)(2,1)} %get-tuple-element.104, bf16[1,1024,1408]{1,2,0:T(8,128)(2,1)} %get-tuple-element.103), kind=kOutput, calls=%fused_computation.2 | convolution fusion | flops 11816140800 | bytes 21495808 | tf_op jit(solution)/shard_map/krc,kdc->rd/dot_general | solution.py:744
  326.4 5.5 reduce-scatter.5.cloned.1.call-done
  335.8 35.2 %square_reduce.5 = f32[256,2048]{1,0:T(8,128)S(1)} custom-call(bf16[1024,2048]{1,0:T(8,128)(2,1)S(1)} %copy-done.3, f32[1408,256]{1,0:T(8,128)S(1)} %convert_element_type.108.ready_ref), custom_call_target="tpu_custom_call" | custom-call | bytes 125829120 | tf_op jit(solution)/shard_map/square_reduce/pallas_call | solution.py:357
  375.0 34.6 %square_gather.3 = bf16[1024,2048]{1,0:T(8,128)(2,1)} custom-call(bf16[256,2048]{1,0:T(8,128)(2,1)} %get-tuple-element.99.block_ref), custom_call_target="tpu_custom_call" | custom-call | bytes 62914560 | tf_op jit(solution)/shard_map/square_gather/pallas_call | solution.py:289
  409.7 5.9 convolution_convert_fusion.3
  415.5 5.5 convolution_convert_fusion.4.grad_ref
  421.0 23.4 %attend_backward.1 = (bf16[3,1024,512]{2,1,0:T(8,128)(2,1)S(1)}, f32[1,3,512]{2,1,0:T(4,128)S(1)}) custom-call(bf16[3,1024,512]{2,1,0:T(8,128)(2,1)} %copy-done.8, bf16[1024,512]{1,0:T(8,128)(2,1)S(1)} %convolution_convert_fusion.4.grad_ref, f32[2,8,1024]{2,1,0:T(8,128)S(1)} %copy-done.5, f32[3,1024,128]{2,1,0:T(8,128)S(1)} %copy-done.7), custom_call_target="tpu_custom_call" | custom-call | flops 10737418240 | bytes 13631488 | tf_op jit(solution)/shard_map/attend_backward/pallas_call | solution.py:206
  446.1 5.6 reduce-scatter.7.cloned.1.call-done
  457.1 35.2 %square_reduce.6 = f32[256,2048]{1,0:T(8,128)S(1)} custom-call(bf16[1024,2048]{1,0:T(8,128)(2,1)S(1)} %copy-done.2, f32[3,512]{1,0:T(4,128)S(1)} %bitcast.87), custom_call_target="tpu_custom_call" | custom-call | bytes 125829120 | tf_op jit(solution)/shard_map/square_reduce/pallas_call | solution.py:357
  493.6 11.4 %convert_bitcast_fusion.1 = bf16[3,2048,512]{2,1,0:T(8,128)(2,1)} fusion(bf16[3,1024,512]{2,1,0:T(8,128)(2,1)S(1)} %copy-done.10, bf16[1024,2048]{1,0:T(8,128)(2,1)} %get-tuple-element.50), kind=kOutput, calls=%fused_computation.5 | convolution fusion | flops 6445596672 | bytes 13631488 | tf_op jit(solution)/shard_map/rd,krc->kdc/dot_general | solution.py:759
  507.4 9.8 %bitcast_convert_fusion.terms_ref = bf16[1024,2048]{1,0:T(8,128)(2,1)S(1)} fusion(bf16[3,1024,512]{2,1,0:T(8,128)(2,1)} %copy-done.9, bf16[3,2048,512]{2,1,0:T(8,128)(2,1)} %get-tuple-element.49), kind=kOutput, calls=%fused_computation.1 | convolution fusion | flops 6444548096 | bytes 13631488 | tf_op jit(solution)/shard_map/krc,kdc->rd/dot_general | solution.py:764
  517.2 33.6 %square_reduce.7 = f32[256,2048]{1,0:T(8,128)S(1)} custom-call(bf16[1024,2048]{1,0:T(8,128)(2,1)S(1)} %bitcast_convert_fusion.terms_ref, f32[3,512]{1,0:T(4,128)S(1)} %bitcast.88), custom_call_target="tpu_custom_call" | custom-call | bytes 125829120 | tf_op jit(solution)/shard_map/square_reduce/pallas_call | solution.py:357
  557.9 18.5 %slice_total.1 = f32[8,1280]{1,0:T(8,128)} custom-call(f32[8,1280]{1,0:T(8,128)} %pad_maximum_fusion.3.values_ref), custom_call_target="tpu_custom_call" | custom-call | bytes 30000000 | tf_op jit(solution)/shard_map/slice_total/pallas_call | solution.py:600
  (180 shorter events, 83.3 us)
Async XLA Ops:
  7.3 198.3 %all-gather.3.cloned.1.call-start = ((), (), s32[]{:S(2)}) async-start(), calls=%async_computation.4 | async-start | bytes 12976128 | tf_op jit(solution)/shard_map/all_gather | solution.py:676
  97.4 169.1 %all-gather.5.cloned.1.call-start = ((), (), s32[]{:S(2)}) async-start(), calls=%async_computation.5 | async-start | bytes 6488064 | tf_op jit(solution)/shard_map/all_gather | solution.py:676
  97.7 11.8 %copy-start.6 = (f32[3,1024,128]{2,1,0:T(8,128)S(1)}, f32[3,1024,128]{2,1,0:T(8,128)}, u32[]{:S(2)}) copy-start(f32[3,1024,128]{2,1,0:T(8,128)} %constant.46.clone.table_ref) | copy-start | bytes 4718596
  109.5 14.9 %copy-start.54 = (bf16[512,2048]{1,0:T(8,128)(2,1)S(1)}, bf16[512,2048]{1,0:T(8,128)(2,1)}, u32[]{:S(2)}) copy-start(bf16[512,2048]{1,0:T(8,128)(2,1)} %get-tuple-element.53) | copy-start | bytes 6291460
  167.8 37.8 %copy-start.22 = (f32[1408,256]{1,0:T(8,128)S(1)}, f32[1408,256]{1,0:T(8,128)}, u32[]{:S(2)}) copy-start(f32[1408,256]{1,0:T(8,128)} %param.33) | copy-start | bytes 4325380
  206.6 125.3 %reduce-scatter.5.cloned.1.call-start = ((), (), s32[]{:S(2)}) async-start(), calls=%async_computation.6 | async-start | bytes 6488064 | tf_op jit(solution)/shard_map/reduce_scatter | solution.py:680
  223.2 5.4 copy-start.18
  223.2 7.0 %copy-start.52 = (bf16[1024,2048]{1,0:T(8,128)(2,1)S(1)}, bf16[1024,2048]{1,0:T(8,128)(2,1)}, u32[]{:S(2)}) copy-start(bf16[1024,2048]{1,0:T(8,128)(2,1)} %get-tuple-element.57) | copy-start | bytes 12582916
  238.2 213.5 %reduce-scatter.7.cloned.1.call-start = ((), (), s32[]{:S(2)}) async-start(), calls=%async_computation.7 | async-start | bytes 12976128 | tf_op jit(solution)/shard_map/reduce_scatter | solution.py:680
  266.5 11.6 %copy-start.51 = (bf16[1408,2048]{1,0:T(8,128)(2,1)S(1)}, bf16[1408,2048]{1,0:T(8,128)(2,1)}, u32[]{:S(2)}) copy-start(bf16[1408,2048]{1,0:T(8,128)(2,1)} %all-gather.5.cloned.1.call-done) | copy-start | bytes 17301508
  266.5 11.6 %copy-start.53 = (bf16[1024,2048]{1,0:T(8,128)(2,1)S(1)}, bf16[1024,2048]{1,0:T(8,128)(2,1)}, u32[]{:S(2)}) copy-start(bf16[1024,2048]{1,0:T(8,128)(2,1)} %get-tuple-element.57) | copy-start | bytes 12582916
  278.1 12.6 %copy-start.24 = (bf16[1024,2048]{1,0:T(8,128)(2,1)S(1)}, bf16[1024,2048]{1,0:T(8,128)(2,1)}, u32[]{:S(2)}) copy-start(bf16[1024,2048]{1,0:T(8,128)(2,1)} %square_gather.2) | copy-start | bytes 12582916
  333.1 261.9 %copy-start = (f32[1408,256]{1,0:T(8,128)}, f32[1408,256]{1,0:T(8,128)S(1)}, u32[]{:S(2)}) copy-start(f32[1408,256]{1,0:T(8,128)S(1)} %convert_element_type.108.ready_ref) | copy-start | bytes 4325380
  333.1 171.9 %reduce-scatter.9.cloned.1.call-start = ((), (), s32[]{:S(2)}) async-start(), calls=%async_computation.8 | async-start | bytes 2359296 | tf_op jit(solution)/shard_map/reduce_scatter | solution.py:680
  335.8 35.2 %copy-start.12 = (f32[256,2048]{1,0:T(8,128)S(1)}, f32[256,2048]{1,0:T(8,128)}, u32[]{:S(2)}) copy-start(f32[256,2048]{1,0:T(8,128)} %copy-done.11) | copy-start | bytes 6291460
  415.5 5.5 copy-start.5
  415.5 5.5 copy-start.7
  454.9 150.3 %reduce-scatter.11.cloned.1.call-start = ((), (), s32[]{:S(2)}) async-start(), calls=%async_computation.9 | async-start | bytes 7077888 | tf_op jit(solution)/shard_map/reduce_scatter | solution.py:680
  457.1 36.5 %copy-start.10 = (bf16[3,1024,512]{2,1,0:T(8,128)(2,1)S(1)}, bf16[3,1024,512]{2,1,0:T(8,128)(2,1)}, u32[]{:S(2)}) copy-start(bf16[3,1024,512]{2,1,0:T(8,128)(2,1)} %copy-done.9) | copy-start | bytes 9437188
  517.2 33.6 %copy-start.14 = (bf16[256,2048]{1,0:T(8,128)(2,1)S(1)}, bf16[256,2048]{1,0:T(8,128)(2,1)}, u32[]{:S(2)}) copy-start(bf16[256,2048]{1,0:T(8,128)(2,1)} %param.25) | copy-start | bytes 3145732
  517.2 33.6 %copy-start.38 = (f32[1,2048]{1,0:T(1,128)S(1)}, f32[1,2048]{1,0:T(1,128)}, u32[]{:S(2)}) copy-start(f32[1,2048]{1,0:T(1,128)} %copy-done.37) | copy-start | bytes 24580
  517.2 33.6 %copy-start.46 = (f32[256]{0:T(256)S(1)}, f32[256]{0:T(256)}, u32[]{:S(2)}) copy-start(f32[256]{0:T(256)} %copy-done.45) | copy-start | bytes 3076
  517.2 33.6 %copy-start.49 = (f32[256]{0:T(256)S(1)}, f32[256]{0:T(256)}, u32[]{:S(2)}) copy-start(f32[256]{0:T(256)} %copy-done.48) | copy-start | bytes 3076
  595.7 5.2 copy-start.26
  (37 other events, 111.7 us)
Sparse Core Ops, SparseCore 0:
  97.5 107.6 all-gather.2
  207.3 59.1 all-gather.4
  268.8 63.0 reduce-scatter.4
  334.0 117.6 reduce-scatter.6
  455.0 34.0 reduce-scatter.8
  506.9 72.0 reduce-scatter.10

commit v2 on v1

--- a/solution.py
+++ b/solution.py
@@ -554,66 +554,307 @@
     )(a, dy, bias, wq, wo)
 
 
-def total_kernel(split, values_ref, out_ref, corners, came, mine, slots_ref, send_sem, recv_sem):
+def tail_kernel(
+    first_ref, block_ref, qkv_ref, proj_ref, normed_ref, recip_ref, gain_ref, grad_ref, resid_ref, second_ref, bias_ref,
+    input_out, block_out, qkv_out, proj_out, vector_out, bias_out,
+    square_x, square_y, staged, square_last, core_qkv, core_proj, near_qkv, near_proj,
+    corners, vector_mine, vector_came, vector_slots, bias_mine, bias_came, bias_slots,
+    square_send, square_recv, core_send, core_recv, line_send, line_recv, vector_send, vector_recv, bias_send, bias_recv,
+):
     place, along_x, along_y = partners()
+    corner = 3 - place
     me = lax.axis_index("dp")
-    chip, sibling = me // 2, me + 1 - 2 * (me % 2)
-    others = [{"tensor": device} for device in (along_x, along_y, 3 - place)]
-    others += [{"dp": sibling}] + [{"dp": (me + 2 * step) % 8} for step in (1, 2, 3)]
-    barrier = pltpu.get_barrier_semaphore()
-    for other in others:
-        pl.semaphore_signal(barrier, inc=1, device_id=other, device_id_type=MESH)
-    pl.semaphore_wait(barrier, len(others))
-
-    def start(source, target, index):
+    chip, core = me // 2, me % 2
+    sibling = me + 1 - 2 * core
+    rows = input_out.shape[0]
+    half = rows // 2
+    depth = qkv_out.shape[1]
+    width = proj_out.shape[1]
+    low, wide = jnp.bfloat16, jnp.float32
+
+    def start(source, target, send_sem, recv_sem, device):
         copy = pltpu.make_async_remote_copy(
-            src_ref=source,
-            dst_ref=target,
-            send_sem=send_sem.at[index],
-            recv_sem=recv_sem.at[index],
-            device_id=others[index],
-            device_id_type=MESH,
+            src_ref=source, dst_ref=target, send_sem=send_sem, recv_sem=recv_sem,
+            device_id=device, device_id_type=MESH,
         )
         copy.start()
         return copy
 
-    corners[place] = values_ref[:, :split]
-    copies = [start(corners.at[place], corners.at[place], index) for index in range(3)]
-    for copy in copies:
+    barrier = pltpu.get_barrier_semaphore()
+    chips = [{"dp": (me + 2 * step) % 8} for step in (1, 2, 3)]
+    square = [{"tensor": device} for device in (along_x, along_y, corner)]
+    for other in square + [{"dp": sibling}] + chips:
+        pl.semaphore_signal(barrier, inc=1, device_id=other, device_id_type=MESH)
+    pl.semaphore_wait(barrier, 7)
+
+    def turned(slot, which):
+        return 2 * ((chip + slot) % 4) + which
+
+    def qkv_part(owner):
+        return qkv_ref.at[:, pl.ds(pl.multiple_of(owner * depth, depth), depth)]
+
+    def proj_part(owner):
+        return proj_ref.at[:, pl.ds(pl.multiple_of(owner * width, width), width)]
+
+    exchange = {}
+    for slot in (3, 1, 2, 0):
+        owner = turned(slot, 1 - core)
+        exchange[slot] = [
+            start(qkv_part(owner), core_qkv.at[slot], core_send.at[0, slot], core_recv.at[0, slot], {"dp": sibling}),
+            start(proj_part(owner), core_proj.at[slot], core_send.at[1, slot], core_recv.at[1, slot], {"dp": sibling}),
+        ]
+
+    def square_first(terms, base, which):
+        def term(owner, part):
+            return terms.at[pl.ds(pl.multiple_of(owner * rows + part * half, half), half)]
+
+        plan = [
+            (term(corner, 0), square_x.at[which, 1], along_x),
+            (term(corner, 1), square_y.at[which, 1], along_y),
+            (term(along_x, 0), square_x.at[which, 0], along_x),
+            (term(along_y, 1), square_y.at[which, 0], along_y),
+        ]
+        return [
+            start(source, target, square_send.at[base + i], square_recv.at[base + i], {"tensor": device})
+            for i, (source, target, device) in enumerate(plan)
+        ]
+
+    def rows_at(terms, owner, part):
+        return terms[pl.ds(pl.multiple_of(owner * rows + part * half, half), half), :].astype(wide)
+
+    def square_next(terms, base, which, copies):
+        copies[0].wait_recv()
+        staged[which, 0] = (rows_at(terms, along_y, 0) + square_x[which, 1].astype(wide)).astype(low)
+        on_y = start(staged.at[which, 0], square_last.at[which, 0], square_send.at[base + 4], square_recv.at[base + 4], square[1])
+        copies[1].wait_recv()
+        staged[which, 1] = (rows_at(terms, along_x, 1) + square_y[which, 1].astype(wide)).astype(low)
+        on_x = start(staged.at[which, 1], square_last.at[which, 1], square_send.at[base + 5], square_recv.at[base + 5], square[0])
+        return copies + [on_y, on_x]
+
+    def square_sum(terms, which, part):
+        near = square_x if part == 0 else square_y
+        return rows_at(terms, place, part) + near[which, 0].astype(wide) + square_last[which, part].astype(wide)
+
+    first_copies = square_first(first_ref, 0, 0)
+
+    def line(slot, step, part):
+        device = {"dp": turned(step, core)}
+        return [
+            pltpu.make_async_remote_copy(
+                src_ref=source.at[slot], dst_ref=target.at[part],
+                send_sem=line_send.at[i, part], recv_sem=line_recv.at[i, part], device_id=device, device_id_type=MESH,
+            )
+            for i, (source, target) in enumerate(((core_qkv, near_qkv), (core_proj, near_proj)))
+        ]
+
+    def go(slot, step, part):
+        for copy in line(slot, step, part):
+            copy.start()
+
+    def came(part):
+        for copy in line(part, 1, part):
+            copy.wait_recv()
+
+    def sent(slot, step, part):
+        for copy in line(slot, step, part):
+            copy.wait_send()
+
+    for slot in (3, 1, 2):
+        for copy in exchange[slot]:
+            copy.wait_recv()
+        owner = turned(slot, core)
+        for index in range(3):
+            core_qkv[slot, index] = (
+                core_qkv[slot, index].astype(wide) + qkv_part(owner)[index].astype(wide)
+            ).astype(low)
+        core_proj[slot] = (core_proj[slot].astype(wide) + proj_part(owner)[...].astype(wide)).astype(low)
+        if slot == 3:
+
+            @pl.when(chip == 0)
+            def _():
+                go(3, 1, 0)
+
+            @pl.when((chip == 1) | (chip == 2))
+            def _():
+                go(3, 3, 3)
+
+        elif slot == 1:
+
+            @pl.when(chip == 3)
+            def _():
+                go(1, 3, 0)
+
+            @pl.when((chip == 1) | (chip == 2))
+            def _():
+                go(1, 1, 1)
+
+        else:
+
+            @pl.when((chip == 0) | (chip == 3))
+            def _():
+                go(2, 2, 2)
+
+    first_copies = square_next(first_ref, 0, 0, first_copies)
+    block_copies = square_first(block_ref, 6, 1)
+    for copy in first_copies[2:]:
         copy.wait_recv()
-    mine[:, :split] = (corners[0] + corners[1]) + (corners[2] + corners[3])
-    mine[:, split:] = values_ref[:, split:]
-    copies.append(start(mine, came, 3))
-    copies[3].wait_recv()
-    slots_ref[chip] = mine[...] + came[...]
-    last = [start(slots_ref.at[chip], slots_ref.at[chip], index) for index in (4, 5, 6)]
-    for copy in last:
+    gain = gain_ref[...]
+    vector_gain = jnp.zeros_like(gain)
+    vector_shift = jnp.zeros_like(gain)
+    for part in range(2):
+        here = slice(part * half, (part + 1) * half)
+        grad = square_sum(first_ref, 0, part)
+        normed = normed_ref[here, :]
+        vector_gain += jnp.sum(grad * normed, 0, keepdims=True)
+        vector_shift += jnp.sum(grad, 0, keepdims=True)
+        scaled = grad * gain
+        inner = (
+            scaled
+            - jnp.mean(scaled, -1, keepdims=True)
+            - normed * jnp.mean(scaled * normed, -1, keepdims=True)
+        )
+        input_out[here, :] = grad_ref[here, :] + recip_ref[here, :] * inner
+    corners[place, 0:1, :] = vector_gain
+    corners[place, 1:2, :] = second_ref[0:1, :]
+    corners[place, 2:3, :] = vector_shift
+    corners[place, 3:4, :] = second_ref[1:2, :]
+    vector_copies = [
+        start(corners.at[place], corners.at[place], vector_send.at[i], vector_recv.at[i], square[i]) for i in range(3)
+    ]
+    bias_mine[...] = bias_ref[...]
+    bias_copies = [start(bias_mine, bias_came, bias_send.at[0], bias_recv.at[0], {"dp": sibling})]
+
+    def onward(slot, part):
+        for i, (mine, came_) in enumerate(((core_qkv, near_qkv), (core_proj, near_proj))):
+            mine[2] = (mine[2].astype(wide) + came_[0].astype(wide)).astype(low)
+
+    @pl.when((chip == 1) | (chip == 2))
+    def _():
+        came(0)
+        onward(2, 0)
+        go(2, 2, 2)
+
+    @pl.when(chip == 0)
+    def _():
+        sent(3, 1, 0)
+        go(1, 1, 1)
+
+    @pl.when(chip == 3)
+    def _():
+        sent(1, 3, 0)
+        go(3, 3, 3)
+
+    for copy in vector_copies:
         copy.wait_recv()
-    out_ref[...] = (slots_ref[0] + slots_ref[1]) + (slots_ref[2] + slots_ref[3])
-    for copy in copies + last:
+    vector_mine[...] = (corners[0] + corners[1]) + (corners[2] + corners[3])
+    vector_copies.append(start(vector_mine, vector_came, vector_send.at[3], vector_recv.at[3], {"dp": sibling}))
+    block_copies = square_next(block_ref, 6, 1, block_copies)
+    vector_copies[3].wait_recv()
+    bias_copies[0].wait_recv()
+    vector_slots[chip] = vector_mine[...] + vector_came[...]
+    bias_slots[chip] = bias_mine[...] + bias_came[...]
+    vector_copies += [
+        start(vector_slots.at[chip], vector_slots.at[chip], vector_send.at[4 + i], vector_recv.at[4 + i], chips[i])
+        for i in range(3)
+    ]
+    bias_copies += [
+        start(bias_slots.at[chip], bias_slots.at[chip], bias_send.at[1 + i], bias_recv.at[1 + i], chips[i])
+        for i in range(3)
+    ]
+    for copy in exchange[0]:
+        copy.wait_recv()
+    for copy in block_copies[2:]:
+        copy.wait_recv()
+    for part in range(2):
+        here = slice(part * half, (part + 1) * half)
+        block_out[here, :] = (resid_ref[here, :] + square_sum(block_ref, 1, part)).astype(low)
+    for copy in vector_copies[4:] + bias_copies[1:]:
+        copy.wait_recv()
+    vector_out[...] = (vector_slots[0] + vector_slots[1]) + (vector_slots[2] + vector_slots[3])
+    bias_out[...] = (bias_slots[0] + bias_slots[1]) + (bias_slots[2] + bias_slots[3])
+
+    came(2)
+
+    @pl.when(chip > 0)
+    def _():
+        came(1)
+
+    @pl.when(chip < 3)
+    def _():
+        came(3)
+
+    below, above = (chip > 0), (chip < 3)
+    owner = turned(0, core)
+
+    def last(own, other, came_1, came_2, came_3):
+        total = own.astype(wide) + other.astype(wide) + came_2.astype(wide)
+        total = total + jnp.where(below, came_1.astype(wide), 0.0)
+        return total + jnp.where(above, came_3.astype(wide), 0.0)
+
+    for index in range(3):
+        qkv_out[index] = last(
+            qkv_part(owner)[index], core_qkv[0, index], near_qkv[1, index], near_qkv[2, index], near_qkv[3, index]
+        )
+    proj_out[...] = last(proj_part(owner)[...], core_proj[0], near_proj[1], near_proj[2], near_proj[3])
+
+    for copy in first_copies + block_copies + vector_copies + bias_copies:
         copy.wait_send()
-
-
-def slice_total(values, split):
+    for slot in range(4):
+        for copy in exchange[slot]:
+            copy.wait_send()
+    sent(2, 2, 2)
+
+    @pl.when(chip < 3)
+    def _():
+        sent(1, 1, 1)
+
+    @pl.when(chip > 0)
+    def _():
+        sent(3, 3, 3)
+
+
+def tail_reduce(first, block, qkv, proj, normed, recip, gain, grad, resid, second, bias):
     dma = pltpu.SemaphoreType.DMA
-    shape = values.shape
+    low, wide = jnp.bfloat16, jnp.float32
+    shape, vmem = jax.ShapeDtypeStruct, pltpu.VMEM
+    rows, model = resid.shape
+    parts, depth, columns = qkv.shape[0], qkv.shape[1] // 8, qkv.shape[2]
+    width = proj.shape[1] // 8
+    pair = vmem((2, 2, rows // 2, model), low)
     return pl.pallas_call(
-        functools.partial(total_kernel, split),
-        out_shape=jax.ShapeDtypeStruct(shape, values.dtype),
-        in_specs=[pl.BlockSpec(memory_space=pltpu.VMEM)],
-        out_specs=pl.BlockSpec(memory_space=pltpu.VMEM),
+        tail_kernel,
+        out_shape=(
+            shape((rows, model), wide),
+            shape((rows, model), low),
+            shape((parts, depth, columns), wide),
+            shape((proj.shape[0], width), wide),
+            shape((4, model), wide),
+            shape(bias.shape, wide),
+        ),
+        in_specs=[pl.BlockSpec(memory_space=pltpu.VMEM)] * 11,
+        out_specs=(pl.BlockSpec(memory_space=pltpu.VMEM),) * 6,
         scratch_shapes=[
-            pltpu.VMEM((4, 8, split), values.dtype),
-            pltpu.VMEM(shape, values.dtype),
-            pltpu.VMEM(shape, values.dtype),
-            pltpu.VMEM((4, *shape), values.dtype),
-            dma((7,)),
-            dma((7,)),
+            pair, pair, pair, pair,
+            vmem((4, parts, depth, columns), low),
+            vmem((4, proj.shape[0], width), low),
+            vmem((4, parts, depth, columns), low),
+            vmem((4, proj.shape[0], width), low),
+            vmem((4, 4, model), wide),
+            vmem((4, model), wide),
+            vmem((4, model), wide),
+            vmem((4, 4, model), wide),
+            vmem(bias.shape, wide),
+            vmem(bias.shape, wide),
+            vmem((4, *bias.shape), wide),
+            dma((12,)), dma((12,)), dma((2, 4)), dma((2, 4)), dma((2, 4)), dma((2, 4)),
+            dma((7,)), dma((7,)), dma((4,)), dma((4,)),
         ],
-        compiler_params=pltpu.CompilerParams(collective_id=3, has_side_effects=True),
-        cost_estimate=pl.CostEstimate(flops=0, bytes_accessed=30_000_000, transcendentals=0),
-        name="slice_total",
-    )(values)
+        compiler_params=pltpu.CompilerParams(
+            collective_id=3, has_side_effects=True, vmem_limit_bytes=60 * 1024 * 1024
+        ),
+        cost_estimate=pl.CostEstimate(flops=0, bytes_accessed=200_000_000, transcendentals=0),
+        name="tail_reduce",
+    )(first, block, qkv, proj, normed, recip, gain, grad, resid, second, bias)
 
 
 def after(late, early):
@@ -636,8 +877,17 @@
             gather_dp(w_output, 1),
         )
 
-    def totals(self, vectors, sums):
-        return lax.psum(vectors, ("dp", "tensor")), lax.psum(sums, "dp")
+    def finish(self, first, block, qkv, proj, normed, recip, gain, grad, resid, second, bias):
+        first = self.reduce_rows(first, None, 0)
+        vectors = jnp.stack([jnp.sum(first * normed, 0), second[0], jnp.sum(first, 0), second[1]])
+        return (
+            grad + norm_back(first, normed, recip, gain),
+            (resid + self.reduce_rows(block, None, 0)).astype(jnp.bfloat16),
+            scatter_dp(qkv, 1),
+            scatter_dp(proj, 1),
+            lax.psum(vectors, ("dp", "tensor")),
+            lax.psum(bias, "dp"),
+        )
 
 
 class Line(Plain):
@@ -656,16 +906,14 @@
         came = came.reshape(8, -1)[:, : parts * heads * few].reshape(8, parts, heads, few)
         return a, dy, came.transpose(1, 2, 0, 3).reshape(parts, heads, -1), w_qkv, w_output
 
-    def totals(self, vectors, sums):
-        split = vectors.size // 8
-        flat = sums.reshape(-1)
+    def finish(self, first, block, qkv, proj, normed, recip, gain, grad, resid, second, bias):
+        flat = bias.reshape(-1)
         width = -(-flat.shape[0] // 1024) * 1024
         flat = jnp.pad(flat, (0, width - flat.shape[0])).reshape(8, -1)
-        total = slice_total(jnp.concatenate([vectors.reshape(8, split), flat], 1), split)
-        return (
-            total[:, :split].reshape(vectors.shape),
-            total[:, split:].reshape(-1)[: sums.size].reshape(sums.shape),
-        )
+        *found, total = tail_reduce(
+            first, block, qkv, proj, normed, recip, gain.reshape(1, -1), grad, resid, second, flat
+        )
+        return (*found, total.reshape(-1)[: bias.size].reshape(bias.shape))
 
 
 def row_major(values):
@@ -718,13 +966,13 @@
         first_out.astype(low), cotangent, biases.astype(low), qkv_weight.astype(low), out_weight.astype(low)
     )
     bias_all = bias_all.reshape(3, local_width).astype(jnp.float32)
-    w_gate_up = gather_dp(after(gate_up, w_output), 1)
+    w_gate_up = gather_dp(after(gate_up.astype(low), w_output), 1)
     lin = jnp.einsum("rd,kdc->krc", a_all, w_qkv, preferred_element_type=jnp.float32)
     qkv, heads, logs = attention_forward(lin, bias_all, head_size)
     resid = xin + routes.reduce_rows(mxu(heads, w_output, NN).astype(low), logs, 4)
     second_out, second_normed, second_recip = layer_norm(resid, gains[1], shifts[1])
     m_all = routes.gather_rows(second_out.astype(low))
-    w_down = gather_dp(after(down_weight, (w_gate_up, m_all)), 1)
+    w_down = gather_dp(after(down_weight.astype(low), (w_gate_up, m_all)), 1)
     gate_vals = jnp.einsum("rd,kdc->krc", m_all, w_gate_up, preferred_element_type=jnp.float32)
     gate_lin, upward = gate_vals[0], gate_vals[1]
     sigmoid_gate = jax.nn.sigmoid(gate_lin)
@@ -758,25 +1006,28 @@
     lin_grads, bias_terms = attention_backward(qkv, heads_grad, logs, head_size)
     qkv_terms = jnp.einsum("rd,krc->kdc", a_all, lin_grads, preferred_element_type=jnp.float32)
     qkv_terms = row_major(qkv_terms.astype(low))
-    out_grad = scatter_dp(after(out_terms, (gate_grad, lin_grads)), 1)
-    down_sum = routes.reduce_rows(block_terms, bias_terms, 6)
-    qkv_grad = scatter_dp(after(qkv_terms, (out_grad, down_sum)), 1)
     first_terms = jnp.einsum(
         "krc,kdc->rd", lin_grads, w_qkv, preferred_element_type=jnp.float32
     ).astype(low)
-    first_grad = routes.reduce_rows(first_terms, bias_terms, 7)
-    input_grad = resid_grad + norm_back(first_grad, first_normed, first_recip, gains[0])
-    vectors = jnp.stack(
-        [jnp.sum(first_grad * first_normed, 0), gain_second, jnp.sum(first_grad, 0), shift_second]
+    input_grad, block_out, qkv_grad, out_grad, vectors, bias_sum = routes.finish(
+        first_terms,
+        block_terms,
+        qkv_terms,
+        out_terms,
+        first_normed,
+        first_recip,
+        gains[0],
+        resid_grad,
+        resid,
+        jnp.stack([gain_second, shift_second]),
+        bias_terms,
     )
-    vectors, bias_sum = routes.totals(vectors, bias_terms)
     gains_grad, shifts_grad = vectors[:2], vectors[2:]
-    out_grad, down_grad, gate_grad = after((out_grad, down_grad, gate_grad), first_grad)
+    down_grad, gate_grad = after((down_grad, gate_grad), vectors)
     per_dp = biases.shape[2]
     biases_grad = lax.dynamic_slice_in_dim(
         bias_sum.reshape(3, local_heads, head_size), lax.axis_index("dp") * per_dp, per_dp, 2
     )
-    block_out = (resid + down_sum).astype(low)
     gain_new = adamw(gains, gains_grad, momentum_gains, variance_gains, 0.0, vector_rate)
     shift_new = adamw(shifts, shifts_grad, momentum_shifts, variance_shifts, 0.0, vector_rate)
     qkv_new = adamw(qkv_weight, qkv_grad, momentum_qkv, variance_qkv, decay_rate, learn_rate)

time: 627 us -> 608 us (0.970)
  other arithmetic: 53.5 us -> 42.5 us
  Pallas kernels: 351 us -> 358 us
    pallas_call x1, Pallas kernels: 18.5 us -> 94.7 us  [tail_reduce(): pl.pallas_call(tail_kernel, out_shape=(shape((rows, model), wide), shape(...]
    pallas_call x4 -> x2, Pallas kernels: 142 us -> 73.2 us  [square_reduce(): pl.pallas_call(reduce_kernel, out_shape=jax.ShapeDtypeStruct((rows, width...]
    convert_element_type x4 -> x2, other arithmetic: 9.04 us -> 2.18 us  [the longest x1 1.25 us: local(): w_gate_up = gather_dp(after(gate_up.astype(low), w_output), 1)]
    sub x7 -> x6, other arithmetic: 17.6 us -> 19.8 us  [adamw(): return (weight - rate * change, moment_new, second_new)]
    unnamed x111 -> x113, local copies, waits for them, and re-layouts: 17.3 us -> 17.2 us
  transfers between devices with their start and end apart: 6 -> 4, of which waited for: 3 -> 2; matrix products, arithmetic and copies ran while one was open for 28% -> 25% of each run, Pallas kernels for 44% -> 47%
where the time goes in v2:
time: 608 us; the launch traced here: 598 us
  Pallas kernels  358 us (59%)
  matrix products  127 us (21%)
  other arithmetic  42.5 us (7%)
  waiting for transfers between devices  33.4 us (5%)
  local copies, waits for them, and re-layouts  22 us (4%)
  between operations  14.8 us (2%)
    pallas_call x1, Pallas kernels, tail_reduce(): pl.pallas_call(tail_kernel, out_shape=(shape((rows, model), wide), shape(...  94.7 us
    pallas_call x1, Pallas kernels, start_gather(): pl.pallas_call(start_kernel, out_shape=(shape((4 * a.shape[0], a.shape[1]...  79.6 us
    pallas_call x2, Pallas kernels, square_reduce(): pl.pallas_call(reduce_kernel, out_shape=jax.ShapeDtypeStruct((rows, width...  73.2 us
    pallas_call x2, Pallas kernels, square_gather(): pl.pallas_call(gather_kernel, out_shape=jax.ShapeDtypeStruct((4 * rows, w...  72.3 us
    dot_general x6, matrix products, mxu(): lax.dot_general(left, right, dims, preferred_element_type=jnp.float32)  45.8 us
    all_gather x2, waiting for transfers between devices, gather_dp(): lax.all_gather(block.astype(jnp.bfloat16), 'dp', axis=axis, tiled=True)  27.9 us
    pallas_call x1, Pallas kernels, attention_backward(): pl.pallas_call(functools.partial(backward_kernel, head_size), grid=(rows...  23.8 us
    sub x6, other arithmetic, adamw(): return (weight - rate * change, moment_new, second_new)  19.8 us
  transfers between devices with their start and end apart: 4, of which 2 were waited for; matrix products, arithmetic and copies ran while one was open for 25% of the time, Pallas kernels for 47%

profile of v2, /device:TPU:0, one launch (start us, length us, event | category | flops | bytes accessed | tf_op | source)
XLA Modules:
  0.0 598.5 jit_solution(14262594875637912793)
XLA Ops:
  18.7 79.6 %start_gather.1 = (bf16[1024,2048]{1,0:T(8,128)(2,1)}, bf16[1024,2048]{1,0:T(8,128)(2,1)}, f32[8,8,128]{2,1,0:T(8,128)}, bf16[3,2048,512]{2,1,0:T(8,128)(2,1)}, bf16[512,2048]{1,0:T(8,128)(2,1)}) custom-call(bf16[256,2048]{1,0:T(8,128)(2,1)} %get-tuple-element.109.a_ref, bf16[256,2048]{1,0:T(8,128)(2,1)} %dy_ref.1, f32[8,128]{1,0:T(8,128)} %bitcast_convert_fusion.2.bias_ref, ...), custom_call_target="tpu_custom_call" | custom-call | bytes 200000000 | tf_op jit(solution)/shard_map/start_gather/pallas_call | solution.py:536
  99.4 11.9 %fusion.9.lin_ref = f32[3,1024,512]{2,1,0:T(8,128)} fusion(bf16[3,2048,512]{2,1,0:T(8,128)(2,1)} %get-tuple-element.52, bf16[1024,2048]{1,0:T(8,128)(2,1)} %get-tuple-element.53), kind=kOutput, calls=%fused_computation.31 | convolution fusion | flops 6442450944 | bytes 16777216 | tf_op jit(solution)/shard_map/rd,kdc->krc/dot_general | solution.py:970
  111.3 14.9 %attend_forward.1 = (bf16[3,1024,512]{2,1,0:T(8,128)(2,1)S(1)}, bf16[1024,512]{1,0:T(8,128)(2,1)S(1)}, f32[2,8,1024]{2,1,0:T(8,128)S(1)}) custom-call(f32[3,1024,512]{2,1,0:T(8,128)} %fusion.9.lin_ref, f32[3,512]{1,0:T(4,128)S(1)} %reshape_reshape.6.bias_ref, f32[3,1024,128]{2,1,0:T(8,128)S(1)} %copy-done.4), custom_call_target="tpu_custom_call" | custom-call | flops 4294967296 | bytes 13631488 | tf_op jit(solution)/shard_map/attend_forward/pallas_call | solution.py:129
  128.6 38.0 %square_reduce.2 = f32[256,2048]{1,0:T(8,128)S(1)} custom-call(bf16[1024,2048]{1,0:T(8,128)(2,1)S(1)} %convolution_convert_fusion.2.terms_ref, f32[2,8,1024]{2,1,0:T(8,128)S(1)} %get-tuple-element.58.ready_ref.lse_ref), custom_call_target="tpu_custom_call" | custom-call | bytes 125829120 | tf_op jit(solution)/shard_map/square_reduce/pallas_call | solution.py:357
  169.6 37.6 %square_gather.2 = bf16[1024,2048]{1,0:T(8,128)(2,1)} custom-call(bf16[256,2048]{1,0:T(8,128)(2,1)} %add_convert_fusion.block_ref), custom_call_target="tpu_custom_call" | custom-call | bytes 62914560 | tf_op jit(solution)/shard_map/square_gather/pallas_call | solution.py:289
  208.2 16.6 %convolution_bitcast_fusion = f32[2,1024,1408]{1,2,0:T(8,128)S(1)} fusion(bf16[2,2048,1408]{2,1,0:T(8,128)(2,1)} %all-gather.3.cloned.1.call-done, bf16[1024,2048]{1,0:T(8,128)(2,1)} %square_gather.2), kind=kOutput, calls=%fused_computation.4 | convolution fusion | flops 11811160064 | bytes 27262976 | tf_op jit(solution)/shard_map/rd,kdc->krc/dot_general | solution.py:976
  226.7 3.5 copy-done.16
  231.8 8.1 %convolution_convert_fusion = bf16[1408,2048]{1,0:T(8,128)(2,1)} fusion(bf16[1024,1408]{0,1:T(8,128)(2,1)S(1)} %multiply_convert_fusion.2, bf16[1024,2048]{1,0:T(8,128)(2,1)S(1)} %copy-done.49), kind=kOutput, calls=%fused_computation.3 | convolution fusion | flops 5908463616 | bytes 12845056 | tf_op jit(solution)/shard_map/dot_general | solution.py:84
  239.9 27.9 %all-gather.5.cloned.1.call-done = bf16[1408,2048]{1,0:T(8,128)(2,1)} async-done(((bf16[1408,256]{1,0:T(8,128)(2,1)}), bf16[1408,2048]{1,0:T(8,128)(2,1)}) %all-gather.5.cloned.1.call-update) | async-done | bytes 5767184 | tf_op jit(solution)/shard_map/all_gather | solution.py:924
  267.8 11.4 %convolution_convert_fusion.1.block_ref = bf16[1024,2048]{1,0:T(8,128)(2,1)} fusion(bf16[1024,1408]{0,1:T(8,128)(2,1)} %copy-done.25, bf16[1408,2048]{1,0:T(8,128)(2,1)} %all-gather.5.cloned.1.call-done), kind=kOutput, calls=%fused_computation.20 | convolution fusion | flops 5907677184 | bytes 12845056 | tf_op jit(solution)/shard_map/dot_general | solution.py:84
  279.2 12.6 %fusion.8 = (bf16[1,1024,1408]{1,2,0:T(8,128)(2,1)}, bf16[1,1024,1408]{1,2,0:T(8,128)(2,1)}) fusion(f32[2,1024,1408]{1,2,0:T(8,128)} %copy-done.16, bf16[1024,2048]{1,0:T(8,128)(2,1)S(1)} %copy-done.50, bf16[1408,2048]{1,0:T(8,128)(2,1)S(1)} %copy-done.47), kind=kOutput, calls=%fused_computation.30 | convolution fusion | flops 5924323328 | bytes 27262976 | tf_op jit(solution)/shard_map/dot_general | solution.py:84
  291.8 17.4 %convert_bitcast_fusion = bf16[2,2048,1408]{2,1,0:T(8,128)(2,1)} fusion(bf16[1024,2048]{1,0:T(8,128)(2,1)S(1)} %copy-done.23, bf16[1,1024,1408]{1,2,0:T(8,128)(2,1)} %get-tuple-element.107, bf16[1,1024,1408]{1,2,0:T(8,128)(2,1)} %get-tuple-element.106), kind=kOutput, calls=%fused_computation | convolution fusion | flops 11819810816 | bytes 21495808 | tf_op jit(solution)/shard_map/rd,krc->kdc/dot_general | solution.py:990
  309.1 18.6 %bitcast_convert_fusion.1.terms_ref = bf16[1024,2048]{1,0:T(8,128)(2,1)} fusion(bf16[2,2048,1408]{2,1,0:T(8,128)(2,1)} %all-gather.3.cloned.1.call-done, bf16[1,1024,1408]{1,2,0:T(8,128)(2,1)} %get-tuple-element.107, bf16[1,1024,1408]{1,2,0:T(8,128)(2,1)} %get-tuple-element.106), kind=kOutput, calls=%fused_computation.2 | convolution fusion | flops 11816140800 | bytes 21495808 | tf_op jit(solution)/shard_map/krc,kdc->rd/dot_general | solution.py:992
  327.7 5.4 reduce-scatter.3.cloned.1.call-done
  338.1 35.2 %square_reduce.3 = f32[256,2048]{1,0:T(8,128)S(1)} custom-call(bf16[1024,2048]{1,0:T(8,128)(2,1)S(1)} %copy-done.1, f32[1408,256]{1,0:T(8,128)S(1)} %convert_element_type.98.ready_ref), custom_call_target="tpu_custom_call" | custom-call | bytes 125829120 | tf_op jit(solution)/shard_map/square_reduce/pallas_call | solution.py:357
  377.3 34.7 %square_gather.3 = bf16[1024,2048]{1,0:T(8,128)(2,1)} custom-call(bf16[256,2048]{1,0:T(8,128)(2,1)} %get-tuple-element.102.block_ref), custom_call_target="tpu_custom_call" | custom-call | bytes 62914560 | tf_op jit(solution)/shard_map/square_gather/pallas_call | solution.py:289
  412.0 5.4 convolution_convert_fusion.4.grad_ref
  417.5 23.8 %attend_backward.1 = (bf16[3,1024,512]{2,1,0:T(8,128)(2,1)S(1)}, f32[1,3,512]{2,1,0:T(4,128)S(1)}) custom-call(bf16[3,1024,512]{2,1,0:T(8,128)(2,1)} %copy-done.8, bf16[1024,512]{1,0:T(8,128)(2,1)S(1)} %convolution_convert_fusion.4.grad_ref, f32[2,8,1024]{2,1,0:T(8,128)S(1)} %copy-done.3, f32[3,1024,128]{2,1,0:T(8,128)S(1)} %copy-done.5), custom_call_target="tpu_custom_call" | custom-call | flops 10737418240 | bytes 13631488 | tf_op jit(solution)/shard_map/attend_backward/pallas_call | solution.py:206
  444.9 6.0 %convolution_convert_fusion.3.proj_ref = bf16[512,2048]{1,0:T(8,128)(2,1)} fusion(bf16[1024,512]{1,0:T(8,128)(2,1)S(1)} %copy-done.7, bf16[1024,2048]{1,0:T(8,128)(2,1)} %square_gather.3), kind=kOutput, calls=%fused_computation.25 | convolution fusion | flops 2148532224 | bytes 7340032 | tf_op jit(solution)/shard_map/dot_general | solution.py:84
  450.9 8.7 %convert_bitcast_fusion.1.qkv_ref = bf16[3,2048,512]{2,1,0:T(8,128)(2,1)} fusion(bf16[3,1024,512]{2,1,0:T(8,128)(2,1)S(1)} %copy-done.10, bf16[1024,2048]{1,0:T(8,128)(2,1)S(1)} %copy-done.48), kind=kOutput, calls=%fused_computation.5 | convolution fusion | flops 6445596672 | bytes 13631488 | tf_op jit(solution)/shard_map/rd,krc->kdc/dot_general | solution.py:1007
  459.6 8.3 %bitcast_convert_fusion.first_ref = bf16[1024,2048]{1,0:T(8,128)(2,1)} fusion(bf16[3,1024,512]{2,1,0:T(8,128)(2,1)S(1)} %copy-done.10, bf16[3,2048,512]{2,1,0:T(8,128)(2,1)S(1)} %bitcast.100), kind=kOutput, calls=%fused_computation.1 | convolution fusion | flops 6444548096 | bytes 13631488 | tf_op jit(solution)/shard_map/krc,kdc->rd/dot_general | solution.py:1009
  467.9 94.7 %tail_reduce.1 = (f32[256,2048]{1,0:T(8,128)}, bf16[256,2048]{1,0:T(8,128)(2,1)}, f32[3,256,512]{2,1,0:T(8,128)}, f32[512,256]{1,0:T(8,128)}, f32[4,2048]{1,0:T(4,128)}, /*index=5*/f32[8,256]{1,0:T(8,128)}) custom-call(bf16[1024,2048]{1,0:T(8,128)(2,1)} %bitcast_convert_fusion.first_ref, bf16[1024,2048]{1,0:T(8,128)(2,1)} %convolution_convert_fusion.1.block_ref, ...), custom_call_target="tpu_custom_call" | custom-call | bytes 200000000 | tf_op jit(solution)/shard_map/tail_reduce/pallas_call | solution.py:824
  569.3 4.9 multiply_subtract_fusion.1
  576.5 7.0 %multiply_subtract_fusion = (f32[2,256,1408]{2,1,0:T(8,128)}, f32[2,256,1408]{2,1,0:T(8,128)}, f32[2,256,1408]{2,1,0:T(8,128)}) fusion(f32[2,256,1408]{2,1,0:T(8,128)S(1)} %copy-done.14, f32[2,256,1408]{2,1,0:T(8,128)S(1)} %convert_element_type.108, f32[2,256,1408]{2,1,0:T(8,128)} %param.39, f32[2,256,1408]{2,1,0:T(8,128)} %param.46), kind=kLoop, calls=%fused_computation.28 | loop fusion | flops 10813440 | bytes 20185088 | tf_op jit(solution)/shard_map/sub | solution.py:47
  (163 shorter events, 51.7 us)
Async XLA Ops:
  7.2 7.4 %copy-start.26 = (f32[512,256]{1,0:T(8,128)S(1)}, f32[512,256]{1,0:T(8,128)}, u32[]{:S(2)}) copy-start(f32[512,256]{1,0:T(8,128)} %param.31) | copy-start | bytes 1572868
  7.2 200.9 %all-gather.3.cloned.1.call-start = ((), (), s32[]{:S(2)}) async-start(), calls=%async_computation.2 | async-start | bytes 12976128 | tf_op jit(solution)/shard_map/all_gather | solution.py:924
  98.4 169.4 %all-gather.5.cloned.1.call-start = ((), (), s32[]{:S(2)}) async-start(), calls=%async_computation.3 | async-start | bytes 6488064 | tf_op jit(solution)/shard_map/all_gather | solution.py:924
  99.4 11.9 %copy-start.4 = (f32[3,1024,128]{2,1,0:T(8,128)S(1)}, f32[3,1024,128]{2,1,0:T(8,128)}, u32[]{:S(2)}) copy-start(f32[3,1024,128]{2,1,0:T(8,128)} %constant.44.clone.table_ref) | copy-start | bytes 4718596
  111.3 15.0 %copy-start.51 = (bf16[512,2048]{1,0:T(8,128)(2,1)S(1)}, bf16[512,2048]{1,0:T(8,128)(2,1)}, u32[]{:S(2)}) copy-start(bf16[512,2048]{1,0:T(8,128)(2,1)} %get-tuple-element.57) | copy-start | bytes 6291460
  166.9 207.9 %copy-start.11 = (f32[256,2048]{1,0:T(8,128)}, f32[256,2048]{1,0:T(8,128)S(1)}, u32[]{:S(2)}) copy-start(f32[256,2048]{1,0:T(8,128)S(1)} %get-tuple-element.105.resid_ref) | copy-start | bytes 6291460
  169.6 37.7 %copy-start.21 = (f32[1408,256]{1,0:T(8,128)S(1)}, f32[1408,256]{1,0:T(8,128)}, u32[]{:S(2)}) copy-start(f32[1408,256]{1,0:T(8,128)} %param.33) | copy-start | bytes 4325380
  208.2 125.0 %reduce-scatter.3.cloned.1.call-start = ((), (), s32[]{:S(2)}) async-start(), calls=%async_computation.4 | async-start | bytes 6488064 | tf_op jit(solution)/shard_map/reduce_scatter | solution.py:928
  224.8 7.0 %copy-start.49 = (bf16[1024,2048]{1,0:T(8,128)(2,1)S(1)}, bf16[1024,2048]{1,0:T(8,128)(2,1)}, u32[]{:S(2)}) copy-start(bf16[1024,2048]{1,0:T(8,128)(2,1)} %get-tuple-element.59) | copy-start | bytes 12582916
  239.8 334.4 %reduce-scatter.5.cloned.1.call-start = ((), (), s32[]{:S(2)}) async-start(), calls=%async_computation.5 | async-start | bytes 12976128 | tf_op jit(solution)/shard_map/reduce_scatter | solution.py:928
  267.8 11.4 %copy-start.47 = (bf16[1408,2048]{1,0:T(8,128)(2,1)S(1)}, bf16[1408,2048]{1,0:T(8,128)(2,1)}, u32[]{:S(2)}) copy-start(bf16[1408,2048]{1,0:T(8,128)(2,1)} %all-gather.5.cloned.1.call-done) | copy-start | bytes 17301508
  267.8 11.4 %copy-start.50 = (bf16[1024,2048]{1,0:T(8,128)(2,1)S(1)}, bf16[1024,2048]{1,0:T(8,128)(2,1)}, u32[]{:S(2)}) copy-start(bf16[1024,2048]{1,0:T(8,128)(2,1)} %get-tuple-element.59) | copy-start | bytes 12582916
  279.2 12.6 %copy-start.23 = (bf16[1024,2048]{1,0:T(8,128)(2,1)S(1)}, bf16[1024,2048]{1,0:T(8,128)(2,1)}, u32[]{:S(2)}) copy-start(bf16[1024,2048]{1,0:T(8,128)(2,1)} %square_gather.2) | copy-start | bytes 12582916
  334.4 249.1 %copy-start = (f32[1408,256]{1,0:T(8,128)}, f32[1408,256]{1,0:T(8,128)S(1)}, u32[]{:S(2)}) copy-start(f32[1408,256]{1,0:T(8,128)S(1)} %convert_element_type.98.ready_ref) | copy-start | bytes 4325380
  338.1 35.2 %copy-start.38 = (f32[256]{0:T(256)S(1)}, f32[256]{0:T(256)}, u32[]{:S(2)}) copy-start(f32[256]{0:T(256)} %copy-done.37) | copy-start | bytes 3076
  338.1 35.2 %copy-start.40 = (f32[256]{0:T(256)S(1)}, f32[256]{0:T(256)}, u32[]{:S(2)}) copy-start(f32[256]{0:T(256)} %copy-done.39) | copy-start | bytes 3076
  417.4 27.4 %copy-start.7 = (bf16[1024,512]{1,0:T(8,128)(2,1)S(1)}, bf16[1024,512]{1,0:T(8,128)(2,1)}, u32[]{:S(2)}) copy-start(bf16[1024,512]{1,0:T(8,128)(2,1)} %copy-done.6) | copy-start | bytes 3145732
  444.8 14.7 %slice-start = ((s8[6291456]{0:T(1024)(128)(4,1)}), s8[4194304]{0:T(1024)(128)(4,1)S(1)}, s32[]{:S(2)}) async-start(s8[6291456]{0:T(1024)(128)(4,1)} %bitcast.99), calls=%async_computation.6 | async-start | bytes 8388608
  450.9 8.7 %slice-start.1 = ((s8[6291456]{0:T(1024)(128)(4,1)}), s8[2097152]{0:T(1024)(128)(4,1)S(1)}, s32[]{:S(2)}) async-start(s8[6291456]{0:T(1024)(128)(4,1)} %bitcast.99), calls=%async_computation.7 | async-start | bytes 4194304
  467.9 97.8 %copy-start.27 = (f32[512,256]{1,0:T(8,128)S(1)}, f32[512,256]{1,0:T(8,128)}, u32[]{:S(2)}) copy-start(f32[512,256]{1,0:T(8,128)} %param.31) | copy-start | bytes 1572868
  576.5 7.0 %copy-start.15 = (f32[2,256,1408]{2,1,0:T(8,128)}, f32[2,256,1408]{2,1,0:T(8,128)S(1)}, u32[]{:S(2)}) copy-start(f32[2,256,1408]{2,1,0:T(8,128)S(1)} %convert_element_type.108) | copy-start | bytes 8650756
  576.5 7.0 %copy-start.22 = (f32[1408,256]{1,0:T(8,128)S(1)}, f32[1408,256]{1,0:T(8,128)}, u32[]{:S(2)}) copy-start(f32[1408,256]{1,0:T(8,128)} %param.33) | copy-start | bytes 4325380
  576.5 7.0 %copy-start.30 = (f32[1408,256]{1,0:T(8,128)S(1)}, f32[1408,256]{1,0:T(8,128)}, u32[]{:S(2)}) copy-start(f32[1408,256]{1,0:T(8,128)} %param.40) | copy-start | bytes 4325380
  576.5 7.0 %copy-start.31 = (f32[1408,256]{1,0:T(8,128)S(1)}, f32[1408,256]{1,0:T(8,128)}, u32[]{:S(2)}) copy-start(f32[1408,256]{1,0:T(8,128)} %param.47) | copy-start | bytes 4325380
  (34 other events, 122.7 us)
Sparse Core Ops, SparseCore 0:
  98.5 107.6 all-gather.2
  208.3 59.4 all-gather.4
  270.1 63.0 reduce-scatter.2
  335.3 117.6 reduce-scatter.4

commit v3 on v1

--- a/solution.py
+++ b/solution.py
@@ -376,7 +376,9 @@
 
 
 def start_kernel(
-    a_ref, dy_ref, bias_ref, wq_ref, wo_ref, a_all, dy_all, bias_all, wq_all, wo_all,
+    x_ref, gain_ref, shift_ref, dy_ref, bias_ref, wq_wide, wo_wide, gate_wide, down_wide,
+    a_all, dy_all, bias_all, wq_all, wo_all, normed_out, recip_out, gate_out, down_out,
+    a_ref, wq_ref, wo_ref, gate_here, down_here,
     square_send, square_recv, bias_send, bias_recv, line_send, line_recv, core_send, core_recv, local_sem,
 ):
     place, along_x, along_y = partners()
@@ -384,6 +386,7 @@
     chip, core = me // 2, me % 2
     sibling = me + 1 - 2 * core
     rows = a_ref.shape[0]
+    low = jnp.bfloat16
     half = rows // 2
     depth = wq_ref.shape[1]
 
@@ -407,12 +410,14 @@
     def turned(step):
         return 2 * ((chip + step) % 4) + core
 
-    locals_ = [
-        pltpu.make_async_copy(a_ref, a_all.at[pl.ds(pl.multiple_of(place * rows, rows), rows)], local_sem.at[0]),
-        pltpu.make_async_copy(dy_ref, dy_all.at[pl.ds(pl.multiple_of(place * rows, rows), rows)], local_sem.at[1]),
-    ] + [pltpu.make_async_copy(own(part), piece(part, me), local_sem.at[2 + part]) for part in range(4)]
-    for copy in locals_:
+    here = [
+        pltpu.make_async_copy(gate_wide, gate_here, local_sem.at[6]),
+        pltpu.make_async_copy(down_wide, down_here, local_sem.at[7]),
+    ]
+    for copy in here:
         copy.start()
+    wq_ref[...] = wq_wide[...].astype(low)
+    wo_ref[...] = wo_wide[...].astype(low)
     bias_all[me] = bias_ref[...]
 
     barrier = pltpu.get_barrier_semaphore()
@@ -440,7 +445,6 @@
         on_x = start(rows_of(whole, along_y, 1), rows_of(whole, along_y, 1), square_send.at[base + 5], square_recv.at[base + 5], {"tensor": along_x})
         return copies + [on_y, on_x]
 
-    a_copies = square_first(a_ref, a_all, 0)
     bias_copies = [
         start(bias_all.at[me], bias_all.at[me], bias_send.at[step], bias_recv.at[step], {"dp": (me + step) % 8})
         for step in range(1, 8)
@@ -490,6 +494,22 @@
             line(part, 3, 1).start()
 
     siblings = [to_sibling(part, 0) for part in range(4)]
+    values = x_ref[...].astype(jnp.float32)
+    centred = values - jnp.mean(values, -1, keepdims=True)
+    recip = lax.rsqrt(jnp.mean(centred * centred, -1, keepdims=True) + norm_eps)
+    recip_out[...] = recip
+    normed_out[...] = centred * recip
+    a_ref[...] = (normed_out[...] * gain_ref[...] + shift_ref[...]).astype(low)
+    a_copies = square_first(a_ref, a_all, 0)
+    locals_ = [
+        pltpu.make_async_copy(a_ref, a_all.at[pl.ds(pl.multiple_of(place * rows, rows), rows)], local_sem.at[0]),
+        pltpu.make_async_copy(dy_ref, dy_all.at[pl.ds(pl.multiple_of(place * rows, rows), rows)], local_sem.at[1]),
+    ] + [pltpu.make_async_copy(own(part), piece(part, me), local_sem.at[2 + part]) for part in range(4)]
+    for copy in locals_:
+        copy.start()
+    for copy, source, target in zip(here, (gate_here, down_here), (gate_out, down_out)):
+        copy.wait()
+        target[...] = source[...].astype(low)
     a_copies = square_next(a_all, 0, a_copies)
     dy_copies = square_first(dy_ref, dy_all, 6)
     for part in range(4):
@@ -528,92 +548,175 @@
         copy.wait()
 
 
-def start_gather(a, dy, bias, wq, wo):
+def start_gather(x, gain, shift, dy, bias, wq, wo, gate, down):
     dma = pltpu.SemaphoreType.DMA
+    low, wide = jnp.bfloat16, jnp.float32
     anywhere = pl.BlockSpec(memory_space=pl.ANY)
     local_ = pl.BlockSpec(memory_space=pltpu.VMEM)
     shape = jax.ShapeDtypeStruct
+    rows, model = x.shape
     return pl.pallas_call(
         start_kernel,
         out_shape=(
-            shape((4 * a.shape[0], a.shape[1]), a.dtype),
-            shape((4 * dy.shape[0], dy.shape[1]), dy.dtype),
+            shape((4 * rows, model), low),
+            shape((4 * rows, model), low),
             shape((8, *bias.shape), bias.dtype),
-            shape((wq.shape[0], 8 * wq.shape[1], wq.shape[2]), wq.dtype),
-            shape((wo.shape[0], 8 * wo.shape[1]), wo.dtype),
-        ),
-        in_specs=[local_] * 5,
-        out_specs=(anywhere, anywhere, local_, anywhere, anywhere),
+            shape((wq.shape[0], 8 * wq.shape[1], wq.shape[2]), low),
+            shape((wo.shape[0], 8 * wo.shape[1]), low),
+            shape((rows, model), wide),
+            shape((rows, 1), wide),
+            shape(gate.shape, low),
+            shape(down.shape, low),
+        ),
+        in_specs=[local_] * 7 + [anywhere] * 2,
+        out_specs=(anywhere, anywhere, local_, anywhere, anywhere, local_, local_, local_, local_),
         scratch_shapes=[
+            pltpu.VMEM((rows, model), low),
+            pltpu.VMEM(wq.shape, low),
+            pltpu.VMEM(wo.shape, low),
+            pltpu.VMEM(gate.shape, wide),
+            pltpu.VMEM(down.shape, wide),
             dma((12,)), dma((12,)), dma((8,)), dma((8,)),
-            dma((4, 4)), dma((4, 4)), dma((4, 4)), dma((4, 4)), dma((6,)),
+            dma((4, 4)), dma((4, 4)), dma((4, 4)), dma((4, 4)), dma((8,)),
         ],
-        compiler_params=pltpu.CompilerParams(collective_id=2, has_side_effects=True),
+        compiler_params=pltpu.CompilerParams(
+            collective_id=2, has_side_effects=True, vmem_limit_bytes=48 * 1024 * 1024
+        ),
         cost_estimate=pl.CostEstimate(flops=0, bytes_accessed=200_000_000, transcendentals=0),
         name="start_gather",
-    )(a, dy, bias, wq, wo)
-
-
-def total_kernel(split, values_ref, out_ref, corners, came, mine, slots_ref, send_sem, recv_sem):
+    )(x, gain, shift, dy, bias, wq, wo, gate, down)
+
+
+def last_kernel(
+    first_ref, normed_ref, recip_ref, gain_ref, grad_ref, second_ref, bias_ref, input_out, vector_out, bias_out,
+    square_x, square_y, staged, square_last,
+    corners, vector_mine, vector_came, vector_slots, bias_mine, bias_came, bias_slots,
+    square_send, square_recv, vector_send, vector_recv, bias_send, bias_recv,
+):
     place, along_x, along_y = partners()
+    corner = 3 - place
     me = lax.axis_index("dp")
     chip, sibling = me // 2, me + 1 - 2 * (me % 2)
-    others = [{"tensor": device} for device in (along_x, along_y, 3 - place)]
-    others += [{"dp": sibling}] + [{"dp": (me + 2 * step) % 8} for step in (1, 2, 3)]
-    barrier = pltpu.get_barrier_semaphore()
-    for other in others:
-        pl.semaphore_signal(barrier, inc=1, device_id=other, device_id_type=MESH)
-    pl.semaphore_wait(barrier, len(others))
-
-    def start(source, target, index):
+    rows = input_out.shape[0]
+    half = rows // 2
+    low, wide = jnp.bfloat16, jnp.float32
+
+    def start(source, target, send_sem, recv_sem, device):
         copy = pltpu.make_async_remote_copy(
-            src_ref=source,
-            dst_ref=target,
-            send_sem=send_sem.at[index],
-            recv_sem=recv_sem.at[index],
-            device_id=others[index],
-            device_id_type=MESH,
+            src_ref=source, dst_ref=target, send_sem=send_sem, recv_sem=recv_sem,
+            device_id=device, device_id_type=MESH,
         )
         copy.start()
         return copy
 
-    corners[place] = values_ref[:, :split]
-    copies = [start(corners.at[place], corners.at[place], index) for index in range(3)]
-    for copy in copies:
+    barrier = pltpu.get_barrier_semaphore()
+    chips = [{"dp": (me + 2 * step) % 8} for step in (1, 2, 3)]
+    square = [{"tensor": device} for device in (along_x, along_y, corner)]
+    for other in square + [{"dp": sibling}] + chips:
+        pl.semaphore_signal(barrier, inc=1, device_id=other, device_id_type=MESH)
+    pl.semaphore_wait(barrier, 7)
+
+    def term(owner, part):
+        return first_ref.at[pl.ds(pl.multiple_of(owner * rows + part * half, half), half)]
+
+    def rows_at(owner, part):
+        return term(owner, part)[...].astype(wide)
+
+    plan = [
+        (term(corner, 0), square_x.at[1], square[0]),
+        (term(corner, 1), square_y.at[1], square[1]),
+        (term(along_x, 0), square_x.at[0], square[0]),
+        (term(along_y, 1), square_y.at[0], square[1]),
+    ]
+    copies = [
+        start(source, target, square_send.at[i], square_recv.at[i], device)
+        for i, (source, target, device) in enumerate(plan)
+    ]
+    bias_mine[...] = bias_ref[...]
+    bias_copies = [start(bias_mine, bias_came, bias_send.at[0], bias_recv.at[0], {"dp": sibling})]
+    bias_copies[0].wait_recv()
+    bias_slots[chip] = bias_mine[...] + bias_came[...]
+    bias_copies += [
+        start(bias_slots.at[chip], bias_slots.at[chip], bias_send.at[1 + i], bias_recv.at[1 + i], chips[i])
+        for i in range(3)
+    ]
+    copies[0].wait_recv()
+    staged[0] = (rows_at(along_y, 0) + square_x[1].astype(wide)).astype(low)
+    copies.append(start(staged.at[0], square_last.at[0], square_send.at[4], square_recv.at[4], square[1]))
+    copies[1].wait_recv()
+    staged[1] = (rows_at(along_x, 1) + square_y[1].astype(wide)).astype(low)
+    copies.append(start(staged.at[1], square_last.at[1], square_send.at[5], square_recv.at[5], square[0]))
+    gain = gain_ref[...]
+    vector_gain = jnp.zeros_like(gain)
+    vector_shift = jnp.zeros_like(gain)
+    for part, near in enumerate((square_x, square_y)):
+        here = slice(part * half, (part + 1) * half)
+        copies[2 + part].wait_recv()
+        copies[4 + part].wait_recv()
+        grad = rows_at(place, part) + near[0].astype(wide) + square_last[part].astype(wide)
+        normed = normed_ref[here, :]
+        vector_gain += jnp.sum(grad * normed, 0, keepdims=True)
+        vector_shift += jnp.sum(grad, 0, keepdims=True)
+        scaled = grad * gain
+        inner = (
+            scaled
+            - jnp.mean(scaled, -1, keepdims=True)
+            - normed * jnp.mean(scaled * normed, -1, keepdims=True)
+        )
+        input_out[here, :] = grad_ref[here, :] + recip_ref[here, :] * inner
+    corners[place, 0:1, :] = vector_gain
+    corners[place, 1:2, :] = second_ref[0:1, :]
+    corners[place, 2:3, :] = vector_shift
+    corners[place, 3:4, :] = second_ref[1:2, :]
+    vector_copies = [
+        start(corners.at[place], corners.at[place], vector_send.at[i], vector_recv.at[i], square[i]) for i in range(3)
+    ]
+    for copy in vector_copies:
         copy.wait_recv()
-    mine[:, :split] = (corners[0] + corners[1]) + (corners[2] + corners[3])
-    mine[:, split:] = values_ref[:, split:]
-    copies.append(start(mine, came, 3))
-    copies[3].wait_recv()
-    slots_ref[chip] = mine[...] + came[...]
-    last = [start(slots_ref.at[chip], slots_ref.at[chip], index) for index in (4, 5, 6)]
-    for copy in last:
+    vector_mine[...] = (corners[0] + corners[1]) + (corners[2] + corners[3])
+    vector_copies.append(start(vector_mine, vector_came, vector_send.at[3], vector_recv.at[3], {"dp": sibling}))
+    vector_copies[3].wait_recv()
+    vector_slots[chip] = vector_mine[...] + vector_came[...]
+    vector_copies += [
+        start(vector_slots.at[chip], vector_slots.at[chip], vector_send.at[4 + i], vector_recv.at[4 + i], chips[i])
+        for i in range(3)
+    ]
+    for copy in vector_copies[4:] + bias_copies[1:]:
         copy.wait_recv()
-    out_ref[...] = (slots_ref[0] + slots_ref[1]) + (slots_ref[2] + slots_ref[3])
-    for copy in copies + last:
+    vector_out[...] = (vector_slots[0] + vector_slots[1]) + (vector_slots[2] + vector_slots[3])
+    bias_out[...] = (bias_slots[0] + bias_slots[1]) + (bias_slots[2] + bias_slots[3])
+    for copy in copies + vector_copies + bias_copies:
         copy.wait_send()
 
 
-def slice_total(values, split):
+def last_reduce(first, normed, recip, gain, grad, second, bias):
     dma = pltpu.SemaphoreType.DMA
-    shape = values.shape
+    low, wide = jnp.bfloat16, jnp.float32
+    shape, vmem = jax.ShapeDtypeStruct, pltpu.VMEM
+    rows, model = normed.shape
+    pair = vmem((2, rows // 2, model), low)
     return pl.pallas_call(
-        functools.partial(total_kernel, split),
-        out_shape=jax.ShapeDtypeStruct(shape, values.dtype),
-        in_specs=[pl.BlockSpec(memory_space=pltpu.VMEM)],
-        out_specs=pl.BlockSpec(memory_space=pltpu.VMEM),
+        last_kernel,
+        out_shape=(shape((rows, model), wide), shape((4, model), wide), shape(bias.shape, wide)),
+        in_specs=[pl.BlockSpec(memory_space=pltpu.VMEM)] * 7,
+        out_specs=(pl.BlockSpec(memory_space=pltpu.VMEM),) * 3,
         scratch_shapes=[
-            pltpu.VMEM((4, 8, split), values.dtype),
-            pltpu.VMEM(shape, values.dtype),
-            pltpu.VMEM(shape, values.dtype),
-            pltpu.VMEM((4, *shape), values.dtype),
-            dma((7,)),
-            dma((7,)),
+            pair, pair, pair, pair,
+            vmem((4, 4, model), wide),
+            vmem((4, model), wide),
+            vmem((4, model), wide),
+            vmem((4, 4, model), wide),
+            vmem(bias.shape, wide),
+            vmem(bias.shape, wide),
+            vmem((4, *bias.shape), wide),
+            dma((6,)), dma((6,)), dma((7,)), dma((7,)), dma((4,)), dma((4,)),
         ],
-        compiler_params=pltpu.CompilerParams(collective_id=3, has_side_effects=True),
-        cost_estimate=pl.CostEstimate(flops=0, bytes_accessed=30_000_000, transcendentals=0),
-        name="slice_total",
-    )(values)
+        compiler_params=pltpu.CompilerParams(
+            collective_id=3, has_side_effects=True, vmem_limit_bytes=40 * 1024 * 1024
+        ),
+        cost_estimate=pl.CostEstimate(flops=0, bytes_accessed=120_000_000, transcendentals=0),
+        name="last_reduce",
+    )(first, normed, recip, gain, grad, second, bias)
 
 
 def after(late, early):
@@ -627,17 +730,26 @@
     def reduce_rows(self, terms, ready, name):
         return lax.psum_scatter(terms, "tensor", scatter_dimension=0, tiled=True).astype(jnp.float32)
 
-    def begin(self, a, dy, bias, w_qkv, w_output):
+    def begin(self, x, gain, shift, dy, bias, w_qkv, w_output, gate_up, down):
+        low = jnp.bfloat16
+        out, normed, recip = layer_norm(x.astype(jnp.float32), gain, shift)
         return (
-            self.gather_rows(a),
+            self.gather_rows(out.astype(low)),
             self.gather_rows(dy),
             lax.all_gather(bias, "dp", axis=2, tiled=True),
-            gather_dp(w_qkv, 1),
-            gather_dp(w_output, 1),
-        )
-
-    def totals(self, vectors, sums):
-        return lax.psum(vectors, ("dp", "tensor")), lax.psum(sums, "dp")
+            gather_dp(w_qkv.astype(low), 1),
+            gather_dp(w_output.astype(low), 1),
+            normed,
+            recip,
+            gate_up.astype(low),
+            down.astype(low),
+        )
+
+    def finish(self, first, normed, recip, gain, grad, second, bias):
+        first = self.reduce_rows(first, None, 0)
+        vectors = jnp.stack([jnp.sum(first * normed, 0), second[0], jnp.sum(first, 0), second[1]])
+        input_grad = grad + norm_back(first, normed, recip, gain)
+        return input_grad, lax.psum(vectors, ("dp", "tensor")), lax.psum(bias, "dp")
 
 
 class Line(Plain):
@@ -647,25 +759,24 @@
     def reduce_rows(self, terms, ready, name):
         return square_reduce(terms, ready, name)
 
-    def begin(self, a, dy, bias, w_qkv, w_output):
+    def begin(self, x, gain, shift, dy, bias, w_qkv, w_output, gate_up, down):
         parts, heads, few = bias.shape
-        flat = bias.astype(jnp.float32).reshape(-1)
-        width = -(-flat.shape[0] // 1024) * 1024
-        flat = jnp.pad(flat, (0, width - flat.shape[0])).reshape(8, -1)
-        a, dy, came, w_qkv, w_output = start_gather(a, dy, flat, w_qkv, w_output)
+        a, dy, came, *others = start_gather(
+            x, gain.reshape(1, -1), shift.reshape(1, -1), dy, self.flat(bias), w_qkv, w_output, gate_up, down
+        )
         came = came.reshape(8, -1)[:, : parts * heads * few].reshape(8, parts, heads, few)
-        return a, dy, came.transpose(1, 2, 0, 3).reshape(parts, heads, -1), w_qkv, w_output
-
-    def totals(self, vectors, sums):
-        split = vectors.size // 8
-        flat = sums.reshape(-1)
-        width = -(-flat.shape[0] // 1024) * 1024
-        flat = jnp.pad(flat, (0, width - flat.shape[0])).reshape(8, -1)
-        total = slice_total(jnp.concatenate([vectors.reshape(8, split), flat], 1), split)
-        return (
-            total[:, :split].reshape(vectors.shape),
-            total[:, split:].reshape(-1)[: sums.size].reshape(sums.shape),
-        )
+        return a, dy, came.transpose(1, 2, 0, 3).reshape(parts, heads, -1), *others
+
+    def flat(self, values):
+        values = values.astype(jnp.float32).reshape(-1)
+        width = -(-values.shape[0] // 1024) * 1024
+        return jnp.pad(values, (0, width - values.shape[0])).reshape(8, -1)
+
+    def finish(self, first, normed, recip, gain, grad, second, bias):
+        input_grad, vectors, total = last_reduce(
+            first, normed, recip, gain.reshape(1, -1), grad, second, self.flat(bias)
+        )
+        return input_grad, vectors, total.reshape(-1)[: bias.size].reshape(bias.shape)
 
 
 def row_major(values):
@@ -677,9 +788,7 @@
 
 
 def scatter_dp(terms, axis):
-    return lax.psum_scatter(terms.astype(jnp.bfloat16), "dp", scatter_dimension=axis, tiled=True).astype(
-        jnp.float32
-    )
+    return lax.psum_scatter(terms.astype(jnp.bfloat16), "dp", scatter_dimension=axis, tiled=True)
 
 
 def local(
@@ -713,18 +822,17 @@
     local_width = qkv_weight.shape[2]
     head_size = local_width // local_heads
     xin = inputs.astype(jnp.float32)
-    first_out, first_normed, first_recip = layer_norm(xin, gains[0], shifts[0])
-    a_all, dy_all, bias_all, w_qkv, w_output = routes.begin(
-        first_out.astype(low), cotangent, biases.astype(low), qkv_weight.astype(low), out_weight.astype(low)
+    a_all, dy_all, bias_all, w_qkv, w_output, first_normed, first_recip, gate_low, down_low = routes.begin(
+        inputs, gains[0], shifts[0], cotangent, biases.astype(low), qkv_weight, out_weight, gate_up, down_weight
     )
     bias_all = bias_all.reshape(3, local_width).astype(jnp.float32)
-    w_gate_up = gather_dp(after(gate_up, w_output), 1)
+    w_gate_up = gather_dp(after(gate_low, w_output), 1)
     lin = jnp.einsum("rd,kdc->krc", a_all, w_qkv, preferred_element_type=jnp.float32)
     qkv, heads, logs = attention_forward(lin, bias_all, head_size)
     resid = xin + routes.reduce_rows(mxu(heads, w_output, NN).astype(low), logs, 4)
     second_out, second_normed, second_recip = layer_norm(resid, gains[1], shifts[1])
     m_all = routes.gather_rows(second_out.astype(low))
-    w_down = gather_dp(after(down_weight, (w_gate_up, m_all)), 1)
+    w_down = gather_dp(after(down_low, (w_gate_up, m_all)), 1)
     gate_vals = jnp.einsum("rd,kdc->krc", m_all, w_gate_up, preferred_element_type=jnp.float32)
     gate_lin, upward = gate_vals[0], gate_vals[1]
     sigmoid_gate = jax.nn.sigmoid(gate_lin)
@@ -758,25 +866,31 @@
     lin_grads, bias_terms = attention_backward(qkv, heads_grad, logs, head_size)
     qkv_terms = jnp.einsum("rd,krc->kdc", a_all, lin_grads, preferred_element_type=jnp.float32)
     qkv_terms = row_major(qkv_terms.astype(low))
-    out_grad = scatter_dp(after(out_terms, (gate_grad, lin_grads)), 1)
-    down_sum = routes.reduce_rows(block_terms, bias_terms, 6)
-    qkv_grad = scatter_dp(after(qkv_terms, (out_grad, down_sum)), 1)
     first_terms = jnp.einsum(
         "krc,kdc->rd", lin_grads, w_qkv, preferred_element_type=jnp.float32
     ).astype(low)
-    first_grad = routes.reduce_rows(first_terms, bias_terms, 7)
-    input_grad = resid_grad + norm_back(first_grad, first_normed, first_recip, gains[0])
-    vectors = jnp.stack(
-        [jnp.sum(first_grad * first_normed, 0), gain_second, jnp.sum(first_grad, 0), shift_second]
+    out_grad = scatter_dp(after(out_terms, (gate_grad, qkv_terms)), 1)
+    down_sum = routes.reduce_rows(block_terms, qkv_terms, 6)
+    qkv_grad = scatter_dp(after(qkv_terms, (out_grad, down_sum)), 1)
+    block_out = (resid + down_sum).astype(low)
+    input_grad, vectors, bias_sum = routes.finish(
+        after(first_terms, down_sum),
+        first_normed,
+        first_recip,
+        gains[0],
+        resid_grad,
+        jnp.stack([gain_second, shift_second]),
+        bias_terms,
     )
-    vectors, bias_sum = routes.totals(vectors, bias_terms)
     gains_grad, shifts_grad = vectors[:2], vectors[2:]
-    out_grad, down_grad, gate_grad = after((out_grad, down_grad, gate_grad), first_grad)
+    down_grad, gate_grad, out_grad = (
+        grad.astype(jnp.float32) for grad in after((down_grad, gate_grad, out_grad), vectors)
+    )
+    qkv_grad = qkv_grad.astype(jnp.float32)
     per_dp = biases.shape[2]
     biases_grad = lax.dynamic_slice_in_dim(
         bias_sum.reshape(3, local_heads, head_size), lax.axis_index("dp") * per_dp, per_dp, 2
     )
-    block_out = (resid + down_sum).astype(low)
     gain_new = adamw(gains, gains_grad, momentum_gains, variance_gains, 0.0, vector_rate)
     shift_new = adamw(shifts, shifts_grad, momentum_shifts, variance_shifts, 0.0, vector_rate)
     qkv_new = adamw(qkv_weight, qkv_grad, momentum_qkv, variance_qkv, decay_rate, learn_rate)

time: 627 us -> 605 us (0.965)
  other arithmetic: 53.5 us -> 31.4 us
    pallas_call x2, Pallas kernels: 98.2 us -> 136 us  [the longest x1 80.9 us: start_gather(): pl.pallas_call(start_kernel, out_shape=(shape((4 * rows, model), low), sh...]
    pallas_call x4 -> x3, Pallas kernels: 142 us -> 106 us  [square_reduce(): pl.pallas_call(reduce_kernel, out_shape=jax.ShapeDtypeStruct((rows, width...]
    convert_element_type x8 -> x0, other arithmetic: 13.3 us -> none  [the longest x3 6.12 us: scatter_dp(): lax.psum_scatter(terms.astype(jnp.bfloat16), 'dp', scatter_dimension=axis...]
    unnamed x111 -> x104, local copies, waits for them, and re-layouts: 17.3 us -> 30.2 us
    sub x7 -> x6, other arithmetic: 17.6 us -> 18.8 us  [adamw(): return (weight - rate * change, moment_new, second_new)]
  transfers between devices with their start and end apart: 6 -> 6, of which waited for: 3 -> 3; matrix products, arithmetic and copies ran while one was open for 28% -> 26% of each run, Pallas kernels for 44% -> 46%
where the time goes in v3:
time: 605 us; the launch traced here: 596 us
  Pallas kernels  353 us (58%)
  matrix products  130 us (21%)
  waiting for transfers between devices  35 us (6%)
  other arithmetic  31.4 us (5%)
  local copies, waits for them, and re-layouts  31.4 us (5%)
  between operations  14.9 us (2%)
    pallas_call x3, Pallas kernels, square_reduce(): pl.pallas_call(reduce_kernel, out_shape=jax.ShapeDtypeStruct((rows, width...  106 us
    pallas_call x1, Pallas kernels, start_gather(): pl.pallas_call(start_kernel, out_shape=(shape((4 * rows, model), low), sh...  80.9 us
    pallas_call x2, Pallas kernels, square_gather(): pl.pallas_call(gather_kernel, out_shape=jax.ShapeDtypeStruct((4 * rows, w...  72.2 us
    pallas_call x1, Pallas kernels, last_reduce(): pl.pallas_call(last_kernel, out_shape=(shape((rows, model), wide), shape(...  55.4 us
    dot_general x6, matrix products, mxu(): lax.dot_general(left, right, dims, preferred_element_type=jnp.float32)  46.3 us
    unnamed x104, local copies, waits for them, and re-layouts  30.2 us
    all_gather x2, waiting for transfers between devices, gather_dp(): lax.all_gather(block.astype(jnp.bfloat16), 'dp', axis=axis, tiled=True)  29.6 us
    pallas_call x1, Pallas kernels, attention_backward(): pl.pallas_call(functools.partial(backward_kernel, head_size), grid=(rows...  23.8 us
  transfers between devices with their start and end apart: 6, of which 3 were waited for; matrix products, arithmetic and copies ran while one was open for 26% of the time, Pallas kernels for 46%

profile of v3, /device:TPU:0, one launch (start us, length us, event | category | flops | bytes accessed | tf_op | source)
XLA Modules:
  0.0 596.2 jit_solution(17077059727805441011)
XLA Ops:
  12.4 80.9 %start_gather.1 = (bf16[1024,2048]{1,0:T(8,128)(2,1)}, bf16[1024,2048]{1,0:T(8,128)(2,1)}, f32[8,8,128]{2,1,0:T(8,128)S(1)}, bf16[3,2048,512]{2,1,0:T(8,128)(2,1...) custom-call(bf16[256,2048]{1,0:T(8,128)(2,1)S(1)} %copy-done.7, ...), custom_call_target="tpu_custom_call" | custom-call | bytes 200000000 | tf_op jit(solution)/shard_map/start_gather/pallas_call | solution.py:558
  93.7 11.8 %fusion.9.lin_ref = f32[3,1024,512]{2,1,0:T(8,128)} fusion(bf16[3,2048,512]{2,1,0:T(8,128)(2,1)} %get-tuple-element.57, bf16[1024,2048]{1,0:T(8,128)(2,1)} %get-tuple-element.58), kind=kOutput, calls=%fused_computation.28 | convolution fusion | flops 6442450944 | bytes 16777216 | tf_op jit(solution)/shard_map/rd,kdc->krc/dot_general | solution.py:830
  105.5 15.0 %attend_forward.1 = (bf16[3,1024,512]{2,1,0:T(8,128)(2,1)S(1)}, bf16[1024,512]{1,0:T(8,128)(2,1)S(1)}, f32[2,8,1024]{2,1,0:T(8,128)S(1)}) custom-call(f32[3,1024,512]{2,1,0:T(8,128)} %fusion.9.lin_ref, f32[3,512]{1,0:T(4,128)S(1)} %reshape_reshape.6.bias_ref, f32[3,1024,128]{2,1,0:T(8,128)S(1)} %copy-done.19), custom_call_target="tpu_custom_call" | custom-call | flops 4294967296 | bytes 13631488 | tf_op jit(solution)/shard_map/attend_forward/pallas_call | solution.py:129
  122.9 38.0 %square_reduce.3 = f32[256,2048]{1,0:T(8,128)S(1)} custom-call(bf16[1024,2048]{1,0:T(8,128)(2,1)S(1)} %convolution_convert_fusion.2.terms_ref, f32[2,8,1024]{2,1,0:T(8,128)S(1)} %get-tuple-element.62.ready_ref.lse_ref), custom_call_target="tpu_custom_call" | custom-call | bytes 125829120 | tf_op jit(solution)/shard_map/square_reduce/pallas_call | solution.py:357
  163.0 37.6 %square_gather.2 = bf16[1024,2048]{1,0:T(8,128)(2,1)} custom-call(bf16[256,2048]{1,0:T(8,128)(2,1)} %add_convert_fusion.1.block_ref), custom_call_target="tpu_custom_call" | custom-call | bytes 62914560 | tf_op jit(solution)/shard_map/square_gather/pallas_call | solution.py:289
  201.2 16.6 %convolution_bitcast_fusion = f32[2,1024,1408]{1,2,0:T(8,128)S(1)} fusion(bf16[2,2048,1408]{2,1,0:T(8,128)(2,1)} %all-gather.3.cloned.1.call-done, bf16[1024,2048]{1,0:T(8,128)(2,1)} %square_gather.2), kind=kOutput, calls=%fused_computation.4 | convolution fusion | flops 11811160064 | bytes 27262976 | tf_op jit(solution)/shard_map/rd,kdc->krc/dot_general | solution.py:836
  224.8 8.0 %convolution_convert_fusion = bf16[1408,2048]{1,0:T(8,128)(2,1)} fusion(bf16[1024,1408]{0,1:T(8,128)(2,1)S(1)} %multiply_convert_fusion.2, bf16[1024,2048]{1,0:T(8,128)(2,1)S(1)} %copy-done.48), kind=kOutput, calls=%fused_computation.3 | convolution fusion | flops 5908463616 | bytes 12845056 | tf_op jit(solution)/shard_map/dot_general | solution.py:84
  232.9 29.0 %all-gather.5.cloned.1.call-done = bf16[1408,2048]{1,0:T(8,128)(2,1)} async-done(((bf16[1408,256]{1,0:T(8,128)(2,1)}), bf16[1408,2048]{1,0:T(8,128)(2,1)}) %all-gather.5.cloned.1.call-update) | async-done | bytes 5767184 | tf_op jit(solution)/shard_map/all_gather | solution.py:787
  261.9 11.7 %convolution_convert_fusion.1.terms_ref = bf16[1024,2048]{1,0:T(8,128)(2,1)} fusion(bf16[1024,1408]{0,1:T(8,128)(2,1)} %copy-done.29, bf16[1408,2048]{1,0:T(8,128)(2,1)} %all-gather.5.cloned.1.call-done), kind=kOutput, calls=%fused_computation.20 | convolution fusion | flops 5907677184 | bytes 12845056 | tf_op jit(solution)/shard_map/dot_general | solution.py:84
  273.7 12.6 %fusion.8 = (bf16[1,1024,1408]{1,2,0:T(8,128)(2,1)}, bf16[1,1024,1408]{1,2,0:T(8,128)(2,1)}) fusion(f32[2,1024,1408]{1,2,0:T(8,128)} %copy-done.25, bf16[1024,2048]{1,0:T(8,128)(2,1)S(1)} %copy-done.49, bf16[1408,2048]{1,0:T(8,128)(2,1)S(1)} %copy-done.46), kind=kOutput, calls=%fused_computation.27 | convolution fusion | flops 5924323328 | bytes 27262976 | tf_op jit(solution)/shard_map/dot_general | solution.py:84
  286.2 17.4 %convert_bitcast_fusion = bf16[2,2048,1408]{2,1,0:T(8,128)(2,1)} fusion(bf16[1024,2048]{1,0:T(8,128)(2,1)S(1)} %copy-done.28, bf16[1,1024,1408]{1,2,0:T(8,128)(2,1)} %get-tuple-element.121, bf16[1,1024,1408]{1,2,0:T(8,128)(2,1)} %get-tuple-element.120), kind=kOutput, calls=%fused_computation | convolution fusion | flops 11819810816 | bytes 21495808 | tf_op jit(solution)/shard_map/rd,krc->kdc/dot_general | solution.py:850
  303.6 18.4 %bitcast_convert_fusion.1.terms_ref = bf16[1024,2048]{1,0:T(8,128)(2,1)} fusion(bf16[2,2048,1408]{2,1,0:T(8,128)(2,1)} %all-gather.3.cloned.1.call-done, bf16[1,1024,1408]{1,2,0:T(8,128)(2,1)} %get-tuple-element.121, bf16[1,1024,1408]{1,2,0:T(8,128)(2,1)} %get-tuple-element.120), kind=kOutput, calls=%fused_computation.2 | convolution fusion | flops 11816140800 | bytes 21495808 | tf_op jit(solution)/shard_map/krc,kdc->rd/dot_general | solution.py:852
  322.0 5.3 reduce-scatter.5.cloned.1.call-done.ready_ref
  330.6 35.2 %square_reduce.4 = f32[256,2048]{1,0:T(8,128)S(1)} custom-call(bf16[1024,2048]{1,0:T(8,128)(2,1)S(1)} %copy-done.4, bf16[1408,256]{1,0:T(8,128)(2,1)S(1)} %copy-done.9), custom_call_target="tpu_custom_call" | custom-call | bytes 125829120 | tf_op jit(solution)/shard_map/square_reduce/pallas_call | solution.py:357
  370.5 34.6 %square_gather.3 = bf16[1024,2048]{1,0:T(8,128)(2,1)} custom-call(bf16[256,2048]{1,0:T(8,128)(2,1)} %get-tuple-element.116.block_ref), custom_call_target="tpu_custom_call" | custom-call | bytes 62914560 | tf_op jit(solution)/shard_map/square_gather/pallas_call | solution.py:289
  405.2 6.2 %convolution_convert_fusion.3 = bf16[512,2048]{1,0:T(8,128)(2,1)} fusion(bf16[1024,512]{1,0:T(8,128)(2,1)} %copy-done.21, bf16[1024,2048]{1,0:T(8,128)(2,1)} %square_gather.3), kind=kOutput, calls=%fused_computation.22 | convolution fusion | flops 2148532224 | bytes 7340032 | tf_op jit(solution)/shard_map/dot_general | solution.py:84
  411.4 5.4 convolution_convert_fusion.4.grad_ref
  416.9 23.8 %attend_backward.1 = (bf16[3,1024,512]{2,1,0:T(8,128)(2,1)S(1)}, f32[1,3,512]{2,1,0:T(4,128)S(1)}) custom-call(bf16[3,1024,512]{2,1,0:T(8,128)(2,1)} %copy-done.22, bf16[1024,512]{1,0:T(8,128)(2,1)S(1)} %convolution_convert_fusion.4.grad_ref, f32[2,8,1024]{2,1,0:T(8,128)S(1)} %copy-done.18, f32[3,1024,128]{2,1,0:T(8,128)S(1)} %copy-done.20), custom_call_target="tpu_custom_call" | custom-call | flops 10737418240 | bytes 13631488 | tf_op jit(solution)/shard_map/attend_backward/pallas_call | solution.py:206
  442.3 8.6 %convert_bitcast_fusion.1.ready_ref = bf16[3,2048,512]{2,1,0:T(8,128)(2,1)} fusion(bf16[3,1024,512]{2,1,0:T(8,128)(2,1)S(1)} %get-tuple-element.70, bf16[1024,2048]{1,0:T(8,128)(2,1)S(1)} %copy-done.47), kind=kOutput, calls=%fused_computation.5 | convolution fusion | flops 6445596672 | bytes 13631488 | tf_op jit(solution)/shard_map/rd,krc->kdc/dot_general | solution.py:867
  455.9 32.6 %square_reduce.5 = f32[256,2048]{1,0:T(8,128)S(1)} custom-call(bf16[1024,2048]{1,0:T(8,128)(2,1)S(1)} %copy-done.2, bf16[3,2048,512]{2,1,0:T(8,128)(2,1)S(1)} %copy-done), custom_call_target="tpu_custom_call" | custom-call | bytes 125829120 | tf_op jit(solution)/shard_map/square_reduce/pallas_call | solution.py:357
  489.8 11.3 %bitcast_convert_fusion.first_ref = bf16[1024,2048]{1,0:T(8,128)(2,1)} fusion(bf16[3,1024,512]{2,1,0:T(8,128)(2,1)} %copy-done.23, bf16[3,2048,512]{2,1,0:T(8,128)(2,1)} %get-tuple-element.57), kind=kOutput, calls=%fused_computation.1 | convolution fusion | flops 6444548096 | bytes 13631488 | tf_op jit(solution)/shard_map/krc,kdc->rd/dot_general | solution.py:869
  505.6 55.4 %last_reduce.1 = (f32[256,2048]{1,0:T(8,128)S(1)}, f32[4,2048]{1,0:T(4,128)S(1)}, f32[8,256]{1,0:T(8,128)S(1)}) custom-call(bf16[1024,2048]{1,0:T(8,128)(2,1)S(1)} %copy-done.3, f32[256,2048]{1,0:T(8,128)S(1)} %copy-done.12, f32[256,1]{1,0:T(8,128)S(1)} %get-tuple-element.73.recip_ref, f32[1,2048]{1,0:T(1,128)S(1)} %copy-done.16, ...), custom_call_target="tpu_custom_call" | custom-call | bytes 120000000 | tf_op jit(solution)/shard_map/last_reduce/pallas_call | solution.py:698
  575.2 6.7 %multiply_subtract_fusion = (f32[2,256,1408]{2,1,0:T(8,128)}, f32[2,256,1408]{2,1,0:T(8,128)}, f32[2,256,1408]{2,1,0:T(8,128)}, f32[2,256,1408]{2,1,0:T(8,128)}) fusion(f32[2,256,1408]{2,1,0:T(8,128)S(1)} %copy-done.26, f32[2,256,1408]{2,1,0:T(8,128)S(1)} %copy-done.30, f32[2,256,1408]{2,1,0:T(8,128)} %param.46, bf16[2,256,1408]{2,1,0:T(8,128)(2,1)S(1)} %copy-done.33), kind=kLoop, calls=%fused_computation.25 | loop fusion | flops 11534336 | bytes 21626880 | tf_op jit(solution)/shard_map/sub | solution.py:47
  581.9 6.0 multiply_subtract_fusion.1
  (149 shorter events, 53.4 us)
Async XLA Ops:
  7.2 194.0 %all-gather.3.cloned.1.call-start = ((), (), s32[]{:S(2)}) async-start(), calls=%async_computation.4 | async-start | bytes 12976128 | tf_op jit(solution)/shard_map/all_gather | solution.py:787
  8.9 84.4 %copy-start.15 = (f32[1,2048]{1,0:T(1,128)}, f32[1,2048]{1,0:T(1,128)S(1)}, u32[]{:S(2)}) copy-start(f32[1,2048]{1,0:T(1,128)S(1)} %get-tuple-element.127.gain_ref) | copy-start | bytes 24580
  93.4 168.6 %all-gather.5.cloned.1.call-start = ((), (), s32[]{:S(2)}) async-start(), calls=%async_computation.5 | async-start | bytes 6488064 | tf_op jit(solution)/shard_map/all_gather | solution.py:787
  93.7 11.8 %copy-start.19 = (f32[3,1024,128]{2,1,0:T(8,128)S(1)}, f32[3,1024,128]{2,1,0:T(8,128)}, u32[]{:S(2)}) copy-start(f32[3,1024,128]{2,1,0:T(8,128)} %constant.42.clone.table_ref) | copy-start | bytes 4718596
  105.5 15.0 %copy-start.50 = (bf16[512,2048]{1,0:T(8,128)(2,1)S(1)}, bf16[512,2048]{1,0:T(8,128)(2,1)}, u32[]{:S(2)}) copy-start(bf16[512,2048]{1,0:T(8,128)(2,1)} %get-tuple-element.61) | copy-start | bytes 6291460
  122.9 38.0 %copy-start.8 = (bf16[256,2048]{1,0:T(8,128)(2,1)S(1)}, bf16[256,2048]{1,0:T(8,128)(2,1)}, u32[]{:S(2)}) copy-start(bf16[256,2048]{1,0:T(8,128)(2,1)} %x_ref.1) | copy-start | bytes 3145732
  161.2 204.6 %copy-start.24 = (f32[256,2048]{1,0:T(8,128)}, f32[256,2048]{1,0:T(8,128)S(1)}, u32[]{:S(2)}) copy-start(f32[256,2048]{1,0:T(8,128)S(1)} %get-tuple-element.119) | copy-start | bytes 6291460
  201.2 126.1 %reduce-scatter.5.cloned.1.call-start = ((), (), s32[]{:S(2)}) async-start(), calls=%async_computation.6 | async-start | bytes 6488064 | tf_op jit(solution)/shard_map/reduce_scatter | solution.py:791
  232.8 218.0 %reduce-scatter.7.cloned.1.call-start = ((), (), s32[]{:S(2)}) async-start(), calls=%async_computation.7 | async-start | bytes 12976128 | tf_op jit(solution)/shard_map/reduce_scatter | solution.py:791
  261.9 11.7 %copy-start.46 = (bf16[1408,2048]{1,0:T(8,128)(2,1)S(1)}, bf16[1408,2048]{1,0:T(8,128)(2,1)}, u32[]{:S(2)}) copy-start(bf16[1408,2048]{1,0:T(8,128)(2,1)} %all-gather.5.cloned.1.call-done) | copy-start | bytes 17301508
  261.9 11.7 %copy-start.49 = (bf16[1024,2048]{1,0:T(8,128)(2,1)S(1)}, bf16[1024,2048]{1,0:T(8,128)(2,1)}, u32[]{:S(2)}) copy-start(bf16[1024,2048]{1,0:T(8,128)(2,1)} %get-tuple-element.67) | copy-start | bytes 12582916
  273.6 12.6 %copy-start.28 = (bf16[1024,2048]{1,0:T(8,128)(2,1)S(1)}, bf16[1024,2048]{1,0:T(8,128)(2,1)}, u32[]{:S(2)}) copy-start(bf16[1024,2048]{1,0:T(8,128)(2,1)} %square_gather.2) | copy-start | bytes 12582916
  327.3 162.5 %reduce-scatter.9.cloned.1.call-start = ((), (), s32[]{:S(2)}) async-start(), calls=%async_computation.8 | async-start | bytes 2359296 | tf_op jit(solution)/shard_map/reduce_scatter | solution.py:791
  416.8 25.4 %copy-start.47 = (bf16[1024,2048]{1,0:T(8,128)(2,1)S(1)}, bf16[1024,2048]{1,0:T(8,128)(2,1)}, u32[]{:S(2)}) copy-start(bf16[1024,2048]{1,0:T(8,128)(2,1)} %get-tuple-element.58) | copy-start | bytes 12582916
  450.9 131.0 %reduce-scatter.11.cloned.1.call-start = ((), (), s32[]{:S(2)}) async-start(), calls=%async_computation.9 | async-start | bytes 7077888 | tf_op jit(solution)/shard_map/reduce_scatter | solution.py:791
  505.5 56.9 %copy-start.39 = (f32[3,8,8]{2,1,0:T(8,128)S(1)}, f32[3,8,8]{2,1,0:T(8,128)}, u32[]{:S(2)}) copy-start(f32[3,8,8]{2,1,0:T(8,128)} %param.30) | copy-start | bytes 2308
  505.5 56.9 %copy-start.44 = (f32[3,8,8]{2,1,0:T(8,128)S(1)}, f32[3,8,8]{2,1,0:T(8,128)}, u32[]{:S(2)}) copy-start(f32[3,8,8]{2,1,0:T(8,128)} %param.37) | copy-start | bytes 2308
  505.5 56.9 %copy-start.45 = (f32[3,8,8]{2,1,0:T(8,128)S(1)}, f32[3,8,8]{2,1,0:T(8,128)}, u32[]{:S(2)}) copy-start(f32[3,8,8]{2,1,0:T(8,128)} %param.44) | copy-start | bytes 2308
  505.5 57.6 %copy-start.37 = (f32[2,2048]{1,0:T(2,128)S(1)}, f32[2,2048]{1,0:T(2,128)}, u32[]{:S(2)}) copy-start(f32[2,2048]{1,0:T(2,128)} %param.27) | copy-start | bytes 49156
  505.5 57.6 %copy-start.38 = (f32[2,2048]{1,0:T(2,128)S(1)}, f32[2,2048]{1,0:T(2,128)}, u32[]{:S(2)}) copy-start(f32[2,2048]{1,0:T(2,128)} %param.28) | copy-start | bytes 49156
  505.5 57.6 %copy-start.40 = (f32[2,2048]{1,0:T(2,128)S(1)}, f32[2,2048]{1,0:T(2,128)}, u32[]{:S(2)}) copy-start(f32[2,2048]{1,0:T(2,128)} %param.35) | copy-start | bytes 49156
  505.5 57.6 %copy-start.41 = (f32[2,2048]{1,0:T(2,128)S(1)}, f32[2,2048]{1,0:T(2,128)}, u32[]{:S(2)}) copy-start(f32[2,2048]{1,0:T(2,128)} %param.42) | copy-start | bytes 49156
  505.5 57.6 %copy-start.42 = (f32[2,2048]{1,0:T(2,128)S(1)}, f32[2,2048]{1,0:T(2,128)}, u32[]{:S(2)}) copy-start(f32[2,2048]{1,0:T(2,128)} %param.41) | copy-start | bytes 49156
  505.6 57.6 %copy-start.43 = (f32[2,2048]{1,0:T(2,128)S(1)}, f32[2,2048]{1,0:T(2,128)}, u32[]{:S(2)}) copy-start(f32[2,2048]{1,0:T(2,128)} %param.34) | copy-start | bytes 49156
  (33 other events, 114.5 us)
Sparse Core Ops, SparseCore 0:
  93.5 107.6 all-gather.2
  202.8 59.1 all-gather.4
  264.2 63.0 reduce-scatter.4
  329.5 117.6 reduce-scatter.6
  451.0 38.4 reduce-scatter.8
  491.7 76.8 reduce-scatter.10

commit v4 on v3

--- a/solution.py
+++ b/solution.py
@@ -588,15 +588,18 @@
 
 
 def last_kernel(
-    first_ref, normed_ref, recip_ref, gain_ref, grad_ref, second_ref, bias_ref, input_out, vector_out, bias_out,
-    square_x, square_y, staged, square_last,
+    first_ref, proj_ref, normed_ref, recip_ref, gain_ref, grad_ref, second_ref, bias_ref,
+    input_out, proj_out, vector_out, bias_out,
+    square_x, square_y, staged, square_last, mine, near,
     corners, vector_mine, vector_came, vector_slots, bias_mine, bias_came, bias_slots,
-    square_send, square_recv, vector_send, vector_recv, bias_send, bias_recv,
+    square_send, square_recv, vector_send, vector_recv, bias_send, bias_recv, core_send, core_recv, line_send, line_recv,
 ):
     place, along_x, along_y = partners()
     corner = 3 - place
     me = lax.axis_index("dp")
-    chip, sibling = me // 2, me + 1 - 2 * (me % 2)
+    chip, core = me // 2, me % 2
+    sibling = me + 1 - 2 * core
+    width = proj_out.shape[1]
     rows = input_out.shape[0]
     half = rows // 2
     low, wide = jnp.bfloat16, jnp.float32
@@ -615,6 +618,25 @@
     for other in square + [{"dp": sibling}] + chips:
         pl.semaphore_signal(barrier, inc=1, device_id=other, device_id_type=MESH)
     pl.semaphore_wait(barrier, 7)
+
+    def turned(slot, which):
+        return 2 * ((chip + slot) % 4) + which
+
+    def proj_part(owner):
+        return proj_ref.at[:, pl.ds(pl.multiple_of(owner * width, width), width)]
+
+    exchange = {
+        slot: start(
+            proj_part(turned(slot, 1 - core)), mine.at[slot], core_send.at[slot], core_recv.at[slot], {"dp": sibling}
+        )
+        for slot in (3, 1, 2, 0)
+    }
+
+    def line(slot, step, part):
+        return pltpu.make_async_remote_copy(
+            src_ref=mine.at[slot], dst_ref=near.at[part], send_sem=line_send.at[part], recv_sem=line_recv.at[part],
+            device_id={"dp": turned(step, core)}, device_id_type=MESH,
+        )
 
     def term(owner, part):
         return first_ref.at[pl.ds(pl.multiple_of(owner * rows + part * half, half), half)]
@@ -632,6 +654,35 @@
         start(source, target, square_send.at[i], square_recv.at[i], device)
         for i, (source, target, device) in enumerate(plan)
     ]
+    for slot in (3, 1, 2):
+        exchange[slot].wait_recv()
+        mine[slot] = (mine[slot].astype(wide) + proj_part(turned(slot, core))[...].astype(wide)).astype(low)
+        if slot == 3:
+
+            @pl.when(chip == 0)
+            def _():
+                line(3, 1, 0).start()
+
+            @pl.when((chip == 1) | (chip == 2))
+            def _():
+                line(3, 3, 3).start()
+
+        elif slot == 1:
+
+            @pl.when(chip == 3)
+            def _():
+                line(1, 3, 0).start()
+
+            @pl.when((chip == 1) | (chip == 2))
+            def _():
+                line(1, 1, 1).start()
+
+        else:
+
+            @pl.when((chip == 0) | (chip == 3))
+            def _():
+                line(2, 2, 2).start()
+
     bias_mine[...] = bias_ref[...]
     bias_copies = [start(bias_mine, bias_came, bias_send.at[0], bias_recv.at[0], {"dp": sibling})]
     bias_copies[0].wait_recv()
@@ -646,14 +697,31 @@
     copies[1].wait_recv()
     staged[1] = (rows_at(along_x, 1) + square_y[1].astype(wide)).astype(low)
     copies.append(start(staged.at[1], square_last.at[1], square_send.at[5], square_recv.at[5], square[0]))
+
+    @pl.when((chip == 1) | (chip == 2))
+    def _():
+        line(0, 1, 0).wait_recv()
+        mine[2] = (mine[2].astype(wide) + near[0].astype(wide)).astype(low)
+        line(2, 2, 2).start()
+
+    @pl.when(chip == 0)
+    def _():
+        line(3, 1, 0).wait_send()
+        line(1, 1, 1).start()
+
+    @pl.when(chip == 3)
+    def _():
+        line(1, 3, 0).wait_send()
+        line(3, 3, 3).start()
+
     gain = gain_ref[...]
     vector_gain = jnp.zeros_like(gain)
     vector_shift = jnp.zeros_like(gain)
-    for part, near in enumerate((square_x, square_y)):
+    for part, came in enumerate((square_x, square_y)):
         here = slice(part * half, (part + 1) * half)
         copies[2 + part].wait_recv()
         copies[4 + part].wait_recv()
-        grad = rows_at(place, part) + near[0].astype(wide) + square_last[part].astype(wide)
+        grad = rows_at(place, part) + came[0].astype(wide) + square_last[part].astype(wide)
         normed = normed_ref[here, :]
         vector_gain += jnp.sum(grad * normed, 0, keepdims=True)
         vector_shift += jnp.sum(grad, 0, keepdims=True)
@@ -685,23 +753,53 @@
         copy.wait_recv()
     vector_out[...] = (vector_slots[0] + vector_slots[1]) + (vector_slots[2] + vector_slots[3])
     bias_out[...] = (bias_slots[0] + bias_slots[1]) + (bias_slots[2] + bias_slots[3])
-    for copy in copies + vector_copies + bias_copies:
+
+    exchange[0].wait_recv()
+    line(2, 2, 2).wait_recv()
+
+    @pl.when(chip > 0)
+    def _():
+        line(1, 1, 1).wait_recv()
+
+    @pl.when(chip < 3)
+    def _():
+        line(3, 3, 3).wait_recv()
+
+    total = proj_part(turned(0, core))[...].astype(wide) + mine[0].astype(wide) + near[2].astype(wide)
+    total = total + jnp.where(chip > 0, near[1].astype(wide), 0.0)
+    proj_out[...] = total + jnp.where(chip < 3, near[3].astype(wide), 0.0)
+    for copy in copies + vector_copies + bias_copies + list(exchange.values()):
         copy.wait_send()
-
-
-def last_reduce(first, normed, recip, gain, grad, second, bias):
+    line(2, 2, 2).wait_send()
+
+    @pl.when(chip < 3)
+    def _():
+        line(1, 1, 1).wait_send()
+
+    @pl.when(chip > 0)
+    def _():
+        line(3, 3, 3).wait_send()
+
+
+def last_reduce(first, proj, normed, recip, gain, grad, second, bias):
     dma = pltpu.SemaphoreType.DMA
     low, wide = jnp.bfloat16, jnp.float32
     shape, vmem = jax.ShapeDtypeStruct, pltpu.VMEM
     rows, model = normed.shape
     pair = vmem((2, rows // 2, model), low)
+    blocks = vmem((4, proj.shape[0], proj.shape[1] // 8), low)
     return pl.pallas_call(
         last_kernel,
-        out_shape=(shape((rows, model), wide), shape((4, model), wide), shape(bias.shape, wide)),
-        in_specs=[pl.BlockSpec(memory_space=pltpu.VMEM)] * 7,
-        out_specs=(pl.BlockSpec(memory_space=pltpu.VMEM),) * 3,
+        out_shape=(
+            shape((rows, model), wide),
+            shape((proj.shape[0], proj.shape[1] // 8), wide),
+            shape((4, model), wide),
+            shape(bias.shape, wide),
+        ),
+        in_specs=[pl.BlockSpec(memory_space=pltpu.VMEM)] * 8,
+        out_specs=(pl.BlockSpec(memory_space=pltpu.VMEM),) * 4,
         scratch_shapes=[
-            pair, pair, pair, pair,
+            pair, pair, pair, pair, blocks, blocks,
             vmem((4, 4, model), wide),
             vmem((4, model), wide),
             vmem((4, model), wide),
@@ -710,13 +808,14 @@
             vmem(bias.shape, wide),
             vmem((4, *bias.shape), wide),
             dma((6,)), dma((6,)), dma((7,)), dma((7,)), dma((4,)), dma((4,)),
+            dma((4,)), dma((4,)), dma((4,)), dma((4,)),
         ],
         compiler_params=pltpu.CompilerParams(
             collective_id=3, has_side_effects=True, vmem_limit_bytes=40 * 1024 * 1024
         ),
         cost_estimate=pl.CostEstimate(flops=0, bytes_accessed=120_000_000, transcendentals=0),
         name="last_reduce",
-    )(first, normed, recip, gain, grad, second, bias)
+    )(first, proj, normed, recip, gain, grad, second, bias)
 
 
 def after(late, early):
@@ -745,11 +844,13 @@
             down.astype(low),
         )
 
-    def finish(self, first, normed, recip, gain, grad, second, bias):
+    reduce_beside = reduce_rows
+
+    def finish(self, first, proj, normed, recip, gain, grad, second, bias):
         first = self.reduce_rows(first, None, 0)
         vectors = jnp.stack([jnp.sum(first * normed, 0), second[0], jnp.sum(first, 0), second[1]])
         input_grad = grad + norm_back(first, normed, recip, gain)
-        return input_grad, lax.psum(vectors, ("dp", "tensor")), lax.psum(bias, "dp")
+        return input_grad, scatter_dp(proj, 1), lax.psum(vectors, ("dp", "tensor")), lax.psum(bias, "dp")
 
 
 class Line(Plain):
@@ -772,11 +873,21 @@
         width = -(-values.shape[0] // 1024) * 1024
         return jnp.pad(values, (0, width - values.shape[0])).reshape(8, -1)
 
-    def finish(self, first, normed, recip, gain, grad, second, bias):
-        input_grad, vectors, total = last_reduce(
-            first, normed, recip, gain.reshape(1, -1), grad, second, self.flat(bias)
-        )
-        return input_grad, vectors, total.reshape(-1)[: bias.size].reshape(bias.shape)
+    def reduce_beside(self, terms, ready, name):
+        me = lax.axis_index("tensor")
+        rows = terms.shape[0] // 4
+        parts = [lax.dynamic_slice_in_dim(terms, (me ^ step) * rows, rows, 0) for step in range(4)]
+        total = parts[0].astype(jnp.float32)
+        for step in (3, 1, 2):
+            came = lax.ppermute(parts[step], "tensor", [(i, i ^ step) for i in range(4)])
+            total = total + came.astype(jnp.float32)
+        return total
+
+    def finish(self, first, proj, normed, recip, gain, grad, second, bias):
+        input_grad, proj_grad, vectors, total = last_reduce(
+            first, proj, normed, recip, gain.reshape(1, -1), grad, second, self.flat(bias)
+        )
+        return input_grad, proj_grad, vectors, total.reshape(-1)[: bias.size].reshape(bias.shape)
 
 
 def row_major(values):
@@ -841,7 +952,9 @@
     down_terms = mxu(hidden, dy_all, TN).astype(low)
     down_grad = scatter_dp(down_terms, 1)
     w_down = after(w_down, down_terms)
-    hidden_grad = mxu(dy_all, w_down, NT)
+    block_terms = mxu(hidden, w_down, NN).astype(low)
+    down_sum = routes.reduce_beside(block_terms, None, 6)
+    hidden_grad = mxu(dy_all, after(w_down, block_terms), NT)
     gate_grad_low = (
         hidden_grad * upward * sigmoid_gate * (1.0 + gate_lin * (1.0 - sigmoid_gate))
     ).astype(low)
@@ -852,9 +965,9 @@
     second_terms = jnp.einsum(
         "krc,kdc->rd", both_grads, w_gate_up, preferred_element_type=jnp.float32
     ).astype(low)
-    block_terms = mxu(hidden, w_down, NN).astype(low)
-    gate_grad = scatter_dp(after(gate_terms, (down_grad, second_terms, block_terms)), 1)
-    second_grad = routes.reduce_rows(second_terms, down_grad, 5)
+    block_out = (resid + down_sum).astype(low)
+    gate_grad = scatter_dp(after(gate_terms, (down_grad, second_terms, block_out)), 1)
+    second_grad = routes.reduce_rows(after(second_terms, down_grad), block_out[:16, :128], 5)
     resid_grad = cotangent.astype(jnp.float32) + norm_back(
         second_grad, second_normed, second_recip, gains[1]
     )
@@ -869,12 +982,10 @@
     first_terms = jnp.einsum(
         "krc,kdc->rd", lin_grads, w_qkv, preferred_element_type=jnp.float32
     ).astype(low)
-    out_grad = scatter_dp(after(out_terms, (gate_grad, qkv_terms)), 1)
-    down_sum = routes.reduce_rows(block_terms, qkv_terms, 6)
-    qkv_grad = scatter_dp(after(qkv_terms, (out_grad, down_sum)), 1)
-    block_out = (resid + down_sum).astype(low)
-    input_grad, vectors, bias_sum = routes.finish(
-        after(first_terms, down_sum),
+    qkv_grad = scatter_dp(after(qkv_terms, gate_grad), 1)
+    input_grad, out_grad, vectors, bias_sum = routes.finish(
+        first_terms,
+        out_terms,
         first_normed,
         first_recip,
         gains[0],
@@ -884,7 +995,7 @@
     )
     gains_grad, shifts_grad = vectors[:2], vectors[2:]
     down_grad, gate_grad, out_grad = (
-        grad.astype(jnp.float32) for grad in after((down_grad, gate_grad, out_grad), vectors)
+        grad.astype(jnp.float32) for grad in (*after((down_grad, gate_grad), vectors), out_grad)
     )
     qkv_grad = qkv_grad.astype(jnp.float32)
     per_dp = biases.shape[2]

time: 605 us -> 561 us (0.927)
  Pallas kernels: 353 us -> 316 us
  local copies, waits for them, and re-layouts: 31.4 us -> 24.6 us
    pallas_call x3 -> x2, Pallas kernels: 106 us -> 74.9 us  [square_reduce(): pl.pallas_call(reduce_kernel, out_shape=jax.ShapeDtypeStruct((rows, width...]
    unnamed x104 -> x97, local copies, waits for them, and re-layouts: 30.2 us -> 21.8 us
    pallas_call x1, Pallas kernels: 55.4 us -> 47.6 us  [last_reduce(): pl.pallas_call(last_kernel, out_shape=(shape((rows, model), wide), shape(...]
  transfers between devices with their start and end apart: 6 -> 8, of which waited for: 3 -> 3; matrix products, arithmetic and copies ran while one was open for 26% -> 27% of each run, Pallas kernels for 46% -> 42%
where the time goes in v4:
time: 561 us; the launch traced here: 553 us
  Pallas kernels  316 us (56%)
  matrix products  124 us (22%)
  waiting for transfers between devices  37.6 us (7%)
  other arithmetic  31.9 us (6%)
  local copies, waits for them, and re-layouts  24.6 us (4%)
  between operations  14.9 us (3%)
    pallas_call x1, Pallas kernels, start_gather(): pl.pallas_call(start_kernel, out_shape=(shape((4 * rows, model), low), sh...  80.8 us
    pallas_call x2, Pallas kernels, square_reduce(): pl.pallas_call(reduce_kernel, out_shape=jax.ShapeDtypeStruct((rows, width...  74.9 us
    pallas_call x2, Pallas kernels, square_gather(): pl.pallas_call(gather_kernel, out_shape=jax.ShapeDtypeStruct((4 * rows, w...  74 us
    pallas_call x1, Pallas kernels, last_reduce(): pl.pallas_call(last_kernel, out_shape=(shape((rows, model), wide), shape(...  47.6 us
    dot_general x6, matrix products, mxu(): lax.dot_general(left, right, dims, preferred_element_type=jnp.float32)  42.8 us
    all_gather x2, waiting for transfers between devices, gather_dp(): lax.all_gather(block.astype(jnp.bfloat16), 'dp', axis=axis, tiled=True)  29.6 us
    pallas_call x1, Pallas kernels, attention_backward(): pl.pallas_call(functools.partial(backward_kernel, head_size), grid=(rows...  23.3 us
    unnamed x97, local copies, waits for them, and re-layouts  21.8 us
  transfers between devices with their start and end apart: 8, of which 3 were waited for; matrix products, arithmetic and copies ran while one was open for 27% of the time, Pallas kernels for 42%

profile of v4, /device:TPU:0, one launch (start us, length us, event | category | flops | bytes accessed | tf_op | source)
XLA Modules:
  0.0 552.7 jit_solution(5954470788613531376)
XLA Ops:
  12.4 80.8 %start_gather.1 = (bf16[1024,2048]{1,0:T(8,128)(2,1)}, bf16[1024,2048]{1,0:T(8,128)(2,1)}, f32[8,8,128]{2,1,0:T(8,128)S(1)}, bf16[3,2048,512]{2,1,0:T(8,128)(2,1...) custom-call(bf16[256,2048]{1,0:T(8,128)(2,1)S(1)} %copy-done.3, ...), custom_call_target="tpu_custom_call" | custom-call | bytes 200000000 | tf_op jit(solution)/shard_map/start_gather/pallas_call | solution.py:558
  93.6 11.8 %fusion.9.lin_ref = f32[3,1024,512]{2,1,0:T(8,128)} fusion(bf16[3,2048,512]{2,1,0:T(8,128)(2,1)} %get-tuple-element.57, bf16[1024,2048]{1,0:T(8,128)(2,1)} %get-tuple-element.58), kind=kOutput, calls=%fused_computation.28 | convolution fusion | flops 6442450944 | bytes 16777216 | tf_op jit(solution)/shard_map/rd,kdc->krc/dot_general | solution.py:941
  105.4 14.9 %attend_forward.1 = (bf16[3,1024,512]{2,1,0:T(8,128)(2,1)S(1)}, bf16[1024,512]{1,0:T(8,128)(2,1)S(1)}, f32[2,8,1024]{2,1,0:T(8,128)S(1)}) custom-call(f32[3,1024,512]{2,1,0:T(8,128)} %fusion.9.lin_ref, f32[3,512]{1,0:T(4,128)S(1)} %reshape_reshape.6.bias_ref, f32[3,1024,128]{2,1,0:T(8,128)S(1)} %copy-done.14), custom_call_target="tpu_custom_call" | custom-call | flops 4294967296 | bytes 13631488 | tf_op jit(solution)/shard_map/attend_forward/pallas_call | solution.py:129
  122.7 38.0 %square_reduce.2 = f32[256,2048]{1,0:T(8,128)S(1)} custom-call(bf16[1024,2048]{1,0:T(8,128)(2,1)S(1)} %convolution_convert_fusion.2.terms_ref, f32[2,8,1024]{2,1,0:T(8,128)S(1)} %get-tuple-element.62.ready_ref.lse_ref), custom_call_target="tpu_custom_call" | custom-call | bytes 125829120 | tf_op jit(solution)/shard_map/square_reduce/pallas_call | solution.py:357
  162.8 37.6 %square_gather.2 = bf16[1024,2048]{1,0:T(8,128)(2,1)} custom-call(bf16[256,2048]{1,0:T(8,128)(2,1)} %add_convert_fusion.1.block_ref), custom_call_target="tpu_custom_call" | custom-call | bytes 62914560 | tf_op jit(solution)/shard_map/square_gather/pallas_call | solution.py:289
  201.1 16.6 %convolution_bitcast_fusion = f32[2,1024,1408]{1,2,0:T(8,128)S(1)} fusion(bf16[2,2048,1408]{2,1,0:T(8,128)(2,1)} %all-gather.3.cloned.1.call-done, bf16[1024,2048]{1,0:T(8,128)(2,1)} %square_gather.2), kind=kOutput, calls=%fused_computation.4 | convolution fusion | flops 11811160064 | bytes 27262976 | tf_op jit(solution)/shard_map/rd,kdc->krc/dot_general | solution.py:947
  224.7 8.0 %convolution_convert_fusion = bf16[1408,2048]{1,0:T(8,128)(2,1)} fusion(bf16[1024,1408]{0,1:T(8,128)(2,1)S(1)} %multiply_convert_fusion.2, bf16[1024,2048]{1,0:T(8,128)(2,1)S(1)} %copy-done.43), kind=kOutput, calls=%fused_computation.3 | convolution fusion | flops 5908463616 | bytes 12845056 | tf_op jit(solution)/shard_map/dot_general | solution.py:84
  232.8 29.0 %all-gather.5.cloned.1.call-done = bf16[1408,2048]{1,0:T(8,128)(2,1)} async-done(((bf16[1408,256]{1,0:T(8,128)(2,1)}), bf16[1408,2048]{1,0:T(8,128)(2,1)}) %all-gather.5.cloned.1.call-update) | async-done | bytes 5767184 | tf_op jit(solution)/shard_map/all_gather | solution.py:898
  261.8 10.0 %convolution_convert_fusion.1 = bf16[1024,2048]{1,0:T(8,128)(2,1)S(1)} fusion(bf16[1024,1408]{0,1:T(8,128)(2,1)} %copy-done.26, bf16[1408,2048]{1,0:T(8,128)(2,1)} %all-gather.5.cloned.1.call-done), kind=kOutput, calls=%fused_computation.20 | convolution fusion | flops 5907677184 | bytes 12845056 | tf_op jit(solution)/shard_map/dot_general | solution.py:84
  278.5 11.9 %fusion.8 = (bf16[1,1024,1408]{1,2,0:T(8,128)(2,1)S(1)}, bf16[1,1024,1408]{1,2,0:T(8,128)(2,1)}) fusion(f32[2,1024,1408]{1,2,0:T(8,128)} %copy-done.21, bf16[1024,2048]{1,0:T(8,128)(2,1)S(1)} %copy-done.44, bf16[1408,2048]{1,0:T(8,128)(2,1)S(1)} %copy-done.41), kind=kOutput, calls=%fused_computation.27 | convolution fusion | flops 5924323328 | bytes 27262976 | tf_op jit(solution)/shard_map/dot_general | solution.py:84
  292.0 17.9 %bitcast_convert_fusion.1.terms_ref = bf16[1024,2048]{1,0:T(8,128)(2,1)} fusion(bf16[2,2048,1408]{2,1,0:T(8,128)(2,1)} %all-gather.3.cloned.1.call-done, bf16[1,1024,1408]{1,2,0:T(8,128)(2,1)} %get-tuple-element.120, bf16[1,1024,1408]{1,2,0:T(8,128)(2,1)S(1)} %get-tuple-element.119), kind=kOutput, calls=%fused_computation.2 | convolution fusion | flops 11816140800 | bytes 21495808 | tf_op jit(solution)/shard_map/krc,kdc->rd/dot_general | solution.py:965
  309.9 17.3 %convert_bitcast_fusion = bf16[2,2048,1408]{2,1,0:T(8,128)(2,1)} fusion(bf16[1024,2048]{1,0:T(8,128)(2,1)S(1)} %copy-done.24, bf16[1,1024,1408]{1,2,0:T(8,128)(2,1)} %get-tuple-element.120, bf16[1,1024,1408]{1,2,0:T(8,128)(2,1)} %copy-done.46), kind=kOutput, calls=%fused_computation | convolution fusion | flops 11819810816 | bytes 21495808 | tf_op jit(solution)/shard_map/rd,krc->kdc/dot_general | solution.py:963
  333.4 37.0 %square_reduce.3 = f32[256,2048]{1,0:T(8,128)S(1)} custom-call(bf16[1024,2048]{1,0:T(8,128)(2,1)S(1)} %copy-done, bf16[16,128]{1,0:T(8,128)(2,1)S(1)} %slice.50.ready_ref), custom_call_target="tpu_custom_call" | custom-call | bytes 125829120 | tf_op jit(solution)/shard_map/square_reduce/pallas_call | solution.py:357
  375.1 36.4 %square_gather.3 = bf16[1024,2048]{1,0:T(8,128)(2,1)} custom-call(bf16[256,2048]{1,0:T(8,128)(2,1)} %get-tuple-element.115.block_ref), custom_call_target="tpu_custom_call" | custom-call | bytes 62914560 | tf_op jit(solution)/shard_map/square_gather/pallas_call | solution.py:289
  411.6 5.5 convolution_convert_fusion.4.grad_ref
  417.1 23.3 %attend_backward.1 = (bf16[3,1024,512]{2,1,0:T(8,128)(2,1)S(1)}, f32[1,3,512]{2,1,0:T(4,128)S(1)}) custom-call(bf16[3,1024,512]{2,1,0:T(8,128)(2,1)} %copy-done.17, bf16[1024,512]{1,0:T(8,128)(2,1)S(1)} %convolution_convert_fusion.4.grad_ref, f32[2,8,1024]{2,1,0:T(8,128)S(1)} %copy-done.13, f32[3,1024,128]{2,1,0:T(8,128)S(1)} %copy-done.15), custom_call_target="tpu_custom_call" | custom-call | flops 10737418240 | bytes 13631488 | tf_op jit(solution)/shard_map/attend_backward/pallas_call | solution.py:206
  442.1 8.9 %convert_bitcast_fusion.1 = bf16[3,2048,512]{2,1,0:T(8,128)(2,1)} fusion(bf16[3,1024,512]{2,1,0:T(8,128)(2,1)S(1)} %get-tuple-element.72, bf16[1024,2048]{1,0:T(8,128)(2,1)S(1)} %copy-done.42), kind=kOutput, calls=%fused_computation.5 | convolution fusion | flops 6445596672 | bytes 13631488 | tf_op jit(solution)/shard_map/rd,krc->kdc/dot_general | solution.py:980
  451.0 5.0 convolution_convert_fusion.3.proj_ref
  456.1 9.0 %bitcast_convert_fusion.first_ref = bf16[1024,2048]{1,0:T(8,128)(2,1)S(1)} fusion(bf16[3,1024,512]{2,1,0:T(8,128)(2,1)S(1)} %copy-done.19, bf16[3,2048,512]{2,1,0:T(8,128)(2,1)} %get-tuple-element.57), kind=kOutput, calls=%fused_computation.1 | convolution fusion | flops 6444548096 | bytes 13631488 | tf_op jit(solution)/shard_map/krc,kdc->rd/dot_general | solution.py:982
  465.1 47.6 %last_reduce.1 = (f32[256,2048]{1,0:T(8,128)S(1)}, f32[512,256]{1,0:T(8,128)S(1)}, f32[4,2048]{1,0:T(4,128)S(1)}, f32[8,256]{1,0:T(8,128)S(1)}) custom-call(bf16[1024,2048]{1,0:T(8,128)(2,1)S(1)} %bitcast_convert_fusion.first_ref, bf16[512,2048]{1,0:T(8,128)(2,1)S(1)} %convolution_convert_fusion.3.proj_ref, f32[256,2048]{1,0:T(8,128)S(1)} %copy-done.7, ...), custom_call_target="tpu_custom_call" | custom-call | bytes 120000000 | tf_op jit(solution)/shard_map/last_reduce/pallas_call | solution.py:791
  518.5 4.9 multiply_subtract_fusion.2
  525.1 4.9 multiply_subtract_fusion
  530.0 7.8 %reduce-scatter.8.cloned.1.call-done = bf16[3,256,512]{2,1,0:T(8,128)(2,1)} async-done(((bf16[3,2048,512]{2,1,0:T(8,128)(2,1)}), bf16[3,256,512]{2,1,0:T(8,128)(2,1)}) %reduce-scatter.8.cloned.1.call-update) | async-done | bytes 786448 | tf_op jit(solution)/shard_map/reduce_scatter | solution.py:902
  537.8 5.8 %multiply_subtract_fusion.1 = (f32[3,256,512]{2,1,0:T(8,128)}, f32[3,256,512]{2,1,0:T(8,128)}, f32[3,256,512]{2,1,0:T(8,128)}, f32[3,256,512]{2,1,0:T(8,128)}) fusion(f32[3,256,512]{2,1,0:T(8,128)} %wq_wide.1, f32[3,256,512]{2,1,0:T(8,128)} %param.36, f32[3,256,512]{2,1,0:T(8,128)} %param.43, bf16[3,256,512]{2,1,0:T(8,128)(2,1)} %reduce-scatter.8.cloned.1.call-done), kind=kLoop, calls=%fused_computation.41 | loop fusion | flops 6291456 | bytes 11796480 | tf_op jit(solution)/shard_map/sub | solution.py:47
  (146 shorter events, 47.8 us)
Async XLA Ops:
  7.2 193.8 %all-gather.3.cloned.1.call-start = ((), (), s32[]{:S(2)}) async-start(), calls=%async_computation.3 | async-start | bytes 12976128 | tf_op jit(solution)/shard_map/all_gather | solution.py:898
  8.9 84.3 %copy-start.10 = (f32[1,2048]{1,0:T(1,128)}, f32[1,2048]{1,0:T(1,128)S(1)}, u32[]{:S(2)}) copy-start(f32[1,2048]{1,0:T(1,128)S(1)} %get-tuple-element.129.gain_ref) | copy-start | bytes 24580
  93.2 168.6 %all-gather.5.cloned.1.call-start = ((), (), s32[]{:S(2)}) async-start(), calls=%async_computation.4 | async-start | bytes 6488064 | tf_op jit(solution)/shard_map/all_gather | solution.py:898
  93.5 11.8 %copy-start.14 = (f32[3,1024,128]{2,1,0:T(8,128)S(1)}, f32[3,1024,128]{2,1,0:T(8,128)}, u32[]{:S(2)}) copy-start(f32[3,1024,128]{2,1,0:T(8,128)} %constant.51.clone.table_ref) | copy-start | bytes 4718596
  105.4 15.0 %copy-start.45 = (bf16[512,2048]{1,0:T(8,128)(2,1)S(1)}, bf16[512,2048]{1,0:T(8,128)(2,1)}, u32[]{:S(2)}) copy-start(bf16[512,2048]{1,0:T(8,128)(2,1)} %get-tuple-element.61) | copy-start | bytes 6291460
  122.7 38.0 %copy-start.4 = (bf16[256,2048]{1,0:T(8,128)(2,1)S(1)}, bf16[256,2048]{1,0:T(8,128)(2,1)}, u32[]{:S(2)}) copy-start(bf16[256,2048]{1,0:T(8,128)(2,1)} %x_ref.1) | copy-start | bytes 3145732
  161.0 209.4 %copy-start.20 = (f32[256,2048]{1,0:T(8,128)}, f32[256,2048]{1,0:T(8,128)S(1)}, u32[]{:S(2)}) copy-start(f32[256,2048]{1,0:T(8,128)S(1)} %get-tuple-element.118) | copy-start | bytes 6291460
  201.1 129.2 %reduce-scatter.4.cloned.1.call-start = ((), (), s32[]{:S(2)}) async-start(), calls=%async_computation.5 | async-start | bytes 6488064 | tf_op jit(solution)/shard_map/reduce_scatter | solution.py:902
  217.7 7.0 %copy-start.43 = (bf16[1024,2048]{1,0:T(8,128)(2,1)S(1)}, bf16[1024,2048]{1,0:T(8,128)(2,1)}, u32[]{:S(2)}) copy-start(bf16[1024,2048]{1,0:T(8,128)(2,1)} %get-tuple-element.67) | copy-start | bytes 12582916
  232.7 218.2 %reduce-scatter.6.cloned.1.call-start = ((), (), s32[]{:S(2)}) async-start(), calls=%async_computation.6 | async-start | bytes 12976128 | tf_op jit(solution)/shard_map/reduce_scatter | solution.py:902
  261.8 16.7 %copy-start.44 = (bf16[1024,2048]{1,0:T(8,128)(2,1)S(1)}, bf16[1024,2048]{1,0:T(8,128)(2,1)}, u32[]{:S(2)}) copy-start(bf16[1024,2048]{1,0:T(8,128)(2,1)} %get-tuple-element.67) | copy-start | bytes 12582916
  275.0 52.3 %collective-permute-start = (bf16[256,2048]{1,0:T(8,128)(2,1)}, bf16[256,2048]{1,0:T(8,128)(2,1)}, u32[]{:S(2)}, u32[]{:S(2)}) collective-permute-start(bf16[256,2048]{1,0:T(8,128)(2,1)} %get-tuple-element.121), channel_id=1, source_target_pairs={{0,3},{1,2},{2,1},{3,0},{4,7},{5,6},{6,5},{7,4},{8,11},{9,10},{10,... | collective-permute-start | bytes 3145736 | tf_op jit(solution)/shard_map/ppermute | solution.py:882
  277.4 49.9 %collective-permute-start.2 = (bf16[256,2048]{1,0:T(8,128)(2,1)}, bf16[256,2048]{1,0:T(8,128)(2,1)}, u32[]{:S(2)}, u32[]{:S(2)}) collective-permute-start(bf16[256,2048]{1,0:T(8,128)(2,1)} %get-tuple-element.122), channel_id=1, source_target_pairs={{0,2},{1,3},{2,0},{3,1},{4,6},{5,7},{6,4},{7,5},{8,10},{9,11},{10,... | collective-permute-start | bytes 3145736 | tf_op jit(solution)/shard_map/ppermute | solution.py:882
  277.9 49.4 %collective-permute-start.1 = (bf16[256,2048]{1,0:T(8,128)(2,1)S(1)}, bf16[256,2048]{1,0:T(8,128)(2,1)}, u32[]{:S(2)}, u32[]{:S(2)}) collective-permute-start(bf16[256,2048]{1,0:T(8,128)(2,1)S(1)} %get-tuple-element.123), channel_id=1, source_target_pairs={{0,1},{1,0},{2,3},{3,2},{4,5},{5,4},{6,7},{7,6},{8,9},{9,8},{10,11... | collective-permute-start | bytes 3145736 | tf_op jit(solution)/shard_map/ppermute | solution.py:882
  292.0 17.9 %copy-start.24 = (bf16[1024,2048]{1,0:T(8,128)(2,1)S(1)}, bf16[1024,2048]{1,0:T(8,128)(2,1)}, u32[]{:S(2)}) copy-start(bf16[1024,2048]{1,0:T(8,128)(2,1)} %square_gather.2) | copy-start | bytes 12582916
  330.3 207.5 %reduce-scatter.8.cloned.1.call-start = ((), (), s32[]{:S(2)}) async-start(), calls=%async_computation.7 | async-start | bytes 7077888 | tf_op jit(solution)/shard_map/reduce_scatter | solution.py:902
  417.1 24.9 %copy-start.42 = (bf16[1024,2048]{1,0:T(8,128)(2,1)S(1)}, bf16[1024,2048]{1,0:T(8,128)(2,1)}, u32[]{:S(2)}) copy-start(bf16[1024,2048]{1,0:T(8,128)(2,1)} %get-tuple-element.58) | copy-start | bytes 12582916
  456.1 9.0 %copy-start.7 = (f32[256,2048]{1,0:T(8,128)S(1)}, f32[256,2048]{1,0:T(8,128)}, u32[]{:S(2)}) copy-start(f32[256,2048]{1,0:T(8,128)} %get-tuple-element.73.normed_ref) | copy-start | bytes 6291460
  456.1 9.0 %copy-start.11 = (f32[1,2048]{1,0:T(1,128)S(1)}, f32[1,2048]{1,0:T(1,128)}, u32[]{:S(2)}) copy-start(f32[1,2048]{1,0:T(1,128)} %copy-done.10) | copy-start | bytes 24580
  465.1 49.1 %copy-start.34 = (f32[3,8,8]{2,1,0:T(8,128)S(1)}, f32[3,8,8]{2,1,0:T(8,128)}, u32[]{:S(2)}) copy-start(f32[3,8,8]{2,1,0:T(8,128)} %param.30) | copy-start | bytes 2308
  465.1 49.0 %copy-start.39 = (f32[3,8,8]{2,1,0:T(8,128)S(1)}, f32[3,8,8]{2,1,0:T(8,128)}, u32[]{:S(2)}) copy-start(f32[3,8,8]{2,1,0:T(8,128)} %param.37) | copy-start | bytes 2308
  465.1 49.0 %copy-start.40 = (f32[3,8,8]{2,1,0:T(8,128)S(1)}, f32[3,8,8]{2,1,0:T(8,128)}, u32[]{:S(2)}) copy-start(f32[3,8,8]{2,1,0:T(8,128)} %param.44) | copy-start | bytes 2308
  465.1 49.7 %copy-start.9 = (f32[512,256]{1,0:T(8,128)S(1)}, f32[512,256]{1,0:T(8,128)}, u32[]{:S(2)}) copy-start(f32[512,256]{1,0:T(8,128)} %wo_wide.1) | copy-start | bytes 1572868
  530.0 13.6 %copy-start.6 = (f32[256,2048]{1,0:T(8,128)S(1)}, f32[256,2048]{1,0:T(8,128)}, u32[]{:S(2)}) copy-start(f32[256,2048]{1,0:T(8,128)} %copy-done.5) | copy-start | bytes 6291460
  (31 other events, 105.7 us)
Sparse Core Ops, SparseCore 0:
  93.3 107.6 all-gather.2
  202.6 59.1 all-gather.4
  264.1 63.0 reduce-scatter.3
  330.5 117.4 reduce-scatter.5
  451.1 86.7 reduce-scatter.7

commit v5 on v4

--- a/solution.py
+++ b/solution.py
@@ -376,9 +376,9 @@
 
 
 def start_kernel(
-    x_ref, gain_ref, shift_ref, dy_ref, bias_ref, wq_wide, wo_wide, gate_wide, down_wide,
+    x_from, gain_ref, shift_ref, dy_from, bias_ref, wq_from, wo_from, gate_from, down_from,
     a_all, dy_all, bias_all, wq_all, wo_all, normed_out, recip_out, gate_out, down_out,
-    a_ref, wq_ref, wo_ref, gate_here, down_here,
+    a_ref, wq_ref, wo_ref, x_ref, dy_ref, wq_wide, wo_wide, gate_wide, down_wide,
     square_send, square_recv, bias_send, bias_recv, line_send, line_recv, core_send, core_recv, local_sem,
 ):
     place, along_x, along_y = partners()
@@ -410,14 +410,13 @@
     def turned(step):
         return 2 * ((chip + step) % 4) + core
 
-    here = [
-        pltpu.make_async_copy(gate_wide, gate_here, local_sem.at[6]),
-        pltpu.make_async_copy(down_wide, down_here, local_sem.at[7]),
-    ]
+    moves = (
+        (wq_from, wq_wide), (wo_from, wo_wide), (x_from, x_ref), (dy_from, dy_ref), (gate_from, gate_wide),
+        (down_from, down_wide),
+    )
+    here = [pltpu.make_async_copy(source, target, local_sem.at[6 + i]) for i, (source, target) in enumerate(moves)]
     for copy in here:
         copy.start()
-    wq_ref[...] = wq_wide[...].astype(low)
-    wo_ref[...] = wo_wide[...].astype(low)
     bias_all[me] = bias_ref[...]
 
     barrier = pltpu.get_barrier_semaphore()
@@ -425,6 +424,10 @@
         pl.semaphore_signal(barrier, inc=1, device_id={"dp": (me + step) % 8}, device_id_type=MESH)
     for device in (along_x, along_y):
         pl.semaphore_signal(barrier, inc=1, device_id={"tensor": device}, device_id_type=MESH)
+    here[0].wait()
+    wq_ref[...] = wq_wide[...].astype(low)
+    here[1].wait()
+    wo_ref[...] = wo_wide[...].astype(low)
     pl.semaphore_wait(barrier, 9)
 
     def rows_of(whole, owner, which):
@@ -494,6 +497,7 @@
             line(part, 3, 1).start()
 
     siblings = [to_sibling(part, 0) for part in range(4)]
+    here[2].wait()
     values = x_ref[...].astype(jnp.float32)
     centred = values - jnp.mean(values, -1, keepdims=True)
     recip = lax.rsqrt(jnp.mean(centred * centred, -1, keepdims=True) + norm_eps)
@@ -501,13 +505,14 @@
     normed_out[...] = centred * recip
     a_ref[...] = (normed_out[...] * gain_ref[...] + shift_ref[...]).astype(low)
     a_copies = square_first(a_ref, a_all, 0)
+    here[3].wait()
     locals_ = [
         pltpu.make_async_copy(a_ref, a_all.at[pl.ds(pl.multiple_of(place * rows, rows), rows)], local_sem.at[0]),
         pltpu.make_async_copy(dy_ref, dy_all.at[pl.ds(pl.multiple_of(place * rows, rows), rows)], local_sem.at[1]),
     ] + [pltpu.make_async_copy(own(part), piece(part, me), local_sem.at[2 + part]) for part in range(4)]
     for copy in locals_:
         copy.start()
-    for copy, source, target in zip(here, (gate_here, down_here), (gate_out, down_out)):
+    for copy, source, target in zip(here[4:], (gate_wide, down_wide), (gate_out, down_out)):
         copy.wait()
         target[...] = source[...].astype(low)
     a_copies = square_next(a_all, 0, a_copies)
@@ -568,28 +573,142 @@
             shape(gate.shape, low),
             shape(down.shape, low),
         ),
-        in_specs=[local_] * 7 + [anywhere] * 2,
+        in_specs=[anywhere, local_, local_, anywhere, local_] + [anywhere] * 4,
         out_specs=(anywhere, anywhere, local_, anywhere, anywhere, local_, local_, local_, local_),
         scratch_shapes=[
             pltpu.VMEM((rows, model), low),
             pltpu.VMEM(wq.shape, low),
             pltpu.VMEM(wo.shape, low),
+            pltpu.VMEM(x.shape, low),
+            pltpu.VMEM(dy.shape, low),
+            pltpu.VMEM(wq.shape, wide),
+            pltpu.VMEM(wo.shape, wide),
             pltpu.VMEM(gate.shape, wide),
             pltpu.VMEM(down.shape, wide),
             dma((12,)), dma((12,)), dma((8,)), dma((8,)),
-            dma((4, 4)), dma((4, 4)), dma((4, 4)), dma((4, 4)), dma((8,)),
+            dma((4, 4)), dma((4, 4)), dma((4, 4)), dma((4, 4)), dma((12,)),
         ],
         compiler_params=pltpu.CompilerParams(
-            collective_id=2, has_side_effects=True, vmem_limit_bytes=48 * 1024 * 1024
+            collective_id=2, has_side_effects=True, vmem_limit_bytes=60 * 1024 * 1024
         ),
         cost_estimate=pl.CostEstimate(flops=0, bytes_accessed=200_000_000, transcendentals=0),
         name="start_gather",
     )(x, gain, shift, dy, bias, wq, wo, gate, down)
 
 
+def back_kernel(
+    terms_ref, ready_ref, resid_ref, gain_ref, dy_ref, whole_ref, grad_out, second_out,
+    first_x, first_y, staged, second, normed, low_ref,
+    send_sem, recv_sem, row_send, row_recv, local_sem,
+):
+    del ready_ref
+    me, along_x, along_y = partners()
+    rows = grad_out.shape[0]
+    half = rows // 2
+    corner = 3 - me
+    low, wide = jnp.bfloat16, jnp.float32
+
+    def term(owner, which):
+        return terms_ref.at[pl.ds(pl.multiple_of(owner * rows + which * half, half), half)]
+
+    def part(owner, which):
+        return whole_ref.at[pl.ds(pl.multiple_of(owner * rows + which * half, half), half)]
+
+    def start(source, target_ref, target, sends, receives, index):
+        copy = pltpu.make_async_remote_copy(
+            src_ref=source,
+            dst_ref=target_ref,
+            send_sem=sends.at[index],
+            recv_sem=receives.at[index],
+            device_id={"tensor": target},
+            device_id_type=MESH,
+        )
+        copy.start()
+        return copy
+
+    greet((along_x, along_y))
+    x_on = start(term(corner, 0), first_x.at[1], along_x, send_sem, recv_sem, 0)
+    y_on = start(term(corner, 1), first_y.at[1], along_y, send_sem, recv_sem, 1)
+    x_own = start(term(along_x, 0), first_x.at[0], along_x, send_sem, recv_sem, 2)
+    y_own = start(term(along_y, 1), first_y.at[0], along_y, send_sem, recv_sem, 3)
+    resid = resid_ref[...]
+    centred = resid - jnp.mean(resid, -1, keepdims=True)
+    recip = lax.rsqrt(jnp.mean(centred * centred, -1, keepdims=True) + norm_eps)
+    normed[...] = centred * recip
+    x_on.wait_recv()
+    staged[0] = (term(along_y, 0)[...].astype(wide) + first_x[1].astype(wide)).astype(low)
+    y_last = start(staged.at[0], second.at[0], along_y, send_sem, recv_sem, 4)
+    y_on.wait_recv()
+    staged[1] = (term(along_x, 1)[...].astype(wide) + first_y[1].astype(wide)).astype(low)
+    x_last = start(staged.at[1], second.at[1], along_x, send_sem, recv_sem, 5)
+    gain = gain_ref[...]
+    sums = [jnp.zeros_like(gain), jnp.zeros_like(gain)]
+    for which, own, last, came in ((0, x_own, y_last, first_x), (1, y_own, x_last, first_y)):
+        here = slice(which * half, (which + 1) * half)
+        own.wait_recv()
+        last.wait_recv()
+        grad = term(me, which)[...].astype(wide) + came[0].astype(wide) + second[which].astype(wide)
+        scaled = grad * gain
+        inner = (
+            scaled
+            - jnp.mean(scaled, -1, keepdims=True)
+            - normed[here, :] * jnp.mean(scaled * normed[here, :], -1, keepdims=True)
+        )
+        total = dy_ref[here, :].astype(wide) + recip[here, :] * inner
+        grad_out[here, :] = total
+        low_ref[here, :] = total.astype(low)
+        if which == 0:
+            copies = [start(low_ref.at[pl.ds(0, half)], part(me, 0), along_x, row_send, row_recv, 0)]
+        else:
+            copies += [
+                start(low_ref.at[pl.ds(half, half)], part(me, 1), along_y, row_send, row_recv, 1),
+                start(low_ref.at[pl.ds(half, half)], part(me, 1), along_x, row_send, row_recv, 2),
+                start(low_ref.at[pl.ds(0, half)], part(me, 0), along_y, row_send, row_recv, 3),
+            ]
+        sums[0] += jnp.sum(grad * normed[here, :], 0, keepdims=True)
+        sums[1] += jnp.sum(grad, 0, keepdims=True)
+    mine = pltpu.make_async_copy(low_ref, whole_ref.at[pl.ds(pl.multiple_of(me * rows, rows), rows)], local_sem)
+    mine.start()
+    second_out[0:1, :] = sums[0]
+    second_out[1:2, :] = sums[1]
+    copies[0].wait_recv()
+    copies.append(start(part(along_x, 0), part(along_x, 0), along_y, row_send, row_recv, 4))
+    copies[1].wait_recv()
+    copies.append(start(part(along_y, 1), part(along_y, 1), along_x, row_send, row_recv, 5))
+    for copy in copies[2:]:
+        copy.wait_recv()
+    for copy in [x_on, y_on, x_own, y_own, y_last, x_last] + copies:
+        copy.wait_send()
+    mine.wait()
+
+
+def square_back(terms, ready, resid, gain, dy):
+    dma = pltpu.SemaphoreType.DMA
+    low, wide = jnp.bfloat16, jnp.float32
+    shape, vmem = jax.ShapeDtypeStruct, pltpu.VMEM
+    rows, width = resid.shape
+    anywhere, local_ = pl.BlockSpec(memory_space=pl.ANY), pl.BlockSpec(memory_space=pltpu.VMEM)
+    pair = vmem((2, rows // 2, width), low)
+    return pl.pallas_call(
+        back_kernel,
+        out_shape=(shape((4 * rows, width), low), shape((rows, width), wide), shape((2, width), wide)),
+        in_specs=[local_, anywhere, local_, local_, local_],
+        out_specs=(anywhere, local_, local_),
+        scratch_shapes=[
+            pair, pair, pair, pair, vmem((rows, width), wide), vmem((rows, width), low),
+            dma((6,)), dma((6,)), dma((6,)), dma((6,)), dma,
+        ],
+        compiler_params=pltpu.CompilerParams(
+            collective_id=1, has_side_effects=True, vmem_limit_bytes=32 * 1024 * 1024
+        ),
+        cost_estimate=pl.CostEstimate(flops=0, bytes_accessed=rows * width * 400, transcendentals=0),
+        name="square_back",
+    )(terms, ready, resid, gain, dy)
+
+
 def last_kernel(
-    first_ref, proj_ref, normed_ref, recip_ref, gain_ref, grad_ref, second_ref, bias_ref,
-    input_out, proj_out, vector_out, bias_out,
+    first_ref, proj_ref, normed_ref, recip_ref, gain_ref, second_ref, bias_ref,
+    step_out, proj_out, vector_out, bias_out,
     square_x, square_y, staged, square_last, mine, near,
     corners, vector_mine, vector_came, vector_slots, bias_mine, bias_came, bias_slots,
     square_send, square_recv, vector_send, vector_recv, bias_send, bias_recv, core_send, core_recv, line_send, line_recv,
@@ -600,7 +719,7 @@
     chip, core = me // 2, me % 2
     sibling = me + 1 - 2 * core
     width = proj_out.shape[1]
-    rows = input_out.shape[0]
+    rows = step_out.shape[0]
     half = rows // 2
     low, wide = jnp.bfloat16, jnp.float32
 
@@ -731,7 +850,7 @@
             - jnp.mean(scaled, -1, keepdims=True)
             - normed * jnp.mean(scaled * normed, -1, keepdims=True)
         )
-        input_out[here, :] = grad_ref[here, :] + recip_ref[here, :] * inner
+        step_out[here, :] = recip_ref[here, :] * inner
     corners[place, 0:1, :] = vector_gain
     corners[place, 1:2, :] = second_ref[0:1, :]
     corners[place, 2:3, :] = vector_shift
@@ -781,7 +900,7 @@
         line(3, 3, 3).wait_send()
 
 
-def last_reduce(first, proj, normed, recip, gain, grad, second, bias):
+def last_reduce(first, proj, normed, recip, gain, second, bias):
     dma = pltpu.SemaphoreType.DMA
     low, wide = jnp.bfloat16, jnp.float32
     shape, vmem = jax.ShapeDtypeStruct, pltpu.VMEM
@@ -796,7 +915,7 @@
             shape((4, model), wide),
             shape(bias.shape, wide),
         ),
-        in_specs=[pl.BlockSpec(memory_space=pltpu.VMEM)] * 8,
+        in_specs=[pl.BlockSpec(memory_space=pltpu.VMEM)] * 7,
         out_specs=(pl.BlockSpec(memory_space=pltpu.VMEM),) * 4,
         scratch_shapes=[
             pair, pair, pair, pair, blocks, blocks,
@@ -815,7 +934,7 @@
         ),
         cost_estimate=pl.CostEstimate(flops=0, bytes_accessed=120_000_000, transcendentals=0),
         name="last_reduce",
-    )(first, proj, normed, recip, gain, grad, second, bias)
+    )(first, proj, normed, recip, gain, second, bias)
 
 
 def after(late, early):
@@ -844,13 +963,21 @@
             down.astype(low),
         )
 
-    reduce_beside = reduce_rows
-
-    def finish(self, first, proj, normed, recip, gain, grad, second, bias):
+    def reduce_beside(self, terms):
+        return (self.reduce_rows(terms, None, 0),)
+
+    def back(self, terms, ready, resid, gain, dy):
+        grad = self.reduce_rows(terms, None, 0)
+        _, normed, recip = layer_norm(resid, gain, gain)
+        total = dy.astype(jnp.float32) + norm_back(grad, normed, recip, gain)
+        sums = jnp.stack([jnp.sum(grad * normed, 0), jnp.sum(grad, 0)])
+        return self.gather_rows(total.astype(jnp.bfloat16)), total, sums
+
+    def finish(self, first, proj, normed, recip, gain, second, bias):
         first = self.reduce_rows(first, None, 0)
         vectors = jnp.stack([jnp.sum(first * normed, 0), second[0], jnp.sum(first, 0), second[1]])
-        input_grad = grad + norm_back(first, normed, recip, gain)
-        return input_grad, scatter_dp(proj, 1), lax.psum(vectors, ("dp", "tensor")), lax.psum(bias, "dp")
+        step = norm_back(first, normed, recip, gain)
+        return step, scatter_dp(proj, 1), lax.psum(vectors, ("dp", "tensor")), lax.psum(bias, "dp")
 
 
 class Line(Plain):
@@ -873,21 +1000,22 @@
         width = -(-values.shape[0] // 1024) * 1024
         return jnp.pad(values, (0, width - values.shape[0])).reshape(8, -1)
 
-    def reduce_beside(self, terms, ready, name):
+    def reduce_beside(self, terms):
         me = lax.axis_index("tensor")
         rows = terms.shape[0] // 4
         parts = [lax.dynamic_slice_in_dim(terms, (me ^ step) * rows, rows, 0) for step in range(4)]
-        total = parts[0].astype(jnp.float32)
         for step in (3, 1, 2):
-            came = lax.ppermute(parts[step], "tensor", [(i, i ^ step) for i in range(4)])
-            total = total + came.astype(jnp.float32)
-        return total
-
-    def finish(self, first, proj, normed, recip, gain, grad, second, bias):
-        input_grad, proj_grad, vectors, total = last_reduce(
-            first, proj, normed, recip, gain.reshape(1, -1), grad, second, self.flat(bias)
-        )
-        return input_grad, proj_grad, vectors, total.reshape(-1)[: bias.size].reshape(bias.shape)
+            parts[step] = lax.ppermute(parts[step], "tensor", [(i, i ^ step) for i in range(4)])
+        return tuple(parts)
+
+    def back(self, terms, ready, resid, gain, dy):
+        return square_back(terms, ready, resid, gain.reshape(1, -1), dy)
+
+    def finish(self, first, proj, normed, recip, gain, second, bias):
+        step, proj_grad, vectors, total = last_reduce(
+            first, proj, normed, recip, gain.reshape(1, -1), second, self.flat(bias)
+        )
+        return step, proj_grad, vectors, total.reshape(-1)[: bias.size].reshape(bias.shape)
 
 
 def row_major(values):
@@ -941,7 +1069,7 @@
     lin = jnp.einsum("rd,kdc->krc", a_all, w_qkv, preferred_element_type=jnp.float32)
     qkv, heads, logs = attention_forward(lin, bias_all, head_size)
     resid = xin + routes.reduce_rows(mxu(heads, w_output, NN).astype(low), logs, 4)
-    second_out, second_normed, second_recip = layer_norm(resid, gains[1], shifts[1])
+    second_out, _, _ = layer_norm(resid, gains[1], shifts[1])
     m_all = routes.gather_rows(second_out.astype(low))
     w_down = gather_dp(after(down_low, (w_gate_up, m_all)), 1)
     gate_vals = jnp.einsum("rd,kdc->krc", m_all, w_gate_up, preferred_element_type=jnp.float32)
@@ -953,7 +1081,7 @@
     down_grad = scatter_dp(down_terms, 1)
     w_down = after(w_down, down_terms)
     block_terms = mxu(hidden, w_down, NN).astype(low)
-    down_sum = routes.reduce_beside(block_terms, None, 6)
+    down_parts = routes.reduce_beside(block_terms)
     hidden_grad = mxu(dy_all, after(w_down, block_terms), NT)
     gate_grad_low = (
         hidden_grad * upward * sigmoid_gate * (1.0 + gate_lin * (1.0 - sigmoid_gate))
@@ -965,15 +1093,10 @@
     second_terms = jnp.einsum(
         "krc,kdc->rd", both_grads, w_gate_up, preferred_element_type=jnp.float32
     ).astype(low)
-    block_out = (resid + down_sum).astype(low)
-    gate_grad = scatter_dp(after(gate_terms, (down_grad, second_terms, block_out)), 1)
-    second_grad = routes.reduce_rows(after(second_terms, down_grad), block_out[:16, :128], 5)
-    resid_grad = cotangent.astype(jnp.float32) + norm_back(
-        second_grad, second_normed, second_recip, gains[1]
+    gate_grad = scatter_dp(after(gate_terms, (down_grad, second_terms, down_parts)), 1)
+    resid_full, resid_grad, second_sums = routes.back(
+        after(second_terms, down_grad), down_grad[:16, :128], resid, gains[1], cotangent
     )
-    gain_second = jnp.sum(second_grad * second_normed, 0)
-    shift_second = jnp.sum(second_grad, 0)
-    resid_full = routes.gather_rows(resid_grad.astype(low))
     out_terms = mxu(heads, resid_full, TN).astype(low)
     heads_grad = mxu(resid_full, w_output, NT).astype(low)
     lin_grads, bias_terms = attention_backward(qkv, heads_grad, logs, head_size)
@@ -983,16 +1106,20 @@
         "krc,kdc->rd", lin_grads, w_qkv, preferred_element_type=jnp.float32
     ).astype(low)
     qkv_grad = scatter_dp(after(qkv_terms, gate_grad), 1)
-    input_grad, out_grad, vectors, bias_sum = routes.finish(
+    input_step, out_grad, vectors, bias_sum = routes.finish(
         first_terms,
         out_terms,
         first_normed,
         first_recip,
         gains[0],
-        resid_grad,
-        jnp.stack([gain_second, shift_second]),
+        second_sums,
         bias_terms,
     )
+    input_grad = resid_grad + input_step
+    block_out = resid
+    for part in after(down_parts, vectors):
+        block_out = block_out + part.astype(jnp.float32)
+    block_out = block_out.astype(low)
     gains_grad, shifts_grad = vectors[:2], vectors[2:]
     down_grad, gate_grad, out_grad = (
         grad.astype(jnp.float32) for grad in (*after((down_grad, gate_grad), vectors), out_grad)

time: 561 us -> 555 us (0.989)
    pallas_call x0 -> x1, Pallas kernels: none -> 72.4 us  [square_back(): pl.pallas_call(back_kernel, out_shape=(shape((4 * rows, width), low), sha...]
    pallas_call x2 -> x1, Pallas kernels: 74.9 us -> 38 us  [square_reduce(): pl.pallas_call(reduce_kernel, out_shape=jax.ShapeDtypeStruct((rows, width...]
    pallas_call x2 -> x1, Pallas kernels: 74 us -> 37.5 us  [square_gather(): pl.pallas_call(gather_kernel, out_shape=jax.ShapeDtypeStruct((4 * rows, w...]
    unnamed x97 -> x96, local copies, waits for them, and re-layouts: 21.8 us -> 15.9 us
  transfers between devices with their start and end apart: 8 -> 8, of which waited for: 3 -> 4; matrix products, arithmetic and copies ran while one was open for 27% -> 28% of each run, Pallas kernels for 42% -> 43%
where the time goes in v5:
time: 555 us; the launch traced here: 547 us
  Pallas kernels  314 us (57%)
  matrix products  122 us (22%)
  waiting for transfers between devices  39.7 us (7%)
  other arithmetic  31.4 us (6%)
  local copies, waits for them, and re-layouts  20.7 us (4%)
  between operations  14.9 us (3%)
    pallas_call x1, Pallas kernels, start_gather(): pl.pallas_call(start_kernel, out_shape=(shape((4 * rows, model), low), sh...  80.1 us
    pallas_call x1, Pallas kernels, square_back(): pl.pallas_call(back_kernel, out_shape=(shape((4 * rows, width), low), sha...  72.4 us
    pallas_call x1, Pallas kernels, last_reduce(): pl.pallas_call(last_kernel, out_shape=(shape((rows, model), wide), shape(...  48.2 us
    dot_general x6, matrix products, mxu(): lax.dot_general(left, right, dims, preferred_element_type=jnp.float32)  39.8 us
    pallas_call x1, Pallas kernels, square_reduce(): pl.pallas_call(reduce_kernel, out_shape=jax.ShapeDtypeStruct((rows, width...  38 us
    pallas_call x1, Pallas kernels, square_gather(): pl.pallas_call(gather_kernel, out_shape=jax.ShapeDtypeStruct((4 * rows, w...  37.5 us
    all_gather x2, waiting for transfers between devices, gather_dp(): lax.all_gather(block.astype(jnp.bfloat16), 'dp', axis=axis, tiled=True)  28.8 us
    pallas_call x1, Pallas kernels, attention_backward(): pl.pallas_call(functools.partial(backward_kernel, head_size), grid=(rows...  23.3 us
  transfers between devices with their start and end apart: 8, of which 4 were waited for; matrix products, arithmetic and copies ran while one was open for 28% of the time, Pallas kernels for 43%

profile of v5, /device:TPU:0, one launch (start us, length us, event | category | flops | bytes accessed | tf_op | source)
XLA Modules:
  0.0 546.9 jit_solution(11138887758072729280)
XLA Ops:
  10.1 80.1 %start_gather.1 = (bf16[1024,2048]{1,0:T(8,128)(2,1)}, bf16[1024,2048]{1,0:T(8,128)(2,1)}, f32[8,8,128]{2,1,0:T(8,128)}, bf16[3,2048,512]{2,1,0:T(8,128)(2,1)}, ...) custom-call(bf16[256,2048]{1,0:T(8,128)(2,1)} %x_from.1, ...), custom_call_target="tpu_custom_call" | custom-call | bytes 200000000 | tf_op jit(solution)/shard_map/start_gather/pallas_call | solution.py:563
  91.2 11.8 %fusion.9.lin_ref = f32[3,1024,512]{2,1,0:T(8,128)} fusion(bf16[3,2048,512]{2,1,0:T(8,128)(2,1)} %get-tuple-element.64, bf16[1024,2048]{1,0:T(8,128)(2,1)} %get-tuple-element.65), kind=kOutput, calls=%fused_computation.28 | convolution fusion | flops 6442450944 | bytes 16777216 | tf_op jit(solution)/shard_map/rd,kdc->krc/dot_general | solution.py:1069
  103.1 14.9 %attend_forward.1 = (bf16[3,1024,512]{2,1,0:T(8,128)(2,1)S(1)}, bf16[1024,512]{1,0:T(8,128)(2,1)S(1)}, f32[2,8,1024]{2,1,0:T(8,128)S(1)}) custom-call(f32[3,1024,512]{2,1,0:T(8,128)} %fusion.9.lin_ref, f32[3,512]{1,0:T(4,128)S(1)} %reshape_reshape.6.bias_ref, f32[3,1024,128]{2,1,0:T(8,128)S(1)} %copy-done.8), custom_call_target="tpu_custom_call" | custom-call | flops 4294967296 | bytes 13631488 | tf_op jit(solution)/shard_map/attend_forward/pallas_call | solution.py:129
  120.4 38.0 %square_reduce.1 = f32[256,2048]{1,0:T(8,128)S(1)} custom-call(bf16[1024,2048]{1,0:T(8,128)(2,1)S(1)} %convolution_convert_fusion.2.terms_ref, f32[2,8,1024]{2,1,0:T(8,128)S(1)} %get-tuple-element.69.ready_ref.lse_ref), custom_call_target="tpu_custom_call" | custom-call | bytes 125829120 | tf_op jit(solution)/shard_map/square_reduce/pallas_call | solution.py:357
  160.6 37.5 %square_gather.1 = bf16[1024,2048]{1,0:T(8,128)(2,1)} custom-call(bf16[256,2048]{1,0:T(8,128)(2,1)} %add_convert_fusion.1.block_ref), custom_call_target="tpu_custom_call" | custom-call | bytes 62914560 | tf_op jit(solution)/shard_map/square_gather/pallas_call | solution.py:289
  198.2 16.6 %convolution_bitcast_fusion = f32[2,1024,1408]{1,2,0:T(8,128)S(1)} fusion(bf16[2,2048,1408]{2,1,0:T(8,128)(2,1)} %all-gather.3.cloned.1.call-done, bf16[1024,2048]{1,0:T(8,128)(2,1)} %square_gather.1), kind=kOutput, calls=%fused_computation.4 | convolution fusion | flops 11811160064 | bytes 27262976 | tf_op jit(solution)/shard_map/rd,kdc->krc/dot_general | solution.py:1075
  216.7 3.5 copy-done.14
  221.8 8.1 %convolution_convert_fusion = bf16[1408,2048]{1,0:T(8,128)(2,1)} fusion(bf16[1024,1408]{0,1:T(8,128)(2,1)S(1)} %multiply_convert_fusion.2, bf16[1024,2048]{1,0:T(8,128)(2,1)S(1)} %copy-done.42), kind=kOutput, calls=%fused_computation.3 | convolution fusion | flops 5908463616 | bytes 12845056 | tf_op jit(solution)/shard_map/dot_general | solution.py:84
  229.9 28.8 %all-gather.5.cloned.1.call-done = bf16[1408,2048]{1,0:T(8,128)(2,1)} async-done(((bf16[1408,256]{1,0:T(8,128)(2,1)}), bf16[1408,2048]{1,0:T(8,128)(2,1)}) %all-gather.5.cloned.1.call-update) | async-done | bytes 5767184 | tf_op jit(solution)/shard_map/all_gather | solution.py:1026
  258.7 10.0 %convolution_convert_fusion.1 = bf16[1024,2048]{1,0:T(8,128)(2,1)S(1)} fusion(bf16[1024,1408]{0,1:T(8,128)(2,1)} %copy-done.21, bf16[1408,2048]{1,0:T(8,128)(2,1)} %all-gather.5.cloned.1.call-done), kind=kOutput, calls=%fused_computation.20 | convolution fusion | flops 5907677184 | bytes 12845056 | tf_op jit(solution)/shard_map/dot_general | solution.py:84
  274.5 12.0 %fusion.8 = (bf16[1,1024,1408]{1,2,0:T(8,128)(2,1)S(1)}, bf16[1,1024,1408]{1,2,0:T(8,128)(2,1)}) fusion(f32[2,1024,1408]{1,2,0:T(8,128)} %copy-done.14, bf16[1024,2048]{1,0:T(8,128)(2,1)S(1)} %copy-done.43, bf16[1408,2048]{1,0:T(8,128)(2,1)S(1)} %copy-done.40), kind=kOutput, calls=%fused_computation.27 | convolution fusion | flops 5924323328 | bytes 27262976 | tf_op jit(solution)/shard_map/dot_general | solution.py:84
  288.1 18.0 %bitcast_convert_fusion.1.terms_ref = bf16[1024,2048]{1,0:T(8,128)(2,1)} fusion(bf16[2,2048,1408]{2,1,0:T(8,128)(2,1)} %all-gather.3.cloned.1.call-done, bf16[1,1024,1408]{1,2,0:T(8,128)(2,1)} %get-tuple-element.128, bf16[1,1024,1408]{1,2,0:T(8,128)(2,1)S(1)} %get-tuple-element.127), kind=kOutput, calls=%fused_computation.2 | convolution fusion | flops 11816140800 | bytes 21495808 | tf_op jit(solution)/shard_map/krc,kdc->rd/dot_general | solution.py:1093
  306.0 17.3 %convert_bitcast_fusion = bf16[2,2048,1408]{2,1,0:T(8,128)(2,1)} fusion(bf16[1024,2048]{1,0:T(8,128)(2,1)S(1)} %copy-done.19, bf16[1,1024,1408]{1,2,0:T(8,128)(2,1)} %get-tuple-element.128, bf16[1,1024,1408]{1,2,0:T(8,128)(2,1)} %copy-done.46), kind=kOutput, calls=%fused_computation | convolution fusion | flops 11819810816 | bytes 21495808 | tf_op jit(solution)/shard_map/rd,krc->kdc/dot_general | solution.py:1091
  327.8 72.4 %square_back.1 = (bf16[1024,2048]{1,0:T(8,128)(2,1)S(1)}, f32[256,2048]{1,0:T(8,128)S(1)}, f32[2,2048]{1,0:T(2,128)S(1)}) custom-call(bf16[1024,2048]{1,0:T(8,128)(2,1)S(1)} %copy-done, bf16[16,128]{1,0:T(8,128)(2,1)S(1)} %slice.50.ready_ref, f32[256,2048]{1,0:T(8,128)S(1)} %get-tuple-element.126.resid_ref, f32[1,2048]{1,0:T(1,128)S(1)} %get-tuple-element.137.gain_ref, ...), custom_call_target="tpu_custom_call" | custom-call | bytes 209715200 | tf_op jit(solution)/shard_map/square_back/pallas_call | solution.py:692
  402.9 23.3 %attend_backward.1 = (bf16[3,1024,512]{2,1,0:T(8,128)(2,1)S(1)}, f32[1,3,512]{2,1,0:T(4,128)S(1)}) custom-call(bf16[3,1024,512]{2,1,0:T(8,128)(2,1)} %copy-done.11, bf16[1024,512]{1,0:T(8,128)(2,1)S(1)} %convolution_convert_fusion.4.grad_ref, f32[2,8,1024]{2,1,0:T(8,128)S(1)} %get-tuple-element.69.ready_ref.lse_ref, f32[3,1024,128]{2,1,0:T(8,128)S(1)} %copy-done.9), custom_call_target="tpu_custom_call" | custom-call | flops 10737418240 | bytes 13631488 | tf_op jit(solution)/shard_map/attend_backward/pallas_call | solution.py:206
  427.8 8.9 %convert_bitcast_fusion.1 = bf16[3,2048,512]{2,1,0:T(8,128)(2,1)} fusion(bf16[3,1024,512]{2,1,0:T(8,128)(2,1)S(1)} %get-tuple-element.80, bf16[1024,2048]{1,0:T(8,128)(2,1)S(1)} %copy-done.41), kind=kOutput, calls=%fused_computation.5 | convolution fusion | flops 6445596672 | bytes 13631488 | tf_op jit(solution)/shard_map/rd,krc->kdc/dot_general | solution.py:1103
  436.7 7.3 %reduce-scatter.6.cloned.1.call-done = bf16[2,256,1408]{2,1,0:T(8,128)(2,1)} async-done(((bf16[2,2048,1408]{2,1,0:T(8,128)(2,1)}), bf16[2,256,1408]{2,1,0:T(8,128)(2,1)}) %reduce-scatter.6.cloned.1.call-update) | async-done | bytes 1441808 | tf_op jit(solution)/shard_map/reduce_scatter | solution.py:1030
  444.0 5.0 convolution_convert_fusion.3.proj_ref
  449.1 9.5 %bitcast_convert_fusion.first_ref = bf16[1024,2048]{1,0:T(8,128)(2,1)S(1)} fusion(bf16[3,1024,512]{2,1,0:T(8,128)(2,1)S(1)} %copy-done.13, bf16[3,2048,512]{2,1,0:T(8,128)(2,1)} %get-tuple-element.64), kind=kOutput, calls=%fused_computation.1 | convolution fusion | flops 6444548096 | bytes 13631488 | tf_op jit(solution)/shard_map/krc,kdc->rd/dot_general | solution.py:1105
  458.7 48.2 %last_reduce.1 = (f32[256,2048]{1,0:T(8,128)S(1)}, f32[512,256]{1,0:T(8,128)S(1)}, f32[4,2048]{1,0:T(4,128)S(1)}, f32[8,256]{1,0:T(8,128)S(1)}) custom-call(bf16[1024,2048]{1,0:T(8,128)(2,1)S(1)} %bitcast_convert_fusion.first_ref, bf16[512,2048]{1,0:T(8,128)(2,1)S(1)} %convolution_convert_fusion.3.proj_ref, f32[256,2048]{1,0:T(8,128)S(1)} %copy-done.4, ...), custom_call_target="tpu_custom_call" | custom-call | bytes 120000000 | tf_op jit(solution)/shard_map/last_reduce/pallas_call | solution.py:910
  508.3 4.0 add.185
  515.4 3.5 add_convert_fusion
  523.7 7.3 %multiply_subtract_fusion = (f32[2,256,1408]{2,1,0:T(8,128)}, f32[2,256,1408]{2,1,0:T(8,128)}, f32[2,256,1408]{2,1,0:T(8,128)}, f32[2,256,1408]{2,1,0:T(8,128)}) fusion(f32[2,256,1408]{2,1,0:T(8,128)S(1)} %copy-done.15, f32[2,256,1408]{2,1,0:T(8,128)S(1)} %copy-done.22, f32[2,256,1408]{2,1,0:T(8,128)} %param.46, ...), kind=kLoop, calls=%fused_computation.25 | loop fusion | flops 11534336 | bytes 21626880 | tf_op jit(solution)/shard_map/sub | solution.py:47
  533.8 5.3 multiply_subtract_fusion.1
  (140 shorter events, 40.7 us)
Async XLA Ops:
  7.2 190.9 %all-gather.3.cloned.1.call-start = ((), (), s32[]{:S(2)}) async-start(), calls=%async_computation.3 | async-start | bytes 12976128 | tf_op jit(solution)/shard_map/all_gather | solution.py:1026
  90.2 168.5 %all-gather.5.cloned.1.call-start = ((), (), s32[]{:S(2)}) async-start(), calls=%async_computation.4 | async-start | bytes 6488064 | tf_op jit(solution)/shard_map/all_gather | solution.py:1026
  91.2 11.9 %copy-start.8 = (f32[3,1024,128]{2,1,0:T(8,128)S(1)}, f32[3,1024,128]{2,1,0:T(8,128)}, u32[]{:S(2)}) copy-start(f32[3,1024,128]{2,1,0:T(8,128)} %constant.51.clone.table_ref) | copy-start | bytes 4718596
  103.1 14.9 %copy-start.44 = (bf16[512,2048]{1,0:T(8,128)(2,1)S(1)}, bf16[512,2048]{1,0:T(8,128)(2,1)}, u32[]{:S(2)}) copy-start(bf16[512,2048]{1,0:T(8,128)(2,1)} %get-tuple-element.68) | copy-start | bytes 6291460
  120.4 38.1 %copy-start.20 = (bf16[256,2048]{1,0:T(8,128)(2,1)S(1)}, bf16[256,2048]{1,0:T(8,128)(2,1)}, u32[]{:S(2)}) copy-start(bf16[256,2048]{1,0:T(8,128)(2,1)} %x_from.1) | copy-start | bytes 3145732
  198.2 125.9 %reduce-scatter.4.cloned.1.call-start = ((), (), s32[]{:S(2)}) async-start(), calls=%async_computation.5 | async-start | bytes 6488064 | tf_op jit(solution)/shard_map/reduce_scatter | solution.py:1030
  214.8 5.4 copy-start.14
  214.8 7.0 %copy-start.42 = (bf16[1024,2048]{1,0:T(8,128)(2,1)S(1)}, bf16[1024,2048]{1,0:T(8,128)(2,1)}, u32[]{:S(2)}) copy-start(bf16[1024,2048]{1,0:T(8,128)(2,1)} %get-tuple-element.74) | copy-start | bytes 12582916
  229.9 214.1 %reduce-scatter.6.cloned.1.call-start = ((), (), s32[]{:S(2)}) async-start(), calls=%async_computation.6 | async-start | bytes 12976128 | tf_op jit(solution)/shard_map/reduce_scatter | solution.py:1030
  258.7 15.8 %copy-start.43 = (bf16[1024,2048]{1,0:T(8,128)(2,1)S(1)}, bf16[1024,2048]{1,0:T(8,128)(2,1)}, u32[]{:S(2)}) copy-start(bf16[1024,2048]{1,0:T(8,128)(2,1)} %get-tuple-element.74) | copy-start | bytes 12582916
  268.8 5.8 %copy-start.40 = (bf16[1408,2048]{1,0:T(8,128)(2,1)S(1)}, bf16[1408,2048]{1,0:T(8,128)(2,1)}, u32[]{:S(2)}) copy-start(bf16[1408,2048]{1,0:T(8,128)(2,1)} %all-gather.5.cloned.1.call-done) | copy-start | bytes 17301508
  271.0 52.4 %collective-permute-start.2 = (bf16[256,2048]{1,0:T(8,128)(2,1)}, bf16[256,2048]{1,0:T(8,128)(2,1)S(1)}, u32[]{:S(2)}, u32[]{:S(2)}) collective-permute-start(bf16[256,2048]{1,0:T(8,128)(2,1)} %get-tuple-element.129), channel_id=1, source_target_pairs={{0,3},{1,2},{2,1},{3,0},{4,7},{5,6},{6,5},{7,4},{8,11},{9,10},{10,... | collective-permute-start | bytes 3145736 | tf_op jit(solution)/shard_map/ppermute | solution.py:1008
  273.4 50.0 %collective-permute-start.1 = (bf16[256,2048]{1,0:T(8,128)(2,1)}, bf16[256,2048]{1,0:T(8,128)(2,1)}, u32[]{:S(2)}, u32[]{:S(2)}) collective-permute-start(bf16[256,2048]{1,0:T(8,128)(2,1)} %get-tuple-element.130), channel_id=1, source_target_pairs={{0,2},{1,3},{2,0},{3,1},{4,6},{5,7},{6,4},{7,5},{8,10},{9,11},{10,... | collective-permute-start | bytes 3145736 | tf_op jit(solution)/shard_map/ppermute | solution.py:1008
  274.0 49.4 %collective-permute-start = (bf16[256,2048]{1,0:T(8,128)(2,1)}, bf16[256,2048]{1,0:T(8,128)(2,1)}, u32[]{:S(2)}, u32[]{:S(2)}) collective-permute-start(bf16[256,2048]{1,0:T(8,128)(2,1)} %get-tuple-element.131), channel_id=1, source_target_pairs={{0,1},{1,0},{2,3},{3,2},{4,5},{5,4},{6,7},{7,6},{8,9},{9,8},{10,11... | collective-permute-start | bytes 3145736 | tf_op jit(solution)/shard_map/ppermute | solution.py:1008
  288.1 18.0 %copy-start.19 = (bf16[1024,2048]{1,0:T(8,128)(2,1)S(1)}, bf16[1024,2048]{1,0:T(8,128)(2,1)}, u32[]{:S(2)}) copy-start(bf16[1024,2048]{1,0:T(8,128)(2,1)} %square_gather.1) | copy-start | bytes 12582916
  324.4 209.4 %reduce-scatter.8.cloned.1.call-start = ((), (), s32[]{:S(2)}) async-start(), calls=%async_computation.7 | async-start | bytes 7077888 | tf_op jit(solution)/shard_map/reduce_scatter | solution.py:1030
  327.8 72.4 %copy-start.45 = (bf16[512,2048]{1,0:T(8,128)(2,1)S(1)}, bf16[512,2048]{1,0:T(8,128)(2,1)}, u32[]{:S(2)}) copy-start(bf16[512,2048]{1,0:T(8,128)(2,1)} %get-tuple-element.68) | copy-start | bytes 6291460
  402.9 25.0 %copy-start.41 = (bf16[1024,2048]{1,0:T(8,128)(2,1)S(1)}, bf16[1024,2048]{1,0:T(8,128)(2,1)}, u32[]{:S(2)}) copy-start(bf16[1024,2048]{1,0:T(8,128)(2,1)} %get-tuple-element.65) | copy-start | bytes 12582916
  444.0 5.0 copy-start.13
  449.1 9.6 %copy-start.4 = (f32[256,2048]{1,0:T(8,128)S(1)}, f32[256,2048]{1,0:T(8,128)}, u32[]{:S(2)}) copy-start(f32[256,2048]{1,0:T(8,128)} %get-tuple-element.81.normed_ref) | copy-start | bytes 6291460
  449.1 9.6 %copy-start.5 = (f32[256,1]{1,0:T(8,128)S(1)}, f32[256,1]{1,0:T(8,128)}, u32[]{:S(2)}) copy-start(f32[256,1]{1,0:T(8,128)} %get-tuple-element.82.recip_ref) | copy-start | bytes 3076
  449.1 9.6 %copy-start.6 = (f32[1,2048]{1,0:T(1,128)S(1)}, f32[1,2048]{1,0:T(1,128)}, u32[]{:S(2)}) copy-start(f32[1,2048]{1,0:T(1,128)} %get-tuple-element.138.gain_ref) | copy-start | bytes 24580
  508.3 4.9 copy-start.23
  523.7 10.1 %copy-start.16 = (f32[3,256,512]{2,1,0:T(8,128)S(1)}, f32[3,256,512]{2,1,0:T(8,128)}, u32[]{:S(2)}) copy-start(f32[3,256,512]{2,1,0:T(8,128)} %wq_from.1) | copy-start | bytes 4718596
  (31 other events, 86.1 us)
Sparse Core Ops, SparseCore 0:
  90.3 107.6 all-gather.2
  199.5 59.1 all-gather.4
  261.0 63.0 reduce-scatter.3
  326.2 117.6 reduce-scatter.5
  446.1 87.6 reduce-scatter.7

commit v6 on v5

--- a/solution.py
+++ b/solution.py
@@ -417,7 +417,7 @@
     here = [pltpu.make_async_copy(source, target, local_sem.at[6 + i]) for i, (source, target) in enumerate(moves)]
     for copy in here:
         copy.start()
-    bias_all[me] = bias_ref[...]
+    bias_all[me] = bias_ref[...].astype(low).astype(jnp.float32)
 
     barrier = pltpu.get_barrier_semaphore()
     for step in range(1, 8):
@@ -503,7 +503,7 @@
     recip = lax.rsqrt(jnp.mean(centred * centred, -1, keepdims=True) + norm_eps)
     recip_out[...] = recip
     normed_out[...] = centred * recip
-    a_ref[...] = (normed_out[...] * gain_ref[...] + shift_ref[...]).astype(low)
+    a_ref[...] = (normed_out[...] * gain_ref[0:1, :] + shift_ref[0:1, :]).astype(low)
     a_copies = square_first(a_ref, a_all, 0)
     here[3].wait()
     locals_ = [
@@ -553,7 +553,7 @@
         copy.wait()
 
 
-def start_gather(x, gain, shift, dy, bias, wq, wo, gate, down):
+def start_gather(x, gains, shifts, dy, bias, wq, wo, gate, down):
     dma = pltpu.SemaphoreType.DMA
     low, wide = jnp.bfloat16, jnp.float32
     anywhere = pl.BlockSpec(memory_space=pl.ANY)
@@ -593,7 +593,7 @@
         ),
         cost_estimate=pl.CostEstimate(flops=0, bytes_accessed=200_000_000, transcendentals=0),
         name="start_gather",
-    )(x, gain, shift, dy, bias, wq, wo, gate, down)
+    )(x, gains, shifts, dy, bias, wq, wo, gate, down)
 
 
 def back_kernel(
@@ -948,13 +948,13 @@
     def reduce_rows(self, terms, ready, name):
         return lax.psum_scatter(terms, "tensor", scatter_dimension=0, tiled=True).astype(jnp.float32)
 
-    def begin(self, x, gain, shift, dy, bias, w_qkv, w_output, gate_up, down):
+    def begin(self, x, gains, shifts, dy, bias, w_qkv, w_output, gate_up, down):
         low = jnp.bfloat16
-        out, normed, recip = layer_norm(x.astype(jnp.float32), gain, shift)
+        out, normed, recip = layer_norm(x.astype(jnp.float32), gains[0], shifts[0])
         return (
             self.gather_rows(out.astype(low)),
             self.gather_rows(dy),
-            lax.all_gather(bias, "dp", axis=2, tiled=True),
+            lax.all_gather(bias.astype(low), "dp", axis=2, tiled=True),
             gather_dp(w_qkv.astype(low), 1),
             gather_dp(w_output.astype(low), 1),
             normed,
@@ -987,13 +987,9 @@
     def reduce_rows(self, terms, ready, name):
         return square_reduce(terms, ready, name)
 
-    def begin(self, x, gain, shift, dy, bias, w_qkv, w_output, gate_up, down):
-        parts, heads, few = bias.shape
-        a, dy, came, *others = start_gather(
-            x, gain.reshape(1, -1), shift.reshape(1, -1), dy, self.flat(bias), w_qkv, w_output, gate_up, down
-        )
-        came = came.reshape(8, -1)[:, : parts * heads * few].reshape(8, parts, heads, few)
-        return a, dy, came.transpose(1, 2, 0, 3).reshape(parts, heads, -1), *others
+    def begin(self, x, gains, shifts, dy, bias, w_qkv, w_output, gate_up, down):
+        a, dy, came, *others = start_gather(x, gains, shifts, dy, bias, w_qkv, w_output, gate_up, down)
+        return a, dy, came.transpose(1, 2, 0, 3).reshape(*bias.shape[:2], -1), *others
 
     def flat(self, values):
         values = values.astype(jnp.float32).reshape(-1)
@@ -1062,7 +1058,7 @@
     head_size = local_width // local_heads
     xin = inputs.astype(jnp.float32)
     a_all, dy_all, bias_all, w_qkv, w_output, first_normed, first_recip, gate_low, down_low = routes.begin(
-        inputs, gains[0], shifts[0], cotangent, biases.astype(low), qkv_weight, out_weight, gate_up, down_weight
+        inputs, gains, shifts, cotangent, biases, qkv_weight, out_weight, gate_up, down_weight
     )
     bias_all = bias_all.reshape(3, local_width).astype(jnp.float32)
     w_gate_up = gather_dp(after(gate_low, w_output), 1)
@@ -1105,7 +1101,7 @@
     first_terms = jnp.einsum(
         "krc,kdc->rd", lin_grads, w_qkv, preferred_element_type=jnp.float32
     ).astype(low)
-    qkv_grad = scatter_dp(after(qkv_terms, gate_grad), 1)
+    qkv_grad = scatter_dp(after(qkv_terms, (gate_grad, out_terms)), 1)
     input_step, out_grad, vectors, bias_sum = routes.finish(
         first_terms,
         out_terms,

time: 555 us -> 554 us (level)
    unnamed x96 -> x99, local copies, waits for them, and re-layouts: 15.9 us -> 13.9 us
  transfers between devices with their start and end apart: 8 -> 8, of which waited for: 4 -> 5; matrix products, arithmetic and copies ran while one was open for 28% -> 28% of each run, Pallas kernels for 43% -> 43%
where the time goes in v6:
time: 554 us; the launch traced here: 546 us
  Pallas kernels  317 us (57%)
  matrix products  123 us (22%)
  waiting for transfers between devices  38.3 us (7%)
  other arithmetic  30.2 us (5%)
  local copies, waits for them, and re-layouts  18.1 us (3%)
  between operations  14.9 us (3%)
    pallas_call x1, Pallas kernels, start_gather(): pl.pallas_call(start_kernel, out_shape=(shape((4 * rows, model), low), sh...  81.2 us
    pallas_call x1, Pallas kernels, square_back(): pl.pallas_call(back_kernel, out_shape=(shape((4 * rows, width), low), sha...  72.4 us
    pallas_call x1, Pallas kernels, last_reduce(): pl.pallas_call(last_kernel, out_shape=(shape((rows, model), wide), shape(...  48.8 us
    dot_general x6, matrix products, mxu(): lax.dot_general(left, right, dims, preferred_element_type=jnp.float32)  38.5 us
    pallas_call x1, Pallas kernels, square_reduce(): pl.pallas_call(reduce_kernel, out_shape=jax.ShapeDtypeStruct((rows, width...  38 us
    pallas_call x1, Pallas kernels, square_gather(): pl.pallas_call(gather_kernel, out_shape=jax.ShapeDtypeStruct((4 * rows, w...  37.5 us
    all_gather x2, waiting for transfers between devices, gather_dp(): lax.all_gather(block.astype(jnp.bfloat16), 'dp', axis=axis, tiled=True)  28.4 us
    pallas_call x1, Pallas kernels, attention_backward(): pl.pallas_call(functools.partial(backward_kernel, head_size), grid=(rows...  24.5 us
  transfers between devices with their start and end apart: 8, of which 5 were waited for; matrix products, arithmetic and copies ran while one was open for 28% of the time, Pallas kernels for 43%

profile of v6, /device:TPU:0, one launch (start us, length us, event | category | flops | bytes accessed | tf_op | source)
XLA Modules:
  0.0 545.6 jit_solution(2597547887638673566)
XLA Ops:
  7.3 81.2 %start_gather.1 = (bf16[1024,2048]{1,0:T(8,128)(2,1)}, bf16[1024,2048]{1,0:T(8,128)(2,1)}, f32[8,3,8,8]{3,2,1,0:T(8,128)}, bf16[3,2048,512]{2,1,0:T(8,128)(2,1)}...) custom-call(bf16[256,2048]{1,0:T(8,128)(2,1)} %x_from.1, ...), custom_call_target="tpu_custom_call" | custom-call | bytes 200000000 | tf_op jit(solution)/shard_map/start_gather/pallas_call | solution.py:563
  89.6 11.8 %fusion.9.lin_ref = f32[3,1024,512]{2,1,0:T(8,128)} fusion(bf16[3,2048,512]{2,1,0:T(8,128)(2,1)} %get-tuple-element.64, bf16[1024,2048]{1,0:T(8,128)(2,1)} %get-tuple-element.65), kind=kOutput, calls=%fused_computation.28 | convolution fusion | flops 6442450944 | bytes 16777216 | tf_op jit(solution)/shard_map/rd,kdc->krc/dot_general | solution.py:1065
  101.4 14.9 %attend_forward.1 = (bf16[3,1024,512]{2,1,0:T(8,128)(2,1)S(1)}, bf16[1024,512]{1,0:T(8,128)(2,1)S(1)}, f32[2,8,1024]{2,1,0:T(8,128)S(1)}) custom-call(f32[3,1024,512]{2,1,0:T(8,128)} %fusion.9.lin_ref, f32[3,512]{1,0:T(4,128)S(1)} %reshape_reshape.6.bias_ref, f32[3,1024,128]{2,1,0:T(8,128)S(1)} %copy-done.9), custom_call_target="tpu_custom_call" | custom-call | flops 4294967296 | bytes 13631488 | tf_op jit(solution)/shard_map/attend_forward/pallas_call | solution.py:129
  118.7 38.0 %square_reduce.1 = f32[256,2048]{1,0:T(8,128)S(1)} custom-call(bf16[1024,2048]{1,0:T(8,128)(2,1)S(1)} %convolution_convert_fusion.2.terms_ref, f32[2,8,1024]{2,1,0:T(8,128)S(1)} %get-tuple-element.69.ready_ref.lse_ref), custom_call_target="tpu_custom_call" | custom-call | bytes 125829120 | tf_op jit(solution)/shard_map/square_reduce/pallas_call | solution.py:357
  159.0 37.5 %square_gather.1 = bf16[1024,2048]{1,0:T(8,128)(2,1)} custom-call(bf16[256,2048]{1,0:T(8,128)(2,1)} %add_convert_fusion.1.block_ref), custom_call_target="tpu_custom_call" | custom-call | bytes 62914560 | tf_op jit(solution)/shard_map/square_gather/pallas_call | solution.py:289
  196.7 16.6 %convolution_bitcast_fusion = f32[2,1024,1408]{1,2,0:T(8,128)S(1)} fusion(bf16[2,2048,1408]{2,1,0:T(8,128)(2,1)} %all-gather.3.cloned.1.call-done, bf16[1024,2048]{1,0:T(8,128)(2,1)} %square_gather.1), kind=kOutput, calls=%fused_computation.4 | convolution fusion | flops 11811160064 | bytes 27262976 | tf_op jit(solution)/shard_map/rd,kdc->krc/dot_general | solution.py:1071
  213.2 4.2 copy-done.14
  220.9 8.1 %convolution_convert_fusion = bf16[1408,2048]{1,0:T(8,128)(2,1)} fusion(bf16[1024,1408]{0,1:T(8,128)(2,1)S(1)} %multiply_convert_fusion.2, bf16[1024,2048]{1,0:T(8,128)(2,1)S(1)} %copy-done.44), kind=kOutput, calls=%fused_computation.3 | convolution fusion | flops 5908463616 | bytes 12845056 | tf_op jit(solution)/shard_map/dot_general | solution.py:84
  229.0 28.3 %all-gather.5.cloned.1.call-done = bf16[1408,2048]{1,0:T(8,128)(2,1)} async-done(((bf16[1408,256]{1,0:T(8,128)(2,1)}), bf16[1408,2048]{1,0:T(8,128)(2,1)}) %all-gather.5.cloned.1.call-update) | async-done | bytes 5767184 | tf_op jit(solution)/shard_map/all_gather | solution.py:1022
  257.3 10.0 %convolution_convert_fusion.1 = bf16[1024,2048]{1,0:T(8,128)(2,1)S(1)} fusion(bf16[1024,1408]{0,1:T(8,128)(2,1)} %copy-done.21, bf16[1408,2048]{1,0:T(8,128)(2,1)} %all-gather.5.cloned.1.call-done), kind=kOutput, calls=%fused_computation.20 | convolution fusion | flops 5907677184 | bytes 12845056 | tf_op jit(solution)/shard_map/dot_general | solution.py:84
  273.1 12.0 %fusion.8 = (bf16[1,1024,1408]{1,2,0:T(8,128)(2,1)S(1)}, bf16[1,1024,1408]{1,2,0:T(8,128)(2,1)}) fusion(f32[2,1024,1408]{1,2,0:T(8,128)} %copy-done.14, bf16[1024,2048]{1,0:T(8,128)(2,1)S(1)} %copy-done.45, bf16[1408,2048]{1,0:T(8,128)(2,1)S(1)} %copy-done.42), kind=kOutput, calls=%fused_computation.27 | convolution fusion | flops 5924323328 | bytes 27262976 | tf_op jit(solution)/shard_map/dot_general | solution.py:84
  286.7 17.9 %bitcast_convert_fusion.1.terms_ref = bf16[1024,2048]{1,0:T(8,128)(2,1)} fusion(bf16[2,2048,1408]{2,1,0:T(8,128)(2,1)} %all-gather.3.cloned.1.call-done, bf16[1,1024,1408]{1,2,0:T(8,128)(2,1)} %get-tuple-element.128, bf16[1,1024,1408]{1,2,0:T(8,128)(2,1)S(1)} %get-tuple-element.127), kind=kOutput, calls=%fused_computation.2 | convolution fusion | flops 11816140800 | bytes 21495808 | tf_op jit(solution)/shard_map/krc,kdc->rd/dot_general | solution.py:1089
  304.6 17.3 %convert_bitcast_fusion = bf16[2,2048,1408]{2,1,0:T(8,128)(2,1)} fusion(bf16[1024,2048]{1,0:T(8,128)(2,1)S(1)} %copy-done.19, bf16[1,1024,1408]{1,2,0:T(8,128)(2,1)} %get-tuple-element.128, bf16[1,1024,1408]{1,2,0:T(8,128)(2,1)} %copy-done.48), kind=kOutput, calls=%fused_computation | convolution fusion | flops 11819810816 | bytes 21495808 | tf_op jit(solution)/shard_map/rd,krc->kdc/dot_general | solution.py:1087
  326.3 72.4 %square_back.1 = (bf16[1024,2048]{1,0:T(8,128)(2,1)S(1)}, f32[256,2048]{1,0:T(8,128)S(1)}, f32[2,2048]{1,0:T(2,128)S(1)}) custom-call(bf16[1024,2048]{1,0:T(8,128)(2,1)S(1)} %copy-done, bf16[16,128]{1,0:T(8,128)(2,1)S(1)} %slice.40.ready_ref, f32[256,2048]{1,0:T(8,128)S(1)} %get-tuple-element.126.resid_ref, f32[1,2048]{1,0:T(1,128)S(1)} %get-tuple-element.138.gain_ref, ...), custom_call_target="tpu_custom_call" | custom-call | bytes 209715200 | tf_op jit(solution)/shard_map/square_back/pallas_call | solution.py:692
  398.8 3.7 convolution_convert_fusion.3.proj_ref
  404.9 24.5 %attend_backward.1 = (bf16[3,1024,512]{2,1,0:T(8,128)(2,1)}, f32[1,3,512]{2,1,0:T(4,128)S(1)}) custom-call(bf16[3,1024,512]{2,1,0:T(8,128)(2,1)} %copy-done.13, bf16[1024,512]{1,0:T(8,128)(2,1)S(1)} %convolution_convert_fusion.4.grad_ref, f32[2,8,1024]{2,1,0:T(8,128)S(1)} %copy-done.8, f32[3,1024,128]{2,1,0:T(8,128)S(1)} %copy-done.10), custom_call_target="tpu_custom_call" | custom-call | flops 10737418240 | bytes 13631488 | tf_op jit(solution)/shard_map/attend_backward/pallas_call | solution.py:206
  429.4 10.9 %convert_bitcast_fusion.1 = bf16[3,2048,512]{2,1,0:T(8,128)(2,1)} fusion(bf16[3,1024,512]{2,1,0:T(8,128)(2,1)} %get-tuple-element.80, bf16[1024,2048]{1,0:T(8,128)(2,1)S(1)} %copy-done.43), kind=kOutput, calls=%fused_computation.5 | convolution fusion | flops 6445596672 | bytes 13631488 | tf_op jit(solution)/shard_map/rd,krc->kdc/dot_general | solution.py:1099
  442.7 9.9 %bitcast_convert_fusion.first_ref = bf16[1024,2048]{1,0:T(8,128)(2,1)S(1)} fusion(bf16[3,1024,512]{2,1,0:T(8,128)(2,1)} %get-tuple-element.80, bf16[3,2048,512]{2,1,0:T(8,128)(2,1)} %get-tuple-element.64), kind=kOutput, calls=%fused_computation.1 | convolution fusion | flops 6444548096 | bytes 13631488 | tf_op jit(solution)/shard_map/krc,kdc->rd/dot_general | solution.py:1101
  452.6 48.8 %last_reduce.1 = (f32[256,2048]{1,0:T(8,128)S(1)}, f32[512,256]{1,0:T(8,128)S(1)}, f32[4,2048]{1,0:T(4,128)S(1)}, f32[8,256]{1,0:T(8,128)S(1)}) custom-call(bf16[1024,2048]{1,0:T(8,128)(2,1)S(1)} %bitcast_convert_fusion.first_ref, bf16[512,2048]{1,0:T(8,128)(2,1)S(1)} %copy-done.5, f32[256,2048]{1,0:T(8,128)S(1)} %copy-done.4, f32[256,1]{1,0:T(8,128)S(1)} %copy-done.6, ...), custom_call_target="tpu_custom_call" | custom-call | bytes 120000000 | tf_op jit(solution)/shard_map/last_reduce/pallas_call | solution.py:910
  502.9 4.0 add.183
  509.9 3.6 add_convert_fusion
  518.3 7.3 %multiply_subtract_fusion = (f32[2,256,1408]{2,1,0:T(8,128)}, f32[2,256,1408]{2,1,0:T(8,128)}, f32[2,256,1408]{2,1,0:T(8,128)}, f32[2,256,1408]{2,1,0:T(8,128)}) fusion(f32[2,256,1408]{2,1,0:T(8,128)S(1)} %copy-done.15, f32[2,256,1408]{2,1,0:T(8,128)S(1)} %copy-done.22, f32[2,256,1408]{2,1,0:T(8,128)} %param.46, ...), kind=kLoop, calls=%fused_computation.25 | loop fusion | flops 11534336 | bytes 21626880 | tf_op jit(solution)/shard_map/sub | solution.py:47
  525.6 6.8 %reduce-scatter.8.cloned.1.call-done = bf16[3,256,512]{2,1,0:T(8,128)(2,1)} async-done(((bf16[3,2048,512]{2,1,0:T(8,128)(2,1)}), bf16[3,256,512]{2,1,0:T(8,128)(2,1)}) %reduce-scatter.8.cloned.1.call-update) | async-done | bytes 786448 | tf_op jit(solution)/shard_map/reduce_scatter | solution.py:1026
  532.4 5.3 multiply_subtract_fusion.1
  (139 shorter events, 35.5 us)
Async XLA Ops:
  7.2 81.3 %copy-start.33 = (f32[2,2048]{1,0:T(2,128)S(1)}, f32[2,2048]{1,0:T(2,128)}, u32[]{:S(2)}) copy-start(f32[2,2048]{1,0:T(2,128)} %shift_ref.1) | copy-start | bytes 49156
  7.2 189.4 %all-gather.3.cloned.1.call-start = ((), (), s32[]{:S(2)}) async-start(), calls=%async_computation.3 | async-start | bytes 12976128 | tf_op jit(solution)/shard_map/all_gather | solution.py:1022
  88.4 168.9 %all-gather.5.cloned.1.call-start = ((), (), s32[]{:S(2)}) async-start(), calls=%async_computation.4 | async-start | bytes 6488064 | tf_op jit(solution)/shard_map/all_gather | solution.py:1022
  89.5 11.9 %copy-start.9 = (f32[3,1024,128]{2,1,0:T(8,128)S(1)}, f32[3,1024,128]{2,1,0:T(8,128)}, u32[]{:S(2)}) copy-start(f32[3,1024,128]{2,1,0:T(8,128)} %constant.49.clone.table_ref) | copy-start | bytes 4718596
  101.4 14.9 %copy-start.46 = (bf16[512,2048]{1,0:T(8,128)(2,1)S(1)}, bf16[512,2048]{1,0:T(8,128)(2,1)}, u32[]{:S(2)}) copy-start(bf16[512,2048]{1,0:T(8,128)(2,1)} %get-tuple-element.68) | copy-start | bytes 6291460
  118.7 38.1 %copy-start.20 = (bf16[256,2048]{1,0:T(8,128)(2,1)S(1)}, bf16[256,2048]{1,0:T(8,128)(2,1)}, u32[]{:S(2)}) copy-start(bf16[256,2048]{1,0:T(8,128)(2,1)} %x_from.1) | copy-start | bytes 3145732
  196.6 126.1 %reduce-scatter.4.cloned.1.call-start = ((), (), s32[]{:S(2)}) async-start(), calls=%async_computation.5 | async-start | bytes 6488064 | tf_op jit(solution)/shard_map/reduce_scatter | solution.py:1026
  228.9 213.6 %reduce-scatter.6.cloned.1.call-start = ((), (), s32[]{:S(2)}) async-start(), calls=%async_computation.6 | async-start | bytes 12976128 | tf_op jit(solution)/shard_map/reduce_scatter | solution.py:1026
  257.3 15.8 %copy-start.45 = (bf16[1024,2048]{1,0:T(8,128)(2,1)S(1)}, bf16[1024,2048]{1,0:T(8,128)(2,1)}, u32[]{:S(2)}) copy-start(bf16[1024,2048]{1,0:T(8,128)(2,1)} %get-tuple-element.74) | copy-start | bytes 12582916
  267.4 5.8 %copy-start.42 = (bf16[1408,2048]{1,0:T(8,128)(2,1)S(1)}, bf16[1408,2048]{1,0:T(8,128)(2,1)}, u32[]{:S(2)}) copy-start(bf16[1408,2048]{1,0:T(8,128)(2,1)} %all-gather.5.cloned.1.call-done) | copy-start | bytes 17301508
  269.6 52.3 %collective-permute-start.2 = (bf16[256,2048]{1,0:T(8,128)(2,1)}, bf16[256,2048]{1,0:T(8,128)(2,1)S(1)}, u32[]{:S(2)}, u32[]{:S(2)}) collective-permute-start(bf16[256,2048]{1,0:T(8,128)(2,1)} %get-tuple-element.129), channel_id=1, source_target_pairs={{0,3},{1,2},{2,1},{3,0},{4,7},{5,6},{6,5},{7,4},{8,11},{9,10},{10,... | collective-permute-start | bytes 3145736 | tf_op jit(solution)/shard_map/ppermute | solution.py:1004
  272.0 49.9 %collective-permute-start.1 = (bf16[256,2048]{1,0:T(8,128)(2,1)}, bf16[256,2048]{1,0:T(8,128)(2,1)}, u32[]{:S(2)}, u32[]{:S(2)}) collective-permute-start(bf16[256,2048]{1,0:T(8,128)(2,1)} %get-tuple-element.130), channel_id=1, source_target_pairs={{0,2},{1,3},{2,0},{3,1},{4,6},{5,7},{6,4},{7,5},{8,10},{9,11},{10,... | collective-permute-start | bytes 3145736 | tf_op jit(solution)/shard_map/ppermute | solution.py:1004
  272.6 49.4 %collective-permute-start = (bf16[256,2048]{1,0:T(8,128)(2,1)}, bf16[256,2048]{1,0:T(8,128)(2,1)}, u32[]{:S(2)}, u32[]{:S(2)}) collective-permute-start(bf16[256,2048]{1,0:T(8,128)(2,1)} %get-tuple-element.131), channel_id=1, source_target_pairs={{0,1},{1,0},{2,3},{3,2},{4,5},{5,4},{6,7},{7,6},{8,9},{9,8},{10,11... | collective-permute-start | bytes 3145736 | tf_op jit(solution)/shard_map/ppermute | solution.py:1004
  286.7 18.0 %copy-start.19 = (bf16[1024,2048]{1,0:T(8,128)(2,1)S(1)}, bf16[1024,2048]{1,0:T(8,128)(2,1)}, u32[]{:S(2)}) copy-start(bf16[1024,2048]{1,0:T(8,128)(2,1)} %square_gather.1) | copy-start | bytes 12582916
  323.0 209.5 %reduce-scatter.8.cloned.1.call-start = ((), (), s32[]{:S(2)}) async-start(), calls=%async_computation.7 | async-start | bytes 7077888 | tf_op jit(solution)/shard_map/reduce_scatter | solution.py:1026
  326.3 72.4 %copy-start.12 = (bf16[1024,512]{1,0:T(8,128)(2,1)S(1)}, bf16[1024,512]{1,0:T(8,128)(2,1)}, u32[]{:S(2)}) copy-start(bf16[1024,512]{1,0:T(8,128)(2,1)} %copy-done.11) | copy-start | bytes 3145732
  404.9 24.5 %copy-start.43 = (bf16[1024,2048]{1,0:T(8,128)(2,1)S(1)}, bf16[1024,2048]{1,0:T(8,128)(2,1)}, u32[]{:S(2)}) copy-start(bf16[1024,2048]{1,0:T(8,128)(2,1)} %get-tuple-element.65) | copy-start | bytes 12582916
  442.6 10.0 %copy-start.4 = (f32[256,2048]{1,0:T(8,128)S(1)}, f32[256,2048]{1,0:T(8,128)}, u32[]{:S(2)}) copy-start(f32[256,2048]{1,0:T(8,128)} %get-tuple-element.81.normed_ref) | copy-start | bytes 6291460
  442.6 10.0 %copy-start.5 = (bf16[512,2048]{1,0:T(8,128)(2,1)S(1)}, bf16[512,2048]{1,0:T(8,128)(2,1)}, u32[]{:S(2)}) copy-start(bf16[512,2048]{1,0:T(8,128)(2,1)} %convolution_convert_fusion.3.proj_ref) | copy-start | bytes 6291460
  442.7 10.0 %copy-start.6 = (f32[256,1]{1,0:T(8,128)S(1)}, f32[256,1]{1,0:T(8,128)}, u32[]{:S(2)}) copy-start(f32[256,1]{1,0:T(8,128)} %get-tuple-element.82.recip_ref) | copy-start | bytes 3076
  502.8 4.9 copy-start.23
  502.8 4.9 copy-start.29
  502.9 4.8 copy-start.30
  518.3 14.1 %copy-start.16 = (f32[3,256,512]{2,1,0:T(8,128)S(1)}, f32[3,256,512]{2,1,0:T(8,128)}, u32[]{:S(2)}) copy-start(f32[3,256,512]{2,1,0:T(8,128)} %wq_from.1) | copy-start | bytes 4718596
  (33 other events, 90.1 us)
Sparse Core Ops, SparseCore 0:
  88.6 107.9 all-gather.2
  198.2 59.1 all-gather.4
  259.6 63.0 reduce-scatter.3
  324.9 117.6 reduce-scatter.5
  444.7 87.6 reduce-scatter.7
